TPU v7x, 32 devices: a whole 2x2x4 slice. The times are simulated.
32 devices in a mesh: grp: 2 (over core), vocab: 4 (over z), tok: 4 (over y, x).
Axes of the slice: x: 2, y: 2, z: 4, core: 2. Of those that a mesh axis runs over, the one named last changes fastest.
Arguments:
- teacher_hidden: bfloat16 [512, 16384], P(('grp', 'vocab'), 'tok'), may hold values from -1000 to 1000
- student_hidden: bfloat16 [512, 8192], P(('grp', 'vocab'), 'tok'), may hold values from -1000 to 1000
- teacher_gain: float32 [16384], P('tok'), may hold values from 0.5 to 1.5
- student_gain: float32 [8192], P('tok'), may hold values from 0.5 to 1.5
- teacher_head: bfloat16 [65536, 16384], P(('grp', 'vocab'), 'tok'), may hold values from -64 to 64
- student_head: bfloat16 [65536, 8192], P(('grp', 'vocab'), 'tok'), may hold values from -64 to 64
- target_ids: int32 [512], replicated, may hold values from 0 to 65535
Outputs:
- loss: float32 [], replicated
- hidden_grad: bfloat16 [512, 8192], P(('grp', 'vocab'), 'tok')
All inputs are finite; a program needn't handle non-finite values.
Results may differ from a plain program's by a relative error of at most 0.0039.
Values may be sent and summed in bfloat16 or wider, within the bound.
No kernel may reach another device: no remote copies, remote signals or barrier semaphores. Data moves between devices by JAX's collectives and lax.ppermute only.
A program may use at most 320 MiB of HBM per device.

v0:
```python
import jax
import jax.numpy as jnp
from jax import lax
from jax.sharding import PartitionSpec as P

DT = 16384
DS = 8192


heat_divisor = 2.0
blend_fraction = 0.5
objective_scale_factor = 1024.0
epsilon = 1e-05


def on_device(
    teacher_hidden,
    student_hidden,
    teacher_gain,
    student_gain,
    teacher_head,
    student_head,
    target_ids,
):
    vocab_local = teacher_head.shape[0]
    tok_devices = lax.axis_size("tok")
    teacher_rows, student_rows = (
        lax.all_gather(teacher_hidden, ("grp", "vocab"), axis=0, tiled=True),
        lax.all_gather(student_hidden, ("grp", "vocab"), axis=0, tiled=True),
    )
    all_rows = teacher_rows.shape[0]
    share_rows = all_rows // tok_devices
    teacher_wide = teacher_rows.astype(jnp.float32)
    student_wide = student_rows.astype(jnp.float32)
    teacher_weighted = (teacher_wide * teacher_gain).astype(jnp.bfloat16)
    student_weighted = (student_wide * student_gain).astype(jnp.bfloat16)
    contract = (((1,), (1,)), ((), ()))
    teacher_part = lax.dot_general(
        teacher_weighted, teacher_head, contract, preferred_element_type=jnp.float32
    )
    student_part = lax.dot_general(
        student_weighted, student_head, contract, preferred_element_type=jnp.float32
    )
    teacher_squares = jnp.sum(teacher_wide * teacher_wide, axis=1)
    student_squares = jnp.sum(student_wide * student_wide, axis=1)
    members = (teacher_part, student_part)
    summed = (
        lax.psum_scatter(members[0], "tok", scatter_dimension=0, tiled=True),
        lax.psum_scatter(members[1], "tok", scatter_dimension=0, tiled=True),
    )
    row_start = lax.axis_index("tok") * share_rows
    teacher_all_sq, student_all_sq = lax.psum((teacher_squares, student_squares), "tok")
    teacher_sq = lax.dynamic_slice_in_dim(teacher_all_sq, row_start, share_rows)
    student_sq = lax.dynamic_slice_in_dim(student_all_sq, row_start, share_rows)
    teacher_inv = lax.rsqrt(teacher_sq / DT + epsilon)
    student_inv = lax.rsqrt(student_sq / DS + epsilon)
    mentor_score_table = summed[0] * teacher_inv[:, None]
    learner_score_table = summed[1] * student_inv[:, None]
    row_targets = lax.dynamic_slice_in_dim(target_ids, row_start, share_rows)
    mentor_warmed_scores = mentor_score_table / heat_divisor
    score_gap = (mentor_score_table - learner_score_table) / heat_divisor
    columns = lax.axis_index(("grp", "vocab")) * vocab_local + jnp.arange(
        vocab_local, dtype=jnp.int32
    )
    label_hits = row_targets[:, None] == columns[None, :]
    target_local = jnp.sum(jnp.where(label_hits, learner_score_table, 0.0), axis=1)
    mentor_example_peak, learner_example_peak = lax.pmax(
        (jnp.max(mentor_warmed_scores, axis=1), jnp.max(learner_score_table, axis=1)),
        ("grp", "vocab"),
    )
    mentor_power = jnp.exp(mentor_warmed_scores - mentor_example_peak[:, None])
    bare_power = jnp.exp(learner_score_table - learner_example_peak[:, None])
    warmed_power = jnp.exp((learner_score_table - learner_example_peak[:, None]) / heat_divisor)
    (
        mentor_power_total,
        likelihood_penalty_total,
        warmed_power_total,
        bare_power_total,
        label_score_entry,
    ) = lax.psum(
        (
            jnp.sum(mentor_power, axis=1),
            jnp.sum(mentor_power * score_gap, axis=1),
            jnp.sum(warmed_power, axis=1),
            jnp.sum(bare_power, axis=1),
            target_local,
        ),
        ("grp", "vocab"),
    )
    objective_by_example = blend_fraction * heat_divisor**2 * (
        likelihood_penalty_total / mentor_power_total
        - mentor_example_peak
        - jnp.log(mentor_power_total)
        + learner_example_peak / heat_divisor
        + jnp.log(warmed_power_total)
    ) + (1.0 - blend_fraction) * (
        learner_example_peak + jnp.log(bare_power_total) - label_score_entry
    )
    loss_part = jnp.sum(objective_by_example)
    learner_score_slope = (
        objective_scale_factor
        * (
            blend_fraction
            * heat_divisor
            * (
                warmed_power / warmed_power_total[:, None]
                - mentor_power / mentor_power_total[:, None]
            )
            + (1.0 - blend_fraction)
            * (bare_power / bare_power_total[:, None] - label_hits.astype(jnp.float32))
        )
    ).astype(jnp.bfloat16)
    grad_all = lax.all_gather(learner_score_slope, "tok", axis=0, tiled=True)
    norm_grad = lax.psum_scatter(
        jnp.dot(grad_all, student_head, preferred_element_type=jnp.float32),
        ("grp", "vocab"),
        scatter_dimension=0,
        tiled=True,
    )
    widened = student_hidden.astype(jnp.float32)
    inner_local = jnp.sum(student_gain * norm_grad * widened, axis=1)
    square_local = jnp.sum(widened * widened, axis=1)
    row_members = (square_local, inner_local, loss_part)
    reduced = lax.psum((row_members[0], row_members[1], row_members[2]), "tok")
    loss_sum = reduced[2]
    loss = loss_sum / all_rows
    own_inv = lax.rsqrt(reduced[0] / DS + epsilon)
    hidden_grad = (
        own_inv[:, None] * student_gain * norm_grad
        - widened * (own_inv**3 * reduced[1] / DS)[:, None]
    ).astype(jnp.bfloat16)
    return (loss, hidden_grad)


def solution(mesh):
    in_specs = (
        P(("grp", "vocab"), "tok"),
        P(("grp", "vocab"), "tok"),
        P("tok"),
        P("tok"),
        P(("grp", "vocab"), "tok"),
        P(("grp", "vocab"), "tok"),
        P(),
    )
    out_specs = (P(), P(("grp", "vocab"), "tok"))
    return jax.shard_map(
        on_device, mesh=mesh, in_specs=in_specs, out_specs=out_specs, check_vma=False
    )
```

profile of v0, /device:TPU:0, one launch (start us, length us, event | category | flops | bytes accessed | tf_op | source)
XLA Modules:
  0.0 680.4 jit_solution(16994767776124832547)
XLA Ops:
  7.2 0.0 all-gather.4.cloned.1.call-start
  7.2 0.7 all-gather.4.cloned.1.call-update
  7.9 0.0 all-gather.6.cloned.1.call-start
  7.9 0.7 all-gather.6.cloned.1.call-update
  8.6 0.0 reduce-scatter.4.cloned.1.call-start
  8.7 50.8 %all-gather.4.cloned.1.call-done = bf16[512,4096]{1,0:T(8,128)(2,1)} async-done(((bf16[64,4096]{1,0:T(8,128)(2,1)}), bf16[512,4096]{1,0:T(8,128)(2,1)}) %all-gather.4.cloned.1.call-update) | async-done | bytes 4194320 | tf_op jit(solution)/shard_map/all_gather | solution.py:28
  59.5 42.2 %fusion.10 = f32[512,8192]{1,0:T(8,128)} fusion(bf16[8192,4096]{1,0:T(8,128)(2,1)} %param.11, bf16[512,4096]{1,0:T(8,128)(2,1)} %all-gather.4.cloned.1.call-done, f32[4096]{0:T(1024)} %param.9), kind=kOutput, calls=%fused_computation.16 | convolution fusion | flops 34366029824 | bytes 88096768 | tf_op jit(solution)/shard_map/dot_general | solution.py:38
  101.7 0.0 copy-start.2
  101.7 0.0 reduce-scatter.4.cloned.1.call-update
  101.7 0.0 reduce-scatter.6.cloned.1.call-start
  101.7 0.0 all-gather.6.cloned.1.call-done
  101.8 0.6 copy-done.2
  102.4 25.8 %fusion.15 = f32[512,8192]{1,0:T(8,128)} fusion(bf16[8192,2048]{1,0:T(8,128)(2,1)} %param.12, bf16[512,2048]{1,0:T(8,128)(2,1)} %all-gather.6.cloned.1.call-done, f32[2048]{0:T(1024)S(1)} %copy-done.2), kind=kOutput, calls=%fused_computation.26 | convolution fusion | flops 17183014912 | bytes 52436992 | tf_op jit(solution)/shard_map/dot_general | solution.py:41
  128.2 0.0 copy-start.1
  128.2 0.0 reduce-scatter.6.cloned.1.call-update
  128.2 0.0 all-gather.8.cloned.1.call-start
  128.3 0.9 dynamic_slice.11
  129.2 0.6 copy-done.1
  129.8 0.5 fusion.3
  130.3 3.2 fusion.1
  133.4 10.2 %all-reduce.2 = (f32[512]{0:T(512)S(1)}, f32[512]{0:T(512)S(1)}) all-reduce(f32[512]{0:T(512)S(1)} %fusion.3, f32[512]{0:T(512)S(1)} %fusion.1), channel_id=1, replica_groups=mesh['grp'=2,'vocab'=4,'tok'=4] {'tok'}, use_global_device_ids=true, to_apply=%region_7.8 | all-reduce | flops 1024 | bytes 8192 | tf_op jit(solution)/shard_map/psum | solution.py:52
  143.6 0.1 add_rsqrt_fusion.1
  143.7 0.1 add_rsqrt_fusion.2
  143.8 110.8 %reduce-scatter.4.cloned.1.call-done = f32[128,8192]{1,0:T(8,128)} async-done(((f32[512,8192]{1,0:T(8,128)}), f32[128,8192]{1,0:T(8,128)}) %reduce-scatter.4.cloned.1.call-update) | async-done | bytes 4194320 | tf_op jit(solution)/shard_map/reduce_scatter | solution.py:48
  254.6 2.8 multiply_reduce_fusion.1
  257.4 16.7 %pmax.14 = f32[128]{0:T(128)S(1)} all-reduce(f32[128]{0:T(128)S(1)} %multiply_reduce_fusion.1), channel_id=1, replica_groups=mesh['grp'=2,'vocab'=4,'tok'=4] {'grp','vocab'}, use_global_device_ids=true, to_apply=%region_4.0 | all-reduce | flops 128 | bytes 1024 | tf_op jit(solution)/shard_map/pmax | solution.py:67
  274.0 137.4 %reduce-scatter.6.cloned.1.call-done = f32[128,8192]{1,0:T(8,128)} async-done(((f32[512,8192]{1,0:T(8,128)}), f32[128,8192]{1,0:T(8,128)}) %reduce-scatter.6.cloned.1.call-update) | async-done | bytes 4194320 | tf_op jit(solution)/shard_map/reduce_scatter | solution.py:49
  411.4 4.8 multiply_reduce_fusion
  416.2 16.5 %pmax.15 = f32[128]{0:T(128)S(1)} all-reduce(f32[128]{0:T(128)S(1)} %get-tuple-element.6), channel_id=1, replica_groups=mesh['grp'=2,'vocab'=4,'tok'=4] {'grp','vocab'}, use_global_device_ids=true, to_apply=%region_13.14 | all-reduce | flops 128 | bytes 1024 | tf_op jit(solution)/shard_map/pmax | solution.py:67
  432.6 3.6 fusion.14
  436.2 13.7 %all-reduce = (f32[128]{0:T(128)S(1)}, f32[128]{0:T(128)S(1)}, f32[128]{0:T(128)S(1)}, f32[128]{0:T(128)S(1)}, f32[128]{0:T(128)S(1)}) all-reduce(f32[128]{0:T(128)S(1)} %get-tuple-element.7, f32[128]{0:T(128)S(1)} %get-tuple-element.5, f32[128]{0:T(128)S(1)} %get-tuple-element.4, ...), channel_id=1, replica_groups=mesh['grp'=2,'vocab'=4,'tok'=4] {'grp','vocab'}, use_global_device_ids=true, to_apply=%region_19.20 | all-reduce | flops 640 | bytes 5120 | tf_op jit(solution)/shard_map/psum | solution.py:80
  449.9 6.6 fusion.9
  456.6 0.0 all-gather.8.cloned.1.call-update
  456.6 0.0 reduce-scatter.8.cloned.1.call-start
  456.6 87.5 %all-gather.8.cloned.1.call-done = bf16[512,8192]{1,0:T(8,128)(2,1)} async-done(((bf16[128,8192]{1,0:T(8,128)(2,1)}), bf16[512,8192]{1,0:T(8,128)(2,1)}) %all-gather.8.cloned.1.call-update) | async-done | bytes 8388624 | tf_op jit(solution)/shard_map/all_gather | solution.py:113
  544.2 24.8 %fusion.24 = f32[512,2048]{1,0:T(8,128)} fusion(bf16[512,8192]{1,0:T(8,128)(2,1)} %all-gather.8.cloned.1.call-done, bf16[8192,2048]{1,0:T(8,128)(2,1)} %param.12), kind=kOutput, calls=%fused_computation.43 | convolution fusion | flops 17179869184 | bytes 46137344 | tf_op jit(solution)/shard_map/dot_general | solution.py:115
  569.0 0.0 copy-start
  569.0 0.0 reduce-scatter.8.cloned.1.call-update
  569.0 0.6 add_reduce_fusion
  569.6 88.5 %reduce-scatter.8.cloned.1.call-done = f32[64,2048]{1,0:T(8,128)} async-done(((f32[512,2048]{1,0:T(8,128)}), f32[64,2048]{1,0:T(8,128)}) %reduce-scatter.8.cloned.1.call-update) | async-done | bytes 524304 | tf_op jit(solution)/shard_map/reduce_scatter | solution.py:114
  658.1 0.0 copy-done
  658.1 1.2 fusion.18
  659.4 10.5 %all-reduce.1 = (f32[]{:T(128)}, f32[64]{0:T(128)S(1)}, f32[64]{0:T(128)S(1)}) all-reduce(f32[]{:T(128)} %add_reduce_fusion, f32[64]{0:T(128)S(1)} %get-tuple-element.9, f32[64]{0:T(128)S(1)} %get-tuple-element.8), channel_id=1, replica_groups=mesh['grp'=2,'vocab'=4,'tok'=4] {'tok'}, use_global_device_ids=true, to_apply=%region_21.22 | all-reduce | flops 129 | bytes 1032 | tf_op jit(solution)/shard_map/psum | solution.py:124
  670.5 1.9 fusion.21
  (2 shorter events, 0.0 us)
Async XLA Ops:
  7.2 52.3 %all-gather.4.cloned.1.call-start = ((), (), s32[]{:S(2)}) async-start(), calls=%async_computation.3 | async-start | bytes 4718592 | tf_op jit(solution)/shard_map/all_gather | solution.py:28
  7.9 93.9 %all-gather.6.cloned.1.call-start = ((), (), s32[]{:S(2)}) async-start(), calls=%async_computation.5 | async-start | bytes 2359296 | tf_op jit(solution)/shard_map/all_gather | solution.py:29
  8.6 245.9 %reduce-scatter.4.cloned.1.call-start = ((), (), s32[]{:S(2)}) async-start(), calls=%async_computation.4 | async-start | bytes 20971520 | tf_op jit(solution)/shard_map/reduce_scatter | solution.py:48
  101.7 0.7 copy-start.2
  101.7 309.7 %reduce-scatter.6.cloned.1.call-start = ((), (), s32[]{:S(2)}) async-start(), calls=%async_computation.6 | async-start | bytes 20971520 | tf_op jit(solution)/shard_map/reduce_scatter | solution.py:49
  128.2 1.6 copy-start.1
  128.2 416.0 %all-gather.8.cloned.1.call-start = ((), (), s32[]{:S(2)}) async-start(), calls=%async_computation.7 | async-start | bytes 10485760 | tf_op jit(solution)/shard_map/all_gather | solution.py:113
  456.6 201.6 %reduce-scatter.8.cloned.1.call-start = ((), (), s32[]{:S(2)}) async-start(), calls=%async_computation.8 | async-start | bytes 4718592 | tf_op jit(solution)/shard_map/reduce_scatter | solution.py:114
  569.0 89.1 %copy-start = (bf16[64,2048]{1,0:T(8,128)(2,1)S(1)}, bf16[64,2048]{1,0:T(8,128)(2,1)}, u32[]{:S(2)}) copy-start(bf16[64,2048]{1,0:T(8,128)(2,1)} %param.8) | copy-start | bytes 786436
Sparse Core Ops, SparseCore 0:
  9.6 49.8 all-gather.3
  61.1 27.8 all-gather.5
  101.8 152.7 reduce-scatter.3
  257.5 153.8 reduce-scatter.5
  456.7 87.4 all-gather.7
  569.1 88.9 reduce-scatter.7
where the time goes:
time: 681 us; the launch traced here: 680 us
  waiting for transfers between devices  476 us (70%)
  matrix products  92.8 us (14%)
  blocking collectives  67.5 us (10%)
  other arithmetic  25.3 us (4%)
  between operations  15.9 us (2%)
    reduce_scatter x1, waiting for transfers between devices, on_device(): lax.psum_scatter(members[1], 'tok', scatter_dimension=0, tiled=True)  137 us
    reduce_scatter x1, waiting for transfers between devices, on_device(): lax.psum_scatter(members[0], 'tok', scatter_dimension=0, tiled=True)  111 us
    reduce_scatter x1, waiting for transfers between devices, on_device(): lax.psum_scatter(jnp.dot(grad_all, student_head, preferred_element_type=j...  88.5 us
    all_gather x1, waiting for transfers between devices, on_device(): grad_all = lax.all_gather(learner_score_slope, 'tok', axis=0, tiled=True)  87.5 us
    all_gather x1, waiting for transfers between devices, on_device(): lax.all_gather(teacher_hidden, ('grp', 'vocab'), axis=0, tiled=True)  50.8 us
    dot_general x1, matrix products, on_device(): lax.dot_general(teacher_weighted, teacher_head, contract, preferred_eleme...  42.2 us
    pmax x2, blocking collectives, on_device(): lax.pmax((jnp.max(mentor_warmed_scores, axis=1), jnp.max(learner_score_ta...  33.1 us
    dot_general x1, matrix products, on_device(): lax.dot_general(student_weighted, student_head, contract, preferred_eleme...  25.8 us
  transfers between devices with their start and end apart: 6, of which 5 were waited for; matrix products, arithmetic and copies ran while one was open for 11% of the time, Pallas kernels for 0%

commit v1 on v0

v1 whole, which is shorter than its diff:
```python
import functools
import jax
import jax.numpy as jnp
from jax import lax
from jax.experimental import pallas as pl
from jax.experimental.pallas import tpu as pltpu
from jax.sharding import PartitionSpec as P

heat = 2.0
blend = 0.5
grad_scale = 1024.0
epsilon = 1e-05

f32 = jnp.float32
VMEM_LIMIT = 56 * 1024 * 1024
LANES = 128

TOK_X = [(i, i ^ 1) for i in range(4)]
TOK_Y = [(i, i ^ 2) for i in range(4)]
TOK_D = [(i, i ^ 3) for i in range(4)]
SWAP = [(0, 1), (1, 0)]


def pow2(k):
    one = jnp.ones_like(k)
    a = jnp.left_shift(one, jnp.clip(k + 60, 0, 30)).astype(f32)
    b = jnp.left_shift(one, jnp.clip(k + 30, 0, 30)).astype(f32)
    c = jnp.left_shift(one, jnp.clip(k, 0, 30)).astype(f32)
    d = jnp.left_shift(one, jnp.clip(k - 30, 0, 30)).astype(f32)
    return (a * (2.0**-60)) * b * c * d


def encode(x):
    top = jnp.max(jnp.abs(x), axis=1, keepdims=True)
    e = jnp.ceil(jnp.log2(jnp.maximum(top, 2.0**-44))).astype(jnp.int32)
    e = jnp.clip(e, -44, 31)
    q = jnp.clip(jnp.round(x * pow2(15 - e)), -32767.0, 32767.0)
    return q.astype(jnp.int32).astype(jnp.int16), e


def decode(q, e):
    return q.astype(jnp.int32).astype(f32) * pow2(e - 15)


def lane_is(shape, j):
    return lax.broadcasted_iota(jnp.int32, shape, 1) == j


def logits_kernel(keep_q, send_q, quarter, tile, a_ref, h_ref, keep_ref, send_ref, exps):
    j = pl.program_id(0)
    r = lax.dot_general(
        a_ref[...], h_ref[...], (((1,), (1,)), ((), ())), preferred_element_type=f32
    )

    @pl.when(j == 0)
    def _():
        exps[...] = jnp.zeros_like(exps)

    for n, k in enumerate(keep_q):
        keep_ref[n * quarter : (n + 1) * quarter, :] = r[k * quarter : (k + 1) * quarter]
    columns = pl.ds(pl.multiple_of(j * tile, tile), tile)
    for n, k in enumerate(send_q):
        rows = slice(n * quarter, (n + 1) * quarter)
        q, e = encode(r[k * quarter : (k + 1) * quarter])
        send_ref[rows, columns] = q
        exps[rows, :] = jnp.where(lane_is((quarter, LANES), j), e, exps[rows, :])

    @pl.when(j == pl.num_programs(0) - 1)
    def _():
        send_ref[:, send_ref.shape[1] - LANES :] = exps[...].astype(jnp.int16)


def partial_logits(a, head, second, tile):
    rows, width = a.shape
    quarter = rows // 4
    half = head.shape[0] // 2
    tiles = half // tile
    first = tiles if second else 0
    keep_q, send_q = ((0, 1), (2, 3)) if second else ((0, 2), (1, 3))
    return pl.pallas_call(
        functools.partial(logits_kernel, keep_q, send_q, quarter, tile),
        grid=(tiles,),
        in_specs=[
            pl.BlockSpec((rows, width), lambda j: (0, 0)),
            pl.BlockSpec((tile, width), lambda j: (first + j, 0)),
        ],
        out_specs=[
            pl.BlockSpec((2 * quarter, tile), lambda j: (0, j)),
            pl.BlockSpec((2 * quarter, half + LANES), lambda j: (0, 0)),
        ],
        out_shape=[
            jax.ShapeDtypeStruct((2 * quarter, half), f32),
            jax.ShapeDtypeStruct((2 * quarter, half + LANES), jnp.int16),
        ],
        scratch_shapes=[pltpu.VMEM((2 * quarter, LANES), jnp.int32)],
        compiler_params=pltpu.CompilerParams(vmem_limit_bytes=VMEM_LIMIT),
        cost_estimate=pl.CostEstimate(
            flops=2 * rows * half * width,
            bytes_accessed=2 * half * width + 2 * rows * width + 6 * rows * half,
            transcendentals=0,
        ),
        name="logits",
    )(a, head)


def relay_kernel(tile, got_ref, keep_ref, out_ref):
    rows, half = keep_ref.shape
    exps = got_ref[:, half : half + LANES].astype(jnp.int32)
    new = jnp.zeros((rows, LANES), jnp.int32)
    for j in range(half // tile):
        cols = slice(j * tile, (j + 1) * tile)
        total = keep_ref[:, cols] + decode(got_ref[:, cols], exps[:, j : j + 1])
        q, e = encode(total)
        out_ref[:, cols] = q
        new = jnp.where(lane_is(new.shape, j), e, new)
    out_ref[:, half : half + LANES] = new.astype(jnp.int16)


def relay(got, keep, tile):
    quarter, half = keep.shape[0] // 2, keep.shape[1]
    return pl.pallas_call(
        functools.partial(relay_kernel, tile),
        grid=(1,),
        in_specs=[
            pl.BlockSpec((quarter, half + LANES), lambda j: (1, 0)),
            pl.BlockSpec((quarter, half), lambda j: (1, 0)),
        ],
        out_specs=pl.BlockSpec((quarter, half + LANES), lambda j: (0, 0)),
        out_shape=jax.ShapeDtypeStruct((quarter, half + LANES), jnp.int16),
        compiler_params=pltpu.CompilerParams(vmem_limit_bytes=VMEM_LIMIT),
        cost_estimate=pl.CostEstimate(
            flops=10 * quarter * half, bytes_accessed=8 * quarter * half, transcendentals=0
        ),
        name="relay",
    )(got, keep)


def put(stats, j, value):
    return jnp.where(lane_is(stats.shape, j), value, stats)


def summed(tile, half, keeps, gots, lasts, inv, out_ref):
    top = None
    for p in range(2):
        first = gots[p][:, half : half + LANES].astype(jnp.int32)
        last = lasts[p][:, half : half + LANES].astype(jnp.int32)
        for j in range(half // tile):
            cols = slice(j * tile, (j + 1) * tile)
            x = keeps[p][:, cols] + decode(gots[p][:, cols], first[:, j : j + 1])
            x = (x + decode(lasts[p][:, cols], last[:, j : j + 1])) * inv
            out_ref[:, p * half + j * tile : p * half + (j + 1) * tile] = x
            high = jnp.max(x, axis=1, keepdims=True)
            top = high if top is None else jnp.maximum(top, high)
    return top


def student_kernel(
    tile, base_ref, kp, kq, gp, gq, lp, lq, inv_ref, target_ref, out_ref, stats_ref
):
    rows, half = kp.shape
    top = summed(tile, half, (kp, kq), (gp, gq), (lp, lq), inv_ref[...], out_ref)
    soft = jnp.zeros((rows, 1), f32)
    plain = jnp.zeros((rows, 1), f32)
    hit = jnp.zeros((rows, 1), f32)
    target = target_ref[...] - base_ref[0]
    for j in range(2 * half // tile):
        x = out_ref[:, j * tile : (j + 1) * tile]
        warm = jnp.exp((x - top) * (1.0 / heat))
        soft = soft + jnp.sum(warm, axis=1, keepdims=True)
        plain = plain + jnp.sum(warm * warm, axis=1, keepdims=True)
        here = lane_is(x.shape, target - j * tile)
        hit = hit + jnp.sum(jnp.where(here, x, 0.0), axis=1, keepdims=True)
    stats = jnp.zeros((rows, LANES), f32)
    for n, value in enumerate((top, soft, plain, hit)):
        stats = put(stats, n, value)
    stats_ref[...] = stats


def teacher_kernel(
    tile, kp, kq, gp, gq, lp, lq, inv_ref, student_ref, before_ref, out_ref, stats_ref
):
    rows, half = kp.shape
    top = summed(tile, half, (kp, kq), (gp, gq), (lp, lq), inv_ref[...], out_ref)
    top = top * (1.0 / heat)
    total = jnp.zeros((rows, 1), f32)
    cross = jnp.zeros((rows, 1), f32)
    for j in range(2 * half // tile):
        cols = slice(j * tile, (j + 1) * tile)
        x = out_ref[:, cols]
        power = jnp.exp(x * (1.0 / heat) - top)
        total = total + jnp.sum(power, axis=1, keepdims=True)
        gap = (x - student_ref[:, cols]) * (1.0 / heat)
        cross = cross + jnp.sum(power * gap, axis=1, keepdims=True)
    stats = before_ref[...]
    for n, value in enumerate((top, total, cross)):
        stats = put(stats, 4 + n, value)
    stats_ref[...] = stats


def finish(keeps, gots, lasts, inv, extra, tile):
    quarter, half = keeps[0].shape[0] // 2, keeps[0].shape[1]
    wide = pl.BlockSpec((quarter, half + LANES), lambda j: (0, 0))
    column = pl.BlockSpec((quarter, 1), lambda j: (0, 0))
    whole = pl.BlockSpec((quarter, 2 * half), lambda j: (0, 0))
    stat = pl.BlockSpec((quarter, LANES), lambda j: (0, 0))
    operands = (*keeps, *gots, *lasts, inv)
    specs = [pl.BlockSpec((quarter, half), lambda j: (0, 0))] * 2 + [wide] * 4 + [column]
    if extra[0].shape == (1,):
        body = student_kernel
        operands = (extra[0], *operands, extra[1])
        specs = [pl.BlockSpec(memory_space=pltpu.SMEM)] + specs + [column]
    else:
        body = teacher_kernel
        operands = (*operands, *extra)
        specs = specs + [whole, stat]
    return pl.pallas_call(
        functools.partial(body, tile),
        grid=(1,),
        in_specs=specs,
        out_specs=[whole, stat],
        out_shape=[
            jax.ShapeDtypeStruct((quarter, 2 * half), f32),
            jax.ShapeDtypeStruct((quarter, LANES), f32),
        ],
        compiler_params=pltpu.CompilerParams(vmem_limit_bytes=VMEM_LIMIT),
        cost_estimate=pl.CostEstimate(
            flops=30 * quarter * half, bytes_accessed=24 * quarter * half, transcendentals=0
        ),
        name="finish",
    )(*operands)


def tree_sum(parts):
    while len(parts) > 1:
        parts = [a + b for a, b in zip(parts[::2], parts[1::2])]
    return parts[0]


def slope_kernel(
    tile, base_ref, student_ref, teacher_ref, stats_ref, target_ref, grad_ref, loss_ref
):
    rows, width = student_ref.shape
    sets = stats_ref.shape[0]
    all_stats = [stats_ref[k] for k in range(sets)]
    top = functools.reduce(jnp.maximum, all_stats)

    def scaled(lane, top_lane, rate):
        return tree_sum(
            [
                s[:, lane : lane + 1]
                * jnp.exp((s[:, top_lane : top_lane + 1] - top[:, top_lane : top_lane + 1]) * rate)
                for s in all_stats
            ]
        )

    student_top, teacher_top = top[:, 0:1], top[:, 4:5]
    soft_total = scaled(1, 0, 1.0 / heat)
    plain_total = scaled(2, 0, 1.0)
    teacher_total = scaled(5, 4, 1.0)
    cross_total = scaled(6, 4, 1.0)
    label = tree_sum([s[:, 3:4] for s in all_stats])
    row_loss = blend * heat**2 * (
        cross_total / teacher_total
        - teacher_top
        - jnp.log(teacher_total)
        + student_top / heat
        + jnp.log(soft_total)
    ) + (1.0 - blend) * (student_top + jnp.log(plain_total) - label)
    loss_ref[...] = put(jnp.zeros((rows, LANES), f32), 0, row_loss)

    soft_rate = grad_scale * blend * heat / soft_total
    teacher_rate = grad_scale * blend * heat / teacher_total
    plain_rate = grad_scale * (1.0 - blend) / plain_total
    target = target_ref[...] - base_ref[0]
    for j in range(width // tile):
        cols = slice(j * tile, (j + 1) * tile)
        warm = jnp.exp((student_ref[:, cols] - student_top) * (1.0 / heat))
        power = jnp.exp(teacher_ref[:, cols] * (1.0 / heat) - teacher_top)
        g = warm * (soft_rate + plain_rate * warm) - power * teacher_rate
        here = lane_is(g.shape, target - j * tile)
        g = jnp.where(here, g - grad_scale * (1.0 - blend), g)
        grad_ref[:, cols] = g.astype(jnp.bfloat16)


def slope(base, student, teacher, stats, targets, tile):
    rows, width = student.shape
    vmem = pl.BlockSpec(memory_space=pltpu.VMEM)
    return pl.pallas_call(
        functools.partial(slope_kernel, tile),
        in_specs=[pl.BlockSpec(memory_space=pltpu.SMEM)] + [vmem] * 4,
        out_specs=[vmem] * 2,
        out_shape=[
            jax.ShapeDtypeStruct((rows, width), jnp.bfloat16),
            jax.ShapeDtypeStruct((rows, LANES), f32),
        ],
        compiler_params=pltpu.CompilerParams(vmem_limit_bytes=VMEM_LIMIT),
        cost_estimate=pl.CostEstimate(
            flops=20 * rows * width, bytes_accessed=10 * rows * width, transcendentals=0
        ),
        name="slope",
    )(base, student, teacher, stats, targets)


def norm_grad_kernel(quarter, half, t_ref, own, gx, gy, dp, dq, h_ref, out_ref, lhs):
    @pl.when(pl.program_id(0) == 0)
    def _():
        for n, ref in enumerate((own, gx, gy)):
            lhs[n * quarter : (n + 1) * quarter, :] = ref[...]
        lhs[3 * quarter :, :half] = dp[...]
        lhs[3 * quarter :, half:] = dq[...]

    r = jnp.dot(lhs[...], h_ref[...], preferred_element_type=f32)
    t = t_ref[0]
    for n in range(4):
        place = pl.multiple_of(jnp.bitwise_xor(t, n) * quarter, quarter)
        out_ref[pl.ds(place, quarter), :] = r[n * quarter : (n + 1) * quarter]


def norm_gradient(t, own, gx, gy, dp, dq, head):
    quarter, vocab = own.shape
    width = head.shape[1]
    tile = min(256, width)
    half = vocab // 2
    full = pl.BlockSpec((quarter, vocab), lambda j: (0, 0))
    part = pl.BlockSpec((quarter, half), lambda j: (0, 0))
    return pl.pallas_call(
        functools.partial(norm_grad_kernel, quarter, half),
        grid=(width // tile,),
        in_specs=[
            pl.BlockSpec(memory_space=pltpu.SMEM),
            full,
            full,
            full,
            part,
            part,
            pl.BlockSpec((vocab, tile), lambda j: (0, j)),
        ],
        out_specs=pl.BlockSpec((4 * quarter, tile), lambda j: (0, j)),
        out_shape=jax.ShapeDtypeStruct((4 * quarter, width), f32),
        scratch_shapes=[pltpu.VMEM((4 * quarter, vocab), jnp.bfloat16)],
        compiler_params=pltpu.CompilerParams(vmem_limit_bytes=VMEM_LIMIT),
        cost_estimate=pl.CostEstimate(
            flops=8 * quarter * vocab * width,
            bytes_accessed=2 * vocab * width + 8 * quarter * vocab,
            transcendentals=0,
        ),
        name="norm_grad",
    )(t, own, gx, gy, dp, dq, head)


def tok_sum(x):
    a = lax.ppermute(x, "tok", TOK_X)
    b = lax.ppermute(x, "tok", TOK_Y)
    c = lax.ppermute(x, "tok", TOK_D)
    return (x + a) + (b + c)


def range_gather(x):
    grps, vocabs = lax.axis_size("grp"), lax.axis_size("vocab")
    me = lax.axis_index(("grp", "vocab"))
    if grps == 2 and vocabs == 4:
        pair = jnp.stack([x, lax.ppermute(x, "grp", SWAP)])
        sets = [pair]
        for k in range(1, 4):
            sets.append(lax.ppermute(pair, "vocab", [(i, i ^ k) for i in range(4)]))
        place = jnp.array([(k % 2) * 4 + k // 2 for k in range(8)], jnp.int32)
        return jnp.concatenate(sets), jnp.bitwise_xor(me, place)
    return lax.all_gather(x, ("grp", "vocab"), axis=0), jnp.arange(grps * vocabs)


def on_device(
    teacher_hidden,
    student_hidden,
    teacher_gain,
    student_gain,
    teacher_head,
    student_head,
    target_ids,
):
    blocks = lax.axis_size("grp") * lax.axis_size("vocab")
    own_rows = teacher_hidden.shape[0]
    all_rows = blocks * own_rows
    part_rows = own_rows // 2
    quarter = blocks * part_rows // 4
    vocab_local = teacher_head.shape[0]
    half = vocab_local // 2
    tile = min(512, half)
    teacher_width = teacher_hidden.shape[1] * lax.axis_size("tok")
    student_width = student_hidden.shape[1] * lax.axis_size("tok")
    t = lax.axis_index("tok")
    t_arr = t.astype(jnp.int32).reshape(1)
    base = (lax.axis_index(("grp", "vocab")) * vocab_local).astype(jnp.int32).reshape(1)

    halves = [slice(0, part_rows), slice(part_rows, own_rows)]
    gathered = []
    for rows in halves:
        s = lax.all_gather(student_hidden[rows], ("grp", "vocab"), axis=0, tiled=True)
        h = lax.all_gather(teacher_hidden[rows], ("grp", "vocab"), axis=0, tiled=True)
        gathered.append((s, h))

    student_wide = student_hidden.astype(f32)
    teacher_wide = teacher_hidden.astype(f32)
    squares = jnp.stack(
        [jnp.sum(student_wide * student_wide, axis=1), jnp.sum(teacher_wide * teacher_wide, axis=1)]
    )
    squares = tok_sum(squares)
    widths = jnp.array([[student_width], [teacher_width]], f32)
    inverse = lax.rsqrt(squares / widths + epsilon)
    everyone, order = range_gather(inverse)
    everyone = jnp.zeros_like(everyone).at[order].set(everyone)
    targets = target_ids.reshape(blocks, own_rows)

    def weighted(rows, gain):
        q = rows.reshape(4, quarter, rows.shape[1])
        q = jnp.concatenate(
            [lax.dynamic_slice_in_dim(q, jnp.bitwise_xor(t, k), 1, 0) for k in range(4)]
        )
        return (q.astype(f32) * gain).astype(jnp.bfloat16).reshape(rows.shape)

    def mine(x, part):
        x = x[:, halves[part]].reshape(4 * quarter)
        return lax.dynamic_slice_in_dim(x, t * quarter, quarter).reshape(quarter, 1)

    def logits_sum(a, head):
        keep_p, send_p = partial_logits(a, head, False, tile)
        keep_q, send_q = partial_logits(a, head, True, tile)
        got_p = lax.ppermute(send_p, "tok", TOK_X)
        got_q = lax.ppermute(send_q, "tok", TOK_Y)
        last_p = lax.ppermute(relay(got_p, keep_p, tile), "tok", TOK_Y)
        last_q = lax.ppermute(relay(got_q, keep_q, tile), "tok", TOK_X)
        return (keep_p, keep_q), (got_p, got_q), (last_p, last_q)

    losses = 0.0
    outs = []
    for part in range(2):
        rows_s, rows_t = gathered[part]
        row_targets = mine(targets, part)
        student_sums = logits_sum(weighted(rows_s, student_gain), student_head)
        teacher_sums = logits_sum(weighted(rows_t, teacher_gain), teacher_head)
        student_logits, stats = finish(
            *student_sums, mine(everyone[:, 0], part), (base, row_targets), tile
        )
        teacher_logits, stats = finish(
            *teacher_sums, mine(everyone[:, 1], part), (student_logits, stats), tile
        )
        all_stats, _ = range_gather(stats)
        grad, row_loss = slope(base, student_logits, teacher_logits, all_stats, row_targets, tile)
        losses = losses + jnp.sum(row_loss[:, 0])
        gx = lax.ppermute(grad, "tok", TOK_X)
        gy = lax.ppermute(grad, "tok", TOK_Y)
        dp = lax.ppermute(gx[:, :half], "tok", TOK_Y)
        dq = lax.ppermute(gy[:, half:], "tok", TOK_X)
        outs.append(norm_gradient(t_arr, grad, gx, gy, dp, dq, student_head))

    norm_grad = jnp.concatenate(
        [
            lax.psum_scatter(o, ("grp", "vocab"), scatter_dimension=0, tiled=True)
            for o in outs
        ]
    )
    inner_local = jnp.sum(student_gain * norm_grad * student_wide, axis=1)
    last = tok_sum(jnp.concatenate([inner_local, jnp.reshape(losses, (1,))]))
    loss = last[own_rows] / all_rows
    inner = last[:own_rows]
    own_inv = inverse[0]
    hidden_grad = (
        own_inv[:, None] * student_gain * norm_grad
        - student_wide * (own_inv**3 * inner / student_width)[:, None]
    ).astype(jnp.bfloat16)
    return (loss, hidden_grad)


def solution(mesh):
    in_specs = (
        P(("grp", "vocab"), "tok"),
        P(("grp", "vocab"), "tok"),
        P("tok"),
        P("tok"),
        P(("grp", "vocab"), "tok"),
        P(("grp", "vocab"), "tok"),
        P(),
    )
    out_specs = (P(), P(("grp", "vocab"), "tok"))
    return jax.shard_map(
        on_device, mesh=mesh, in_specs=in_specs, out_specs=out_specs, check_vma=False
    )
```

time: 681 us -> 525 us (0.77)
  waiting for transfers between devices: 476 us -> 180 us
  Pallas kernels: 0 us -> 226 us
  matrix products: 92.8 us -> 0 us
  blocking collectives: 67.5 us -> 0 us
  starting transfers between devices: 0.24 us -> 51.6 us
  local copies, waits for them, and re-layouts: 2.12 us -> 33.1 us
  other arithmetic: 25.3 us -> 10.6 us
    reduce_scatter x3 -> x2, waiting for transfers between devices: 337 us -> 42.8 us  [on_device(): lax.psum_scatter(o, ('grp', 'vocab'), scatter_dimension=0, tiled=True)]
    pallas_call x0 -> x24, Pallas kernels: none -> 226 us  [the longest x8 129 us: partial_logits(): pl.pallas_call(functools.partial(logits_kernel, keep_q, send_q, quarter,...]
    dot_general x3 -> x0, matrix products: 92.8 us -> none  [the longest x1 42.2 us: on_device(): lax.dot_general(teacher_weighted, teacher_head, contract, preferred_eleme...]
    all_gather x3 -> x4, waiting for transfers between devices: 138 us -> 61.1 us  [the longest x2 34.3 us: on_device(): lax.all_gather(student_hidden[rows], ('grp', 'vocab'), axis=0, tiled=True)]
    ppermute x0 -> x42, waiting for transfers between devices: none -> 75.3 us  [the longest x2 22.2 us: on_device(): gx = lax.ppermute(grad, 'tok', TOK_X)]
    ppermute x0 -> x42, starting transfers between devices: none -> 51.1 us  [the longest x9 15.6 us: range_gather(): sets.append(lax.ppermute(pair, 'vocab', [(i, i ^ k) for i in range(4)]))]
    psum x3 -> x0, blocking collectives: 34.4 us -> none  [the longest x1 13.7 us: on_device(): lax.psum((jnp.sum(mentor_power, axis=1), jnp.sum(mentor_power * score_gap...]
    pmax x2 -> x0, blocking collectives: 33.1 us -> none  [on_device(): lax.pmax((jnp.max(mentor_warmed_scores, axis=1), jnp.max(learner_score_ta...]
  transfers between devices with their start and end apart: 6 -> 48, of which waited for: 5 -> 23; matrix products, arithmetic and copies ran while one was open for 11% -> 5% of each run, Pallas kernels for 0% -> 43%
where the time goes in v1:
time: 525 us; the launch traced here: 520 us
  Pallas kernels  226 us (43%)
  waiting for transfers between devices  180 us (34%)
  starting transfers between devices  51.6 us (10%)
  local copies, waits for them, and re-layouts  33.1 us (6%)
  between operations  18.1 us (3%)
  other arithmetic  10.6 us (2%)
    pallas_call x8, Pallas kernels, partial_logits(): pl.pallas_call(functools.partial(logits_kernel, keep_q, send_q, quarter,...  129 us
    reduce_scatter x2, waiting for transfers between devices, on_device(): lax.psum_scatter(o, ('grp', 'vocab'), scatter_dimension=0, tiled=True)  42.8 us
    pallas_call x2, Pallas kernels, norm_gradient(): pl.pallas_call(functools.partial(norm_grad_kernel, quarter, half), grid=(...  36.6 us
    all_gather x2, waiting for transfers between devices, on_device(): lax.all_gather(student_hidden[rows], ('grp', 'vocab'), axis=0, tiled=True)  34.3 us
    all_gather x2, waiting for transfers between devices, on_device(): lax.all_gather(teacher_hidden[rows], ('grp', 'vocab'), axis=0, tiled=True)  26.8 us
    pallas_call x8, Pallas kernels, relay(): pl.pallas_call(functools.partial(relay_kernel, tile), grid=(1,), in_specs...  26 us
    pallas_call x4, Pallas kernels, finish(): pl.pallas_call(functools.partial(body, tile), grid=(1,), in_specs=specs,...  24.3 us
    ppermute x2, waiting for transfers between devices, on_device(): gx = lax.ppermute(grad, 'tok', TOK_X)  22.2 us
  transfers between devices with their start and end apart: 48, of which 23 were waited for; matrix products, arithmetic and copies ran while one was open for 5% of the time, Pallas kernels for 43%

profile of v1, /device:TPU:0, one launch (start us, length us, event | category | flops | bytes accessed | tf_op | source)
XLA Modules:
  0.0 520.0 jit_solution(7502561681263599911)
XLA Ops:
  7.3 1.8 fusion.13
  9.9 1.9 fusion.12
  12.8 3.0 collective-permute-start.5
  18.2 2.0 collective-permute-done.6
  22.0 1.6 collective-permute-start.8
  23.6 10.9 %all-gather.9.cloned.1.call-done = bf16[256,2048]{1,0:T(8,128)(2,1)} async-done(((bf16[32,2048]{1,0:T(8,128)(2,1)}), bf16[256,2048]{1,0:T(8,128)(2,1)}) %all-gather.9.cloned.1.call-update) | async-done | bytes 1048592 | tf_op jit(solution)/shard_map/all_gather | solution.py:397
  34.5 23.4 %all-gather.5.cloned.1.call-done = bf16[256,2048]{1,0:T(8,128)(2,1)} async-done(((bf16[32,2048]{1,0:T(8,128)(2,1)}), bf16[256,2048]{1,0:T(8,128)(2,1)}) %all-gather.5.cloned.1.call-update) | async-done | bytes 1048592 | tf_op jit(solution)/shard_map/all_gather | solution.py:397
  57.9 1.6 constant_dynamic-slice_fusion.7
  60.2 2.0 fusion.2
  62.3 13.5 %logits.8 = (f32[128,4096]{1,0:T(8,128)}, s16[128,4224]{1,0:T(8,128)(2,1)}) custom-call(bf16[256,2048]{1,0:T(8,128)(2,1)} %get-tuple-element.83.a_ref, bf16[8192,2048]{1,0:T(8,128)(2,1)} %h_ref.19), custom_call_target="tpu_custom_call" | custom-call | flops 4294967296 | bytes 24117248 | tf_op jit(solution)/shard_map/logits/pallas_call | solution.py:80
  75.8 1.5 collective-permute-start
  77.3 13.4 %logits.9 = (f32[128,4096]{1,0:T(8,128)}, s16[128,4224]{1,0:T(8,128)(2,1)}) custom-call(bf16[256,2048]{1,0:T(8,128)(2,1)} %get-tuple-element.83.a_ref, bf16[8192,2048]{1,0:T(8,128)(2,1)} %h_ref.19), custom_call_target="tpu_custom_call" | custom-call | flops 4294967296 | bytes 24117248 | tf_op jit(solution)/shard_map/logits/pallas_call | solution.py:80
  92.2 26.8 %all-gather.7.cloned.1.call-done = bf16[256,4096]{1,0:T(8,128)(2,1)} async-done(((bf16[32,4096]{1,0:T(8,128)(2,1)}), bf16[256,4096]{1,0:T(8,128)(2,1)}) %all-gather.7.cloned.1.call-update) | async-done | bytes 2097168 | tf_op jit(solution)/shard_map/all_gather | solution.py:398
  119.0 2.6 constant_dynamic-slice_fusion.3
  122.6 3.4 fusion
  126.0 18.9 %logits.10 = (f32[128,4096]{1,0:T(8,128)}, s16[128,4224]{1,0:T(8,128)(2,1)}) custom-call(bf16[256,4096]{1,0:T(8,128)(2,1)} %get-tuple-element.81.a_ref, bf16[8192,4096]{1,0:T(8,128)(2,1)} %h_ref.18), custom_call_target="tpu_custom_call" | custom-call | flops 8589934592 | bytes 41943040 | tf_op jit(solution)/shard_map/logits/pallas_call | solution.py:80
  144.9 18.9 %logits.11 = (f32[128,4096]{1,0:T(8,128)}, s16[128,4224]{1,0:T(8,128)(2,1)}) custom-call(bf16[256,4096]{1,0:T(8,128)(2,1)} %get-tuple-element.81.a_ref, bf16[8192,4096]{1,0:T(8,128)(2,1)} %h_ref.18), custom_call_target="tpu_custom_call" | custom-call | flops 8589934592 | bytes 41943040 | tf_op jit(solution)/shard_map/logits/pallas_call | solution.py:80
  165.3 1.5 collective-permute-start.12
  166.8 1.9 collective-permute-start.9
  168.7 2.6 collective-permute-done.9
  171.3 1.9 collective-permute-start.10
  173.2 3.5 collective-permute-done.10
  178.6 3.2 relay.8
  182.4 3.3 relay.9
  186.2 4.5 collective-permute-done.11.got_ref.gp
  191.7 3.2 relay.10
  195.0 1.5 collective-permute-start.13
  197.4 3.2 relay.11
  203.8 13.5 %logits.12 = (f32[128,4096]{1,0:T(8,128)}, s16[128,4224]{1,0:T(8,128)(2,1)}) custom-call(bf16[256,2048]{1,0:T(8,128)(2,1)} %get-tuple-element.82.a_ref, bf16[8192,2048]{1,0:T(8,128)(2,1)} %h_ref.19), custom_call_target="tpu_custom_call" | custom-call | flops 4294967296 | bytes 24117248 | tf_op jit(solution)/shard_map/logits/pallas_call | solution.py:80
  217.9 6.3 %finish.4 = (f32[64,8192]{1,0:T(8,128)}, f32[64,128]{1,0:T(8,128)}) custom-call(s32[1]{0:T(128)} %bitcast.1.base_ref, f32[128,4096]{1,0:T(8,128)} %get-tuple-element.30.keep_ref.kp, f32[128,4096]{1,0:T(8,128)} %get-tuple-element.31.keep_ref.kq, s16[128,4224]{1,0:T(8,128)(2,1)} %copy-done.5, s16[128,4224]{1,0:T(8,128)(2,1)} %collective-permute-done.1.got_ref.gq, ...), custom_call_target="tpu_custom_call" | custom-call | flops 7864320 | bytes 6291456 | tf_op jit(solution)/shard_map/finish/pallas_call | solution.py:216
  225.2 5.8 %finish.5 = (f32[64,8192]{1,0:T(8,128)}, f32[64,128]{1,0:T(8,128)}) custom-call(f32[128,4096]{1,0:T(8,128)} %get-tuple-element.35.keep_ref.kp, f32[128,4096]{1,0:T(8,128)} %get-tuple-element.36.keep_ref.kq, s16[128,4224]{1,0:T(8,128)(2,1)} %copy-done, s16[128,4224]{1,0:T(8,128)(2,1)} %copy-done.1, s16[64,4224]{1,0:T(8,128)(2,1)} %copy-done.15, ...), custom_call_target="tpu_custom_call" | custom-call | flops 7864320 | bytes 6291456 | tf_op jit(solution)/shard_map/finish/pallas_call | solution.py:216
  235.7 1.9 collective-permute-start.18
  237.6 5.2 collective-permute-done.17
  243.5 4.9 slope.2
  248.5 1.5 collective-permute-start.19
  250.5 13.3 %logits.13 = (f32[128,4096]{1,0:T(8,128)}, s16[128,4224]{1,0:T(8,128)(2,1)}) custom-call(bf16[256,2048]{1,0:T(8,128)(2,1)} %get-tuple-element.82.a_ref, bf16[8192,2048]{1,0:T(8,128)(2,1)} %h_ref.19), custom_call_target="tpu_custom_call" | custom-call | flops 4294967296 | bytes 24117248 | tf_op jit(solution)/shard_map/logits/pallas_call | solution.py:80
  265.3 18.8 %logits.14 = (f32[128,4096]{1,0:T(8,128)}, s16[128,4224]{1,0:T(8,128)(2,1)}) custom-call(bf16[256,4096]{1,0:T(8,128)(2,1)} %get-tuple-element.80.a_ref, bf16[8192,4096]{1,0:T(8,128)(2,1)} %h_ref.18), custom_call_target="tpu_custom_call" | custom-call | flops 8589934592 | bytes 41943040 | tf_op jit(solution)/shard_map/logits/pallas_call | solution.py:80
  285.4 1.5 collective-permute-start.22
  287.0 18.9 %logits.15 = (f32[128,4096]{1,0:T(8,128)}, s16[128,4224]{1,0:T(8,128)(2,1)}) custom-call(bf16[256,4096]{1,0:T(8,128)(2,1)} %get-tuple-element.80.a_ref, bf16[8192,4096]{1,0:T(8,128)(2,1)} %h_ref.18), custom_call_target="tpu_custom_call" | custom-call | flops 8589934592 | bytes 41943040 | tf_op jit(solution)/shard_map/logits/pallas_call | solution.py:80
  305.9 1.9 collective-permute-done.21.dp
  308.3 10.6 %collective-permute-done.22.dq = bf16[64,4096]{1,0:T(8,128)(2,1)S(1)} collective-permute-done((bf16[64,4096]{1,0:T(8,128)(2,1)S(1)}, bf16[64,4096]{1,0:T(8,128)(2,1)S(1)}, u32[]{:S(2)}, u32[]{:S(2)}) %collective-permute-start.22) | collective-permute-done | bytes 524320 | tf_op jit(solution)/shard_map/ppermute | solution.py:452
  319.7 18.3 %norm_grad.2 = f32[256,2048]{1,0:T(8,128)} custom-call(s32[1]{0:T(128)} %bitcast.t_ref, bf16[64,8192]{1,0:T(8,128)(2,1)} %get-tuple-element.42.own, bf16[64,8192]{1,0:T(8,128)(2,1)} %copy-done.8, bf16[64,8192]{1,0:T(8,128)(2,1)} %copy-done.9, bf16[64,4096]{1,0:T(8,128)(2,1)} %copy-done.19, bf16[64,4096]{1,0:T(8,128)(2,1)} %copy-done.20, ...), custom_call_target="tpu_custom_call" | custom-call | flops 8589934592 | bytes 37748736 | tf_op jit(solution)/shard_map/norm_grad/pallas_call | solution.py:326
  339.3 3.3 relay.12
  343.2 3.3 relay.13
  348.5 3.2 relay.14
  351.7 1.7 collective-permute-start.29
  354.4 3.3 relay.15
  362.7 6.3 %finish.6 = (f32[64,8192]{1,0:T(8,128)}, f32[64,128]{1,0:T(8,128)}) custom-call(s32[1]{0:T(128)} %bitcast.1.base_ref, f32[128,4096]{1,0:T(8,128)} %get-tuple-element.43.keep_ref.kp, f32[128,4096]{1,0:T(8,128)} %get-tuple-element.44.keep_ref.kq, s16[128,4224]{1,0:T(8,128)(2,1)} %copy-done.4, s16[128,4224]{1,0:T(8,128)(2,1)} %collective-permute-done.24.got_ref.gq, ...), custom_call_target="tpu_custom_call" | custom-call | flops 7864320 | bytes 6291456 | tf_op jit(solution)/shard_map/finish/pallas_call | solution.py:216
  370.0 5.8 %finish.7 = (f32[64,8192]{1,0:T(8,128)}, f32[64,128]{1,0:T(8,128)}) custom-call(f32[128,4096]{1,0:T(8,128)} %get-tuple-element.48.keep_ref.kp, f32[128,4096]{1,0:T(8,128)} %get-tuple-element.49.keep_ref.kq, s16[128,4224]{1,0:T(8,128)(2,1)} %copy-done.2, s16[128,4224]{1,0:T(8,128)(2,1)} %copy-done.3, s16[64,4224]{1,0:T(8,128)(2,1)} %copy-done.14, ...), custom_call_target="tpu_custom_call" | custom-call | flops 7864320 | bytes 6291456 | tf_op jit(solution)/shard_map/finish/pallas_call | solution.py:216
  378.0 3.4 collective-permute-start.32
  381.9 1.9 collective-permute-start.34
  383.9 2.7 collective-permute-done.32
  386.6 1.5 collective-permute-done.33
  388.1 2.3 collective-permute-done.34
  391.2 5.0 slope.3
  396.1 1.5 collective-permute-start.35
  397.6 1.5 collective-permute-start.36
  399.1 22.2 %collective-permute-done.35.gx = bf16[64,8192]{1,0:T(8,128)(2,1)S(1)} collective-permute-done((bf16[64,8192]{1,0:T(8,128)(2,1)}, bf16[64,8192]{1,0:T(8,128)(2,1)S(1)}, u32[]{:S(2)}, u32[]{:S(2)}) %collective-permute-start.35) | collective-permute-done | bytes 1048608 | tf_op jit(solution)/shard_map/ppermute | solution.py:449
  421.3 1.5 collective-permute-start.37
  422.9 1.5 collective-permute-start.38
  424.4 9.8 %collective-permute-done.37.dp = bf16[64,4096]{1,0:T(8,128)(2,1)S(1)} collective-permute-done((bf16[64,4096]{1,0:T(8,128)(2,1)S(1)}, bf16[64,4096]{1,0:T(8,128)(2,1)S(1)}, u32[]{:S(2)}, u32[]{:S(2)}) %collective-permute-start.37) | collective-permute-done | bytes 524320 | tf_op jit(solution)/shard_map/ppermute | solution.py:451
  436.3 18.3 %norm_grad.3 = f32[256,2048]{1,0:T(8,128)} custom-call(s32[1]{0:T(128)} %bitcast.t_ref, bf16[64,8192]{1,0:T(8,128)(2,1)} %get-tuple-element.55.own, bf16[64,8192]{1,0:T(8,128)(2,1)} %copy-done.10, bf16[64,8192]{1,0:T(8,128)(2,1)} %copy-done.11, bf16[64,4096]{1,0:T(8,128)(2,1)} %copy-done.21, bf16[64,4096]{1,0:T(8,128)(2,1)} %copy-done.22, ...), custom_call_target="tpu_custom_call" | custom-call | flops 8589934592 | bytes 37748736 | tf_op jit(solution)/shard_map/norm_grad/pallas_call | solution.py:326
  458.8 42.8 %reduce-scatter.5.cloned.1.call-done = f32[32,2048]{1,0:T(8,128)} async-done(((f32[256,2048]{1,0:T(8,128)}), f32[32,2048]{1,0:T(8,128)}) %reduce-scatter.5.cloned.1.call-update) | async-done | bytes 262160 | tf_op jit(solution)/shard_map/reduce_scatter | solution.py:457
  506.4 2.4 collective-permute-done.41
  (206 shorter events, 56.8 us)
Async XLA Ops:
  7.2 11.1 %copy-start.35 = (s32[8]{0:T(128)S(1)}, s32[8]{0:T(128)}, u32[]{:S(2)}) copy-start(s32[8]{0:T(128)} %constant.49.clone) | copy-start | bytes 100
  7.2 13.6 %copy-start.34 = (f32[2]{0:T(128)S(1)}, f32[2]{0:T(128)}, u32[]{:S(2)}) copy-start(f32[2]{0:T(128)} %constant.51) | copy-start | bytes 28
  7.2 5.2 copy-start.6
  7.2 5.3 %copy-start.12 = (bf16[64,4096]{1,0:T(8,128)(2,1)S(1)}, bf16[64,4096]{1,0:T(8,128)(2,1)}, u32[]{:S(2)}) copy-start(bf16[64,4096]{1,0:T(8,128)(2,1)} %param.9) | copy-start | bytes 1572868
  7.2 10.1 %copy-start.33 = (s32[512]{0:T(512)S(1)}, s32[512]{0:T(512)}, u32[]{:S(2)}) copy-start(s32[512]{0:T(512)} %param.15) | copy-start | bytes 6148
  7.2 27.3 %all-gather.9.cloned.1.call-start = ((), (), s32[]{:S(2)}) async-start(), calls=%async_computation.5 | async-start | bytes 1179648 | tf_op jit(solution)/shard_map/all_gather | solution.py:397
  9.1 48.8 %all-gather.5.cloned.1.call-start = ((), (), s32[]{:S(2)}) async-start(), calls=%async_computation.2 | async-start | bytes 1179648 | tf_op jit(solution)/shard_map/all_gather | solution.py:397
  9.8 82.4 %all-gather.11.cloned.1.call-start = ((), (), s32[]{:S(2)}) async-start(), calls=%async_computation.6 | async-start | bytes 2359296 | tf_op jit(solution)/shard_map/all_gather | solution.py:398
  11.7 107.2 %all-gather.7.cloned.1.call-start = ((), (), s32[]{:S(2)}) async-start(), calls=%async_computation.3 | async-start | bytes 2359296 | tf_op jit(solution)/shard_map/all_gather | solution.py:398
  12.3 445.5 %reduce-scatter.3.cloned.1.call-start = ((), (), s32[]{:S(2)}) async-start(), calls=%async_computation.4 | async-start | bytes 2359296 | tf_op jit(solution)/shard_map/reduce_scatter | solution.py:457
  12.8 5.5 %collective-permute-start.5 = (f32[2,64]{1,0:T(2,128)S(1)}, f32[2,64]{1,0:T(2,128)S(1)}, u32[]{:S(2)}, u32[]{:S(2)}) collective-permute-start(f32[2,64]{1,0:T(2,128)S(1)} %pad_maximum_fusion.7), channel_id=1, source_target_pairs={{0,2},{1,3},{2,0},{3,1},{4,6},{5,7},{6,4},{7,5},{8,10},{9,11},{10,... | collective-permute-start | bytes 1544 | tf_op jit(solution)/shard_map/ppermute | solution.py:353
  15.8 4.5 collective-permute-start.6
  17.2 3.6 collective-permute-start.4
  20.9 38.7 %copy-start.31 = (f32[2,64]{1,0:T(2,128)}, f32[2,64]{1,0:T(2,128)S(1)}, u32[]{:S(2)}) copy-start(f32[2,64]{1,0:T(2,128)S(1)} %get-tuple-element.59) | copy-start | bytes 1540
  20.9 1.2 collective-permute-start.7
  22.0 144.8 %collective-permute-start.8 = (f32[2,2,64]{2,1,0:T(2,128)S(1)}, f32[2,2,64]{2,1,0:T(2,128)S(1)}, u32[]{:S(2)}, u32[]{:S(2)}) collective-permute-start(f32[2,2,64]{2,1,0:T(2,128)S(1)} %pad_maximum_fusion.6), channel_id=1, source_target_pairs={{0,4},{4,0},{8,12},{12,8},{1,5},{5,1},{9,13},{13,9},{2,6},{6,2},{1... | collective-permute-start | bytes 3080 | tf_op jit(solution)/shard_map/ppermute | solution.py:365
  75.8 101.8 %collective-permute-start = (s16[128,4224]{1,0:T(8,128)(2,1)}, s16[128,4224]{1,0:T(8,128)(2,1)S(1)}, u32[]{:S(2)}, u32[]{:S(2)}) collective-permute-start(s16[128,4224]{1,0:T(8,128)(2,1)} %get-tuple-element.32), channel_id=1, source_target_pairs={{0,1},{1,0},{2,3},{3,2},{4,5},{5,4},{6,7},{7,6},{8,9},{9,8},{10,11... | collective-permute-start | bytes 3244040 | tf_op jit(solution)/shard_map/ppermute | solution.py:427
  90.7 91.7 %collective-permute-start.1 = (s16[128,4224]{1,0:T(8,128)(2,1)}, s16[128,4224]{1,0:T(8,128)(2,1)}, u32[]{:S(2)}, u32[]{:S(2)}) collective-permute-start(s16[128,4224]{1,0:T(8,128)(2,1)} %get-tuple-element.33), channel_id=1, source_target_pairs={{0,2},{1,3},{2,0},{3,1},{4,6},{5,7},{6,4},{7,5},{8,10},{9,11},{10,... | collective-permute-start | bytes 3244040 | tf_op jit(solution)/shard_map/ppermute | solution.py:428
  163.8 26.9 %collective-permute-start.11 = (s16[128,4224]{1,0:T(8,128)(2,1)}, s16[128,4224]{1,0:T(8,128)(2,1)S(1)}, u32[]{:S(2)}, u32[]{:S(2)}) collective-permute-start(s16[128,4224]{1,0:T(8,128)(2,1)} %get-tuple-element.37), channel_id=1, source_target_pairs={{0,1},{1,0},{2,3},{3,2},{4,5},{5,4},{6,7},{7,6},{8,9},{9,8},{10,11... | collective-permute-start | bytes 3244040 | tf_op jit(solution)/shard_map/ppermute | solution.py:427
  165.3 31.1 %collective-permute-start.12 = (s16[128,4224]{1,0:T(8,128)(2,1)}, s16[128,4224]{1,0:T(8,128)(2,1)S(1)}, u32[]{:S(2)}, u32[]{:S(2)}) collective-permute-start(s16[128,4224]{1,0:T(8,128)(2,1)} %get-tuple-element.38), channel_id=1, source_target_pairs={{0,2},{1,3},{2,0},{3,1},{4,6},{5,7},{6,4},{7,5},{8,10},{9,11},{10,... | collective-permute-start | bytes 3244040 | tf_op jit(solution)/shard_map/ppermute | solution.py:428
  166.8 4.5 collective-permute-start.9
  171.3 5.4 %collective-permute-start.10 = (f32[2,2,64]{2,1,0:T(2,128)S(1)}, f32[2,2,64]{2,1,0:T(2,128)S(1)}, u32[]{:S(2)}, u32[]{:S(2)}) collective-permute-start(f32[2,2,64]{2,1,0:T(2,128)S(1)} %pad_maximum_fusion.6), channel_id=1, source_target_pairs={{0,12},{4,8},{8,4},{12,0},{1,13},{5,9},{9,5},{13,1},{2,14},{6,10},... | collective-permute-start | bytes 3080 | tf_op jit(solution)/shard_map/ppermute | solution.py:365
  181.9 36.1 %collective-permute-start.2 = (s16[64,4224]{1,0:T(8,128)(2,1)}, s16[64,4224]{1,0:T(8,128)(2,1)}, u32[]{:S(2)}, u32[]{:S(2)}) collective-permute-start(s16[64,4224]{1,0:T(8,128)(2,1)} %relay.8), channel_id=1, source_target_pairs={{0,2},{1,3},{2,0},{3,1},{4,6},{5,7},{6,4},{7,5},{8,10},{9,11},{10,... | collective-permute-start | bytes 1622024 | tf_op jit(solution)/shard_map/ppermute | solution.py:429
  185.7 32.3 %collective-permute-start.3 = (s16[64,4224]{1,0:T(8,128)(2,1)}, s16[64,4224]{1,0:T(8,128)(2,1)}, u32[]{:S(2)}, u32[]{:S(2)}) collective-permute-start(s16[64,4224]{1,0:T(8,128)(2,1)} %relay.9), channel_id=1, source_target_pairs={{0,1},{1,0},{2,3},{3,2},{4,5},{5,4},{6,7},{7,6},{8,9},{9,8},{10,11... | collective-permute-start | bytes 1622024 | tf_op jit(solution)/shard_map/ppermute | solution.py:430
  195.0 29.3 %collective-permute-start.13 = (s16[64,4224]{1,0:T(8,128)(2,1)}, s16[64,4224]{1,0:T(8,128)(2,1)S(1)}, u32[]{:S(2)}, u32[]{:S(2)}) collective-permute-start(s16[64,4224]{1,0:T(8,128)(2,1)} %relay.10), channel_id=1, source_target_pairs={{0,2},{1,3},{2,0},{3,1},{4,6},{5,7},{6,4},{7,5},{8,10},{9,11},{10,... | collective-permute-start | bytes 1622024 | tf_op jit(solution)/shard_map/ppermute | solution.py:429
  200.7 23.6 %collective-permute-start.14 = (s16[64,4224]{1,0:T(8,128)(2,1)}, s16[64,4224]{1,0:T(8,128)(2,1)S(1)}, u32[]{:S(2)}, u32[]{:S(2)}) collective-permute-start(s16[64,4224]{1,0:T(8,128)(2,1)} %relay.11), channel_id=1, source_target_pairs={{0,1},{1,0},{2,3},{3,2},{4,5},{5,4},{6,7},{7,6},{8,9},{9,8},{10,11... | collective-permute-start | bytes 1622024 | tf_op jit(solution)/shard_map/ppermute | solution.py:430
  217.3 121.0 %collective-permute-start.23 = (s16[128,4224]{1,0:T(8,128)(2,1)}, s16[128,4224]{1,0:T(8,128)(2,1)S(1)}, u32[]{:S(2)}, u32[]{:S(2)}) collective-permute-start(s16[128,4224]{1,0:T(8,128)(2,1)} %get-tuple-element.45), channel_id=1, source_target_pairs={{0,1},{1,0},{2,3},{3,2},{4,5},{5,4},{6,7},{7,6},{8,9},{9,8},{10,11... | collective-permute-start | bytes 3244040 | tf_op jit(solution)/shard_map/ppermute | solution.py:427
  231.1 1.4 collective-permute-start.15
  233.2 4.4 collective-permute-start.16
  234.7 8.1 %collective-permute-start.17 = (f32[2,64,128]{2,1,0:T(8,128)S(1)}, f32[2,64,128]{2,1,0:T(8,128)S(1)}, u32[]{:S(2)}, u32[]{:S(2)}) collective-permute-start(f32[2,64,128]{2,1,0:T(8,128)S(1)} %pad_maximum_fusion.4), channel_id=1, source_target_pairs={{0,8},{4,12},{8,0},{12,4},{1,9},{5,13},{9,1},{13,5},{2,10},{6,14},... | collective-permute-start | bytes 196616 | tf_op jit(solution)/shard_map/ppermute | solution.py:365
  235.7 7.1 %collective-permute-start.18 = (f32[2,64,128]{2,1,0:T(8,128)S(1)}, f32[2,64,128]{2,1,0:T(8,128)S(1)}, u32[]{:S(2)}, u32[]{:S(2)}) collective-permute-start(f32[2,64,128]{2,1,0:T(8,128)S(1)} %pad_maximum_fusion.4), channel_id=1, source_target_pairs={{0,12},{4,8},{8,4},{12,0},{1,13},{5,9},{9,5},{13,1},{2,14},{6,10},... | collective-permute-start | bytes 196616 | tf_op jit(solution)/shard_map/ppermute | solution.py:365
  248.5 36.2 %collective-permute-start.19 = (bf16[64,8192]{1,0:T(8,128)(2,1)}, bf16[64,8192]{1,0:T(8,128)(2,1)S(1)}, u32[]{:S(2)}, u32[]{:S(2)}) collective-permute-start(bf16[64,8192]{1,0:T(8,128)(2,1)} %get-tuple-element.42.own), channel_id=1, source_target_pairs={{0,1},{1,0},{2,3},{3,2},{4,5},{5,4},{6,7},{7,6},{8,9},{9,8},{10,11... | collective-permute-start | bytes 3145736 | tf_op jit(solution)/shard_map/ppermute | solution.py:449
  249.9 35.4 %collective-permute-start.20 = (bf16[64,8192]{1,0:T(8,128)(2,1)}, bf16[64,8192]{1,0:T(8,128)(2,1)S(1)}, u32[]{:S(2)}, u32[]{:S(2)}) collective-permute-start(bf16[64,8192]{1,0:T(8,128)(2,1)} %get-tuple-element.42.own), channel_id=1, source_target_pairs={{0,2},{1,3},{2,0},{3,1},{4,6},{5,7},{6,4},{7,5},{8,10},{9,11},{10,... | collective-permute-start | bytes 3145736 | tf_op jit(solution)/shard_map/ppermute | solution.py:450
  263.9 79.3 %collective-permute-start.24 = (s16[128,4224]{1,0:T(8,128)(2,1)}, s16[128,4224]{1,0:T(8,128)(2,1)}, u32[]{:S(2)}, u32[]{:S(2)}) collective-permute-start(s16[128,4224]{1,0:T(8,128)(2,1)} %get-tuple-element.46), channel_id=1, source_target_pairs={{0,2},{1,3},{2,0},{3,1},{4,6},{5,7},{6,4},{7,5},{8,10},{9,11},{10,... | collective-permute-start | bytes 3244040 | tf_op jit(solution)/shard_map/ppermute | solution.py:428
  284.2 63.4 %collective-permute-start.27 = (s16[128,4224]{1,0:T(8,128)(2,1)}, s16[128,4224]{1,0:T(8,128)(2,1)S(1)}, u32[]{:S(2)}, u32[]{:S(2)}) collective-permute-start(s16[128,4224]{1,0:T(8,128)(2,1)} %get-tuple-element.50), channel_id=1, source_target_pairs={{0,1},{1,0},{2,3},{3,2},{4,5},{5,4},{6,7},{7,6},{8,9},{9,8},{10,11... | collective-permute-start | bytes 3244040 | tf_op jit(solution)/shard_map/ppermute | solution.py:427
  284.7 21.1 %copy-start.8 = (bf16[64,8192]{1,0:T(8,128)(2,1)}, bf16[64,8192]{1,0:T(8,128)(2,1)S(1)}, u32[]{:S(2)}) copy-start(bf16[64,8192]{1,0:T(8,128)(2,1)S(1)} %collective-permute-done.19.gx) | copy-start | bytes 3145732
  284.8 23.0 %collective-permute-start.21 = (bf16[64,4096]{1,0:T(8,128)(2,1)S(1)}, bf16[64,4096]{1,0:T(8,128)(2,1)S(1)}, u32[]{:S(2)}, u32[]{:S(2)}) collective-permute-start(bf16[64,4096]{1,0:T(8,128)(2,1)S(1)} %slice.88), channel_id=1, source_target_pairs={{0,2},{1,3},{2,0},{3,1},{4,6},{5,7},{6,4},{7,5},{8,10},{9,11},{10,... | collective-permute-start | bytes 1572872 | tf_op jit(solution)/shard_map/ppermute | solution.py:451
  285.4 20.5 %copy-start.9 = (bf16[64,8192]{1,0:T(8,128)(2,1)}, bf16[64,8192]{1,0:T(8,128)(2,1)S(1)}, u32[]{:S(2)}) copy-start(bf16[64,8192]{1,0:T(8,128)(2,1)S(1)} %collective-permute-done.20.gy) | copy-start | bytes 3145732
  285.4 33.5 %collective-permute-start.22 = (bf16[64,4096]{1,0:T(8,128)(2,1)S(1)}, bf16[64,4096]{1,0:T(8,128)(2,1)S(1)}, u32[]{:S(2)}, u32[]{:S(2)}) collective-permute-start(bf16[64,4096]{1,0:T(8,128)(2,1)S(1)} %slice.89), channel_id=1, source_target_pairs={{0,1},{1,0},{2,3},{3,2},{4,5},{5,4},{6,7},{7,6},{8,9},{9,8},{10,11... | collective-permute-start | bytes 1572872 | tf_op jit(solution)/shard_map/ppermute | solution.py:452
  307.7 11.2 %copy-start.19 = (bf16[64,4096]{1,0:T(8,128)(2,1)}, bf16[64,4096]{1,0:T(8,128)(2,1)S(1)}, u32[]{:S(2)}) copy-start(bf16[64,4096]{1,0:T(8,128)(2,1)S(1)} %collective-permute-done.21.dp) | copy-start | bytes 1572868
  307.7 45.7 %collective-permute-start.28 = (s16[128,4224]{1,0:T(8,128)(2,1)}, s16[128,4224]{1,0:T(8,128)(2,1)S(1)}, u32[]{:S(2)}, u32[]{:S(2)}) collective-permute-start(s16[128,4224]{1,0:T(8,128)(2,1)} %get-tuple-element.51), channel_id=1, source_target_pairs={{0,2},{1,3},{2,0},{3,1},{4,6},{5,7},{6,4},{7,5},{8,10},{9,11},{10,... | collective-permute-start | bytes 3244040 | tf_op jit(solution)/shard_map/ppermute | solution.py:428
  338.0 163.6 %reduce-scatter.5.cloned.1.call-start = ((), (), s32[]{:S(2)}) async-start(), calls=%async_computation.7 | async-start | bytes 2359296 | tf_op jit(solution)/shard_map/reduce_scatter | solution.py:457
  342.6 18.4 %collective-permute-start.25 = (s16[64,4224]{1,0:T(8,128)(2,1)}, s16[64,4224]{1,0:T(8,128)(2,1)S(1)}, u32[]{:S(2)}, u32[]{:S(2)}) collective-permute-start(s16[64,4224]{1,0:T(8,128)(2,1)} %relay.12), channel_id=1, source_target_pairs={{0,2},{1,3},{2,0},{3,1},{4,6},{5,7},{6,4},{7,5},{8,10},{9,11},{10,... | collective-permute-start | bytes 1622024 | tf_op jit(solution)/shard_map/ppermute | solution.py:429
  346.4 14.7 %collective-permute-start.26 = (s16[64,4224]{1,0:T(8,128)(2,1)}, s16[64,4224]{1,0:T(8,128)(2,1)S(1)}, u32[]{:S(2)}, u32[]{:S(2)}) collective-permute-start(s16[64,4224]{1,0:T(8,128)(2,1)} %relay.13), channel_id=1, source_target_pairs={{0,1},{1,0},{2,3},{3,2},{4,5},{5,4},{6,7},{7,6},{8,9},{9,8},{10,11... | collective-permute-start | bytes 1622024 | tf_op jit(solution)/shard_map/ppermute | solution.py:430
  351.7 6.7 %copy-start.30 = (s32[8,32]{1,0:T(8,128)S(1)}, s32[8,32]{1,0:T(8,128)}, u32[]{:S(2)}) copy-start(s32[8,32]{1,0:T(8,128)} %get-tuple-element.88) | copy-start | bytes 3076
  351.7 17.3 %collective-permute-start.29 = (s16[64,4224]{1,0:T(8,128)(2,1)}, s16[64,4224]{1,0:T(8,128)(2,1)S(1)}, u32[]{:S(2)}, u32[]{:S(2)}) collective-permute-start(s16[64,4224]{1,0:T(8,128)(2,1)} %relay.14), channel_id=1, source_target_pairs={{0,2},{1,3},{2,0},{3,1},{4,6},{5,7},{6,4},{7,5},{8,10},{9,11},{10,... | collective-permute-start | bytes 1622024 | tf_op jit(solution)/shard_map/ppermute | solution.py:429
  357.7 11.3 %collective-permute-start.30 = (s16[64,4224]{1,0:T(8,128)(2,1)}, s16[64,4224]{1,0:T(8,128)(2,1)S(1)}, u32[]{:S(2)}, u32[]{:S(2)}) collective-permute-start(s16[64,4224]{1,0:T(8,128)(2,1)} %relay.15), channel_id=1, source_target_pairs={{0,1},{1,0},{2,3},{3,2},{4,5},{5,4},{6,7},{7,6},{8,9},{9,8},{10,11... | collective-permute-start | bytes 1622024 | tf_op jit(solution)/shard_map/ppermute | solution.py:430
  375.8 1.4 collective-permute-start.31
  378.0 8.6 %collective-permute-start.32 = (f32[2,64,128]{2,1,0:T(8,128)S(1)}, f32[2,64,128]{2,1,0:T(8,128)S(1)}, u32[]{:S(2)}, u32[]{:S(2)}) collective-permute-start(f32[2,64,128]{2,1,0:T(8,128)S(1)} %pad_maximum_fusion.5), channel_id=1, source_target_pairs={{0,4},{4,0},{8,12},{12,8},{1,5},{5,1},{9,13},{13,9},{2,6},{6,2},{1... | collective-permute-start | bytes 196616 | tf_op jit(solution)/shard_map/ppermute | solution.py:365
  381.4 6.7 %collective-permute-start.33 = (f32[2,64,128]{2,1,0:T(8,128)S(1)}, f32[2,64,128]{2,1,0:T(8,128)S(1)}, u32[]{:S(2)}, u32[]{:S(2)}) collective-permute-start(f32[2,64,128]{2,1,0:T(8,128)S(1)} %pad_maximum_fusion.5), channel_id=1, source_target_pairs={{0,8},{4,12},{8,0},{12,4},{1,9},{5,13},{9,1},{13,5},{2,10},{6,14},... | collective-permute-start | bytes 196616 | tf_op jit(solution)/shard_map/ppermute | solution.py:365
  381.9 8.5 %collective-permute-start.34 = (f32[2,64,128]{2,1,0:T(8,128)S(1)}, f32[2,64,128]{2,1,0:T(8,128)S(1)}, u32[]{:S(2)}, u32[]{:S(2)}) collective-permute-start(f32[2,64,128]{2,1,0:T(8,128)S(1)} %pad_maximum_fusion.5), channel_id=1, source_target_pairs={{0,12},{4,8},{8,4},{12,0},{1,13},{5,9},{9,5},{13,1},{2,14},{6,10},... | collective-permute-start | bytes 196616 | tf_op jit(solution)/shard_map/ppermute | solution.py:365
  396.1 25.1 %collective-permute-start.35 = (bf16[64,8192]{1,0:T(8,128)(2,1)}, bf16[64,8192]{1,0:T(8,128)(2,1)S(1)}, u32[]{:S(2)}, u32[]{:S(2)}) collective-permute-start(bf16[64,8192]{1,0:T(8,128)(2,1)} %get-tuple-element.55.own), channel_id=1, source_target_pairs={{0,1},{1,0},{2,3},{3,2},{4,5},{5,4},{6,7},{7,6},{8,9},{9,8},{10,11... | collective-permute-start | bytes 3145736 | tf_op jit(solution)/shard_map/ppermute | solution.py:449
  397.6 25.2 %collective-permute-start.36 = (bf16[64,8192]{1,0:T(8,128)(2,1)}, bf16[64,8192]{1,0:T(8,128)(2,1)S(1)}, u32[]{:S(2)}, u32[]{:S(2)}) collective-permute-start(bf16[64,8192]{1,0:T(8,128)(2,1)} %get-tuple-element.55.own), channel_id=1, source_target_pairs={{0,2},{1,3},{2,0},{3,1},{4,6},{5,7},{6,4},{7,5},{8,10},{9,11},{10,... | collective-permute-start | bytes 3145736 | tf_op jit(solution)/shard_map/ppermute | solution.py:450
  421.2 14.2 %copy-start.10 = (bf16[64,8192]{1,0:T(8,128)(2,1)}, bf16[64,8192]{1,0:T(8,128)(2,1)S(1)}, u32[]{:S(2)}) copy-start(bf16[64,8192]{1,0:T(8,128)(2,1)S(1)} %collective-permute-done.35.gx) | copy-start | bytes 3145732
  421.3 12.9 %collective-permute-start.37 = (bf16[64,4096]{1,0:T(8,128)(2,1)S(1)}, bf16[64,4096]{1,0:T(8,128)(2,1)S(1)}, u32[]{:S(2)}, u32[]{:S(2)}) collective-permute-start(bf16[64,4096]{1,0:T(8,128)(2,1)S(1)} %slice.90), channel_id=1, source_target_pairs={{0,2},{1,3},{2,0},{3,1},{4,6},{5,7},{6,4},{7,5},{8,10},{9,11},{10,... | collective-permute-start | bytes 1572872 | tf_op jit(solution)/shard_map/ppermute | solution.py:451
  422.8 12.6 %copy-start.11 = (bf16[64,8192]{1,0:T(8,128)(2,1)}, bf16[64,8192]{1,0:T(8,128)(2,1)S(1)}, u32[]{:S(2)}) copy-start(bf16[64,8192]{1,0:T(8,128)(2,1)S(1)} %collective-permute-done.36.gy) | copy-start | bytes 3145732
  422.9 12.6 %collective-permute-start.38 = (bf16[64,4096]{1,0:T(8,128)(2,1)S(1)}, bf16[64,4096]{1,0:T(8,128)(2,1)S(1)}, u32[]{:S(2)}, u32[]{:S(2)}) collective-permute-start(bf16[64,4096]{1,0:T(8,128)(2,1)S(1)} %slice.91), channel_id=1, source_target_pairs={{0,1},{1,0},{2,3},{3,2},{4,5},{5,4},{6,7},{7,6},{8,9},{9,8},{10,11... | collective-permute-start | bytes 1572872 | tf_op jit(solution)/shard_map/ppermute | solution.py:452
  454.5 1.4 copy-start.28
  454.5 48.1 %copy-start.7 = (bf16[64,2048]{1,0:T(8,128)(2,1)S(1)}, bf16[64,2048]{1,0:T(8,128)(2,1)}, u32[]{:S(2)}) copy-start(bf16[64,2048]{1,0:T(8,128)(2,1)} %param.10) | copy-start | bytes 786436
  454.6 48.1 %copy-start.26 = (f32[2048]{0:T(1024)S(1)}, f32[2048]{0:T(1024)}, u32[]{:S(2)}) copy-start(f32[2048]{0:T(1024)} %param.12) | copy-start | bytes 24580
  454.6 51.8 %copy-start.32 = (f32[2,64]{1,0:T(2,128)S(1)}, f32[2,64]{1,0:T(2,128)}, u32[]{:S(2)}) copy-start(f32[2,64]{1,0:T(2,128)} %copy-done.31) | copy-start | bytes 1540
  502.9 3.5 collective-permute-start.40
  504.4 4.4 collective-permute-start.41
  505.8 3.5 collective-permute-start.39
  (20 other events, 17.6 us)
Sparse Core Ops, SparseCore 0:
  9.7 24.7 all-gather.8
  36.1 21.7 all-gather.4
  60.1 28.6 all-gather.10
  90.2 28.7 all-gather.6
  338.2 48.8 reduce-scatter.2
  454.7 46.8 reduce-scatter.4

commit v2 on v0

v2 whole, which is shorter than its diff:
```python
import functools
import jax
import jax.numpy as jnp
from jax import lax
from jax.experimental import pallas as pl
from jax.experimental.pallas import tpu as pltpu
from jax.sharding import PartitionSpec as P

heat = 2.0
blend = 0.5
grad_scale = 1024.0
epsilon = 1e-05

f32 = jnp.float32
VMEM_LIMIT = 56 * 1024 * 1024
LANES = 128
QUARTER = LANES // 2
PAD = 16
BLOCK_BYTES = 8 * 1024 * 1024

TOK_X = [(i, i ^ 1) for i in range(4)]
TOK_Y = [(i, i ^ 2) for i in range(4)]
TOK_D = [(i, i ^ 3) for i in range(4)]
SWAP = [(0, 1), (1, 0)]

VMEM = pl.BlockSpec(memory_space=pltpu.VMEM)
SMEM = pl.BlockSpec(memory_space=pltpu.SMEM)
ANY = pl.BlockSpec(memory_space=pl.ANY)
PARAMS = pltpu.CompilerParams(vmem_limit_bytes=VMEM_LIMIT)


LIGHT = pl.CostEstimate(flops=1024, bytes_accessed=1024, transcendentals=0)


def pow2(k):
    one = jnp.ones_like(k)
    a = jnp.left_shift(one, jnp.clip(k + 60, 0, 30)).astype(f32)
    b = jnp.left_shift(one, jnp.clip(k + 30, 0, 30)).astype(f32)
    c = jnp.left_shift(one, jnp.clip(k, 0, 30)).astype(f32)
    d = jnp.left_shift(one, jnp.clip(k - 30, 0, 30)).astype(f32)
    return (a * (2.0**-60)) * b * c * d


def encode(x):
    top = jnp.max(jnp.abs(x), axis=0, keepdims=True)
    e = jnp.ceil(jnp.log2(jnp.maximum(top, 2.0**-44))).astype(jnp.int32)
    e = jnp.clip(e, -44, 31)
    q = jnp.clip(jnp.round(x * pow2(15 - e)), -32767.0, 32767.0)
    return q.astype(jnp.int32).astype(jnp.int16), e


def decode(q, e):
    return q.astype(jnp.int32).astype(f32) * pow2(e - 15)


def low_lanes(shape):
    return lax.broadcasted_iota(jnp.int32, shape, 1) < QUARTER


def swap_lanes(x):
    return pltpu.roll(x, QUARTER, 1)


def row_is(shape, j):
    return lax.broadcasted_iota(jnp.int32, shape, 0) == j


ORDER = ((0, 2, 1, 3), (0, 1, 2, 3))


def logits_kernel(parts, tiles, tile, t_ref, rows_ref, gain_ref, h_ref, dep_ref, *refs):
    outs, (a_ref, exps) = refs[: 2 * len(parts)], refs[2 * len(parts) :]
    j = pl.program_id(0)

    @pl.when(j == 0)
    def _():
        t = t_ref[0]
        for k in range(4):
            place = pl.multiple_of(jnp.bitwise_xor(t, k) * QUARTER, QUARTER)
            w = rows_ref[pl.ds(place, QUARTER), :].astype(f32) * gain_ref[...]
            w = w.astype(jnp.bfloat16)
            for n, part in enumerate(parts):
                at = ORDER[part].index(k) * QUARTER
                a_ref[n, at : at + QUARTER, :] = w

    for n in range(len(parts)):
        keep_ref, send_ref = outs[2 * n], outs[2 * n + 1]
        half = send_ref.shape[0] - PAD

        @pl.when((j >= n * tiles) & (j < (n + 1) * tiles))
        def _():
            r = lax.dot_general(
                h_ref[...], a_ref[n], (((1,), (1,)), ((), ())), preferred_element_type=f32
            )
            keep_ref[...] = r[:, :LANES]
            q, e = encode(r[:, LANES:])
            at = j - n * tiles
            send_ref[pl.ds(pl.multiple_of(at * tile, tile), tile), :] = q
            before = jnp.where(at == 0, 0, exps[...])
            exps[...] = jnp.where(row_is((PAD, LANES), at), e, before)

            @pl.when(at == tiles - 1)
            def _():
                send_ref[half:, :] = exps[...].astype(jnp.int16)


def logits_tile(head):
    return min(BLOCK_BYTES // (2 * head.shape[1]), head.shape[0] // 2)


def partial_logits(t, rows, gain, head, parts, dep):
    count, width = rows.shape[0], head.shape[1]
    half = head.shape[0] // 2
    tile = logits_tile(head)
    tiles = half // tile
    first = parts[0] * tiles
    out_specs, out_shape = [], []
    for n in range(len(parts)):
        out_specs += [
            pl.BlockSpec(
                (tile, LANES), lambda j, n=n: (jnp.clip(j - n * tiles, 0, tiles - 1), 0)
            ),
            pl.BlockSpec((half + PAD, LANES), lambda j: (0, 0)),
        ]
        out_shape += [
            jax.ShapeDtypeStruct((half, LANES), f32),
            jax.ShapeDtypeStruct((half + PAD, LANES), jnp.int16),
        ]
    return pl.pallas_call(
        functools.partial(logits_kernel, parts, tiles, tile),
        grid=(len(parts) * tiles,),
        in_specs=[
            SMEM,
            pl.BlockSpec((count, width), lambda j: (0, 0)),
            pl.BlockSpec((1, width), lambda j: (0, 0)),
            pl.BlockSpec((tile, width), lambda j: (first + j, 0)),
            ANY,
        ],
        out_specs=out_specs,
        out_shape=out_shape,
        scratch_shapes=[
            pltpu.VMEM((len(parts), count, width), jnp.bfloat16),
            pltpu.VMEM((PAD, LANES), jnp.int32),
        ],
        compiler_params=PARAMS,
        cost_estimate=LIGHT,
        name="logits",
    )(t, rows, gain.reshape(1, width), head, dep)


def relay_kernel(step, tile, *refs):
    ins, outs, news = refs[:11], refs[11:15], refs[15:]
    n, steps = pl.program_id(0), pl.num_programs(0)
    for p in range(2):
        got_top, got_low, exps_ref, keep_top, keep_low = ins[5 * p : 5 * p + 5]
        next_ref, own_ref, new = outs[2 * p], outs[2 * p + 1], news[p]
        exps = exps_ref[...].astype(jnp.int32)

        def exponent(at):
            here = row_is(exps.shape, at // tile)
            return jnp.sum(jnp.where(here, exps, 0), axis=0, keepdims=True)

        top = keep_top[...] + decode(got_top[...], exponent(n * step))
        low = keep_low[...] + decode(got_low[...], exponent((steps + n) * step))
        mask = low_lanes(top.shape)
        own_ref[...] = jnp.where(mask, top, swap_lanes(low))
        q, e = encode(jnp.where(mask, swap_lanes(top), low))
        next_ref[pl.ds(pl.multiple_of(n * step, step), step), :] = q
        before = jnp.where(n == 0, 0, new[...])
        new[...] = jnp.where(row_is(new.shape, n), e, before)

        @pl.when(n == steps - 1)
        def _():
            next_ref[steps * step :, :] = new[...].astype(jnp.int16)


def relay(gots, keeps, tile, dep):
    half = keeps[0].shape[0]
    step = min(512, half // 2)
    steps = half // 2 // step
    top = pl.BlockSpec((step, LANES), lambda n: (n, 0))
    low = pl.BlockSpec((step, LANES), lambda n: (steps + n, 0))
    exps = pl.BlockSpec((PAD, LANES), lambda n: (half // PAD, 0))
    shapes = [
        jax.ShapeDtypeStruct((half // 2 + PAD, LANES), jnp.int16),
        jax.ShapeDtypeStruct((half // 2, LANES), f32),
    ]
    operands = []
    for got, keep in zip(gots, keeps):
        operands += [got, got, got, keep, keep]
    return pl.pallas_call(
        functools.partial(relay_kernel, step, tile),
        grid=(steps,),
        in_specs=[top, low, exps, top, low] * 2 + [ANY],
        out_specs=[pl.BlockSpec((half // 2 + PAD, LANES), lambda n: (0, 0)), top] * 2,
        out_shape=shapes * 2,
        scratch_shapes=[pltpu.VMEM((PAD, LANES), jnp.int32)] * 2,
        compiler_params=PARAMS,
        cost_estimate=LIGHT,
        name="relay",
    )(*operands, dep)


def merged(op, x):
    return op(x, swap_lanes(x))


def summed(owns, lasts, inv, out_ref):
    top = None
    for p in range(2):
        packed = owns[p].shape[0]
        step = min(512, packed)
        exps = lasts[p][packed : packed + PAD, :].astype(jnp.int32)
        for n in range(packed // step):
            rows = slice(n * step, (n + 1) * step)
            x = owns[p][rows, :] + decode(lasts[p][rows, :], exps[n : n + 1, :])
            x = x * inv
            out_ref[p * packed + n * step : p * packed + (n + 1) * step, :] = x
            high = jnp.max(x, axis=0, keepdims=True)
            top = high if top is None else jnp.maximum(top, high)
    return merged(jnp.maximum, top)


def places(shape, at, packed):
    part, start = at // packed, at % packed
    row = lax.broadcasted_iota(jnp.int32, shape, 0) + (2 * part * packed + start)
    return jnp.where(low_lanes(shape), row, row + packed)


def student_kernel(op, oq, lp, lq, inv_ref, target_ref, base_ref, dep, out_ref, stats_ref):
    packed = op.shape[0]
    step = min(512, packed)
    top = summed((op, oq), (lp, lq), inv_ref[...], out_ref)
    soft = jnp.zeros((1, LANES), f32)
    plain = jnp.zeros((1, LANES), f32)
    hit = jnp.zeros((1, LANES), f32)
    target = target_ref[...] - base_ref[0]
    for n in range(2 * packed // step):
        x = out_ref[n * step : (n + 1) * step, :]
        warm = jnp.exp((x - top) * (1.0 / heat))
        soft = soft + jnp.sum(warm, axis=0, keepdims=True)
        plain = plain + jnp.sum(warm * warm, axis=0, keepdims=True)
        here = places(x.shape, n * step, packed) == target
        hit = hit + jnp.sum(jnp.where(here, x, 0.0), axis=0, keepdims=True)
    stats = jnp.zeros((8, LANES), f32)
    sums = [merged(jnp.add, v) for v in (soft, plain, hit)]
    for n, value in enumerate([top] + sums):
        stats = jnp.where(row_is(stats.shape, n), value, stats)
    stats_ref[...] = stats


def teacher_kernel(op, oq, lp, lq, inv_ref, student_ref, before_ref, dep, out_ref, stats_ref):
    packed = op.shape[0]
    step = min(512, packed)
    top = summed((op, oq), (lp, lq), inv_ref[...], out_ref)
    top = top * (1.0 / heat)
    total = jnp.zeros((1, LANES), f32)
    cross = jnp.zeros((1, LANES), f32)
    for n in range(2 * packed // step):
        rows = slice(n * step, (n + 1) * step)
        x = out_ref[rows, :]
        power = jnp.exp(x * (1.0 / heat) - top)
        total = total + jnp.sum(power, axis=0, keepdims=True)
        gap = (x - student_ref[rows, :]) * (1.0 / heat)
        cross = cross + jnp.sum(power * gap, axis=0, keepdims=True)
    stats = before_ref[...]
    sums = [merged(jnp.add, v) for v in (total, cross)]
    for n, value in enumerate([top] + sums):
        stats = jnp.where(row_is(stats.shape, 4 + n), value, stats)
    stats_ref[...] = stats


def finish(body, owns, lasts, inv, extra, dep):
    packed = owns[0].shape[0]
    last_spec = SMEM if body is student_kernel else VMEM
    return pl.pallas_call(
        body,
        in_specs=[VMEM] * 6 + [last_spec, ANY],
        out_specs=[VMEM] * 2,
        out_shape=[
            jax.ShapeDtypeStruct((2 * packed, LANES), f32),
            jax.ShapeDtypeStruct((8, LANES), f32),
        ],
        compiler_params=PARAMS,
        cost_estimate=LIGHT,
        name="finish",
    )(*owns, *lasts, inv, *extra, dep)


def tree_sum(parts):
    while len(parts) > 1:
        parts = [a + b for a, b in zip(parts[::2], parts[1::2])]
    return parts[0]


def slope_kernel(
    student_ref, teacher_ref, stats_ref, target_ref, base_ref, dep, grad_ref, loss_ref
):
    packed = student_ref.shape[0] // 2
    step = min(512, packed)
    sets = [stats_ref[k] for k in range(stats_ref.shape[0])]
    top = functools.reduce(jnp.maximum, sets)

    def scaled(row, top_row, rate):
        high = top[top_row : top_row + 1]
        return tree_sum(
            [s[row : row + 1] * jnp.exp((s[top_row : top_row + 1] - high) * rate) for s in sets]
        )

    student_top, teacher_top = top[0:1], top[4:5]
    soft_total = scaled(1, 0, 1.0 / heat)
    plain_total = scaled(2, 0, 1.0)
    teacher_total = scaled(5, 4, 1.0)
    cross_total = scaled(6, 4, 1.0)
    label = tree_sum([s[3:4] for s in sets])
    row_loss = blend * heat**2 * (
        cross_total / teacher_total
        - teacher_top
        - jnp.log(teacher_total)
        + student_top / heat
        + jnp.log(soft_total)
    ) + (1.0 - blend) * (student_top + jnp.log(plain_total) - label)
    soft_rate = grad_scale * blend * heat / soft_total
    teacher_rate = grad_scale * blend * heat / teacher_total
    plain_rate = grad_scale * (1.0 - blend) / plain_total
    inner = jnp.zeros((1, LANES), f32)
    target = target_ref[...] - base_ref[0]
    for n in range(2 * packed // step):
        rows = slice(n * step, (n + 1) * step)
        logits = student_ref[rows, :]
        warm = jnp.exp((logits - student_top) * (1.0 / heat))
        power = jnp.exp(teacher_ref[rows, :] * (1.0 / heat) - teacher_top)
        g = warm * (soft_rate + plain_rate * warm) - power * teacher_rate
        here = places(g.shape, n * step, packed) == target
        g = jnp.where(here, g - grad_scale * (1.0 - blend), g)
        g = g.astype(jnp.bfloat16).astype(f32)
        inner = inner + jnp.sum(g * logits, axis=0, keepdims=True)
        g = jnp.transpose(g).astype(jnp.bfloat16)
        at = 2 * (n * step // packed) * packed + (n * step) % packed
        grad_ref[:, at : at + step] = g[:QUARTER]
        grad_ref[:, at + packed : at + packed + step] = g[QUARTER:]
    rows_out = jnp.where(row_is((8, LANES), 0), row_loss, 0.0)
    loss_ref[...] = jnp.where(row_is((8, LANES), 1), merged(jnp.add, inner), rows_out)


def slope(base, student, teacher, stats, targets, dep):
    return pl.pallas_call(
        slope_kernel,
        in_specs=[VMEM] * 4 + [SMEM, ANY],
        out_specs=[VMEM] * 2,
        out_shape=[
            jax.ShapeDtypeStruct((QUARTER, 2 * student.shape[0]), jnp.bfloat16),
            jax.ShapeDtypeStruct((8, LANES), f32),
        ],
        compiler_params=PARAMS,
        cost_estimate=LIGHT,
        name="slope",
    )(student, teacher, stats, targets, base, dep)


def norm_grad_kernel(t_ref, flip_ref, own, gx, gy, dp, dq, h_ref, dep, keep_ref, send_ref, lhs):
    half = dp.shape[1]

    @pl.when(pl.program_id(0) == 0)
    def _():
        for n, ref in enumerate((own, gx, gy)):
            lhs[n * QUARTER : (n + 1) * QUARTER, :] = ref[...]
        lhs[3 * QUARTER :, :half] = dp[...]
        lhs[3 * QUARTER :, half:] = dq[...]

    r = jnp.dot(lhs[...], h_ref[...], preferred_element_type=f32)
    t = jnp.bitwise_xor(t_ref[0], 2 * flip_ref[0])
    for n in range(4):
        quarter = jnp.bitwise_xor(t, n)
        at = pl.ds(pl.multiple_of(lax.rem(quarter, 2) * QUARTER, QUARTER), QUARTER)

        @pl.when(quarter < 2)
        def _():
            keep_ref[at, :] = r[n * QUARTER : (n + 1) * QUARTER]

        @pl.when(quarter >= 2)
        def _():
            send_ref[at, :] = r[n * QUARTER : (n + 1) * QUARTER]


def norm_gradient(t, flip, own, gx, gy, dp, dq, head, dep):
    vocab, width = head.shape
    tile = min(512, width)
    full = pl.BlockSpec((QUARTER, vocab), lambda j: (0, 0))
    part = pl.BlockSpec((QUARTER, vocab // 2), lambda j: (0, 0))
    return pl.pallas_call(
        norm_grad_kernel,
        grid=(width // tile,),
        in_specs=[SMEM, SMEM, full, full, full, part, part]
        + [pl.BlockSpec((vocab, tile), lambda j: (0, j)), ANY],
        out_specs=[pl.BlockSpec((2 * QUARTER, tile), lambda j: (0, j))] * 2,
        out_shape=[jax.ShapeDtypeStruct((2 * QUARTER, width), f32)] * 2,
        scratch_shapes=[pltpu.VMEM((4 * QUARTER, vocab), jnp.bfloat16)],
        compiler_params=PARAMS,
        cost_estimate=LIGHT,
        name="norm_grad",
    )(t, flip, own, gx, gy, dp, dq, head, dep)


def row_encode(x):
    top = jnp.max(jnp.abs(x), axis=1, keepdims=True)
    e = jnp.ceil(jnp.log2(jnp.maximum(top, 2.0**-44))).astype(jnp.int32)
    e = jnp.clip(e, -44, 44)
    q = jnp.clip(jnp.round(x * pow2(15 - e)), -32767.0, 32767.0)
    return q.astype(jnp.int32).astype(jnp.int16), e


def fold_kernel(z_ref, mine_ref, other_ref, own_ref, *sends):
    rows, width = own_ref.shape
    for k in range(4):
        at = pl.ds(pl.multiple_of(jnp.bitwise_xor(z_ref[0], k) * rows, rows), rows)
        x = mine_ref[at, :] + other_ref[at, :]
        if k == 0:
            own_ref[...] = x
        else:
            q, e = row_encode(x)
            sends[k - 1][:, :width] = q
            sends[k - 1][:, width:] = jnp.broadcast_to(e, (rows, LANES)).astype(jnp.int16)


def fold(z, mine, other):
    rows, width = other.shape
    return pl.pallas_call(
        fold_kernel,
        grid=(1,),
        in_specs=[
            SMEM,
            pl.BlockSpec((rows, width), lambda j: (0, 0)),
            pl.BlockSpec((rows, width), lambda j: (0, 0)),
        ],
        out_specs=[VMEM] * 4,
        out_shape=[jax.ShapeDtypeStruct((rows // 4, width), f32)]
        + [jax.ShapeDtypeStruct((rows // 4, width + LANES), jnp.int16)] * 3,
        compiler_params=PARAMS,
        cost_estimate=LIGHT,
        name="fold",
    )(z, mine, other)


def last_kernel(own_ref, p1, p2, p3, hidden_ref, gain_ref, inv_ref, inner_ref, out_ref):
    width = own_ref.shape[1]
    norm = own_ref[...]
    for p in (p1, p2, p3):
        e = p[:, width:].astype(jnp.int32)[:, :1]
        norm = norm + p[:, :width].astype(jnp.int32).astype(f32) * pow2(e - 15)
    out = inv_ref[...] * gain_ref[...] * norm - hidden_ref[...].astype(f32) * inner_ref[...]
    out_ref[...] = out.astype(jnp.bfloat16)


def last(own, gots, hidden, gain, inv, inner):
    return pl.pallas_call(
        last_kernel,
        in_specs=[VMEM] * 8,
        out_specs=VMEM,
        out_shape=jax.ShapeDtypeStruct(own.shape, jnp.bfloat16),
        compiler_params=PARAMS,
        cost_estimate=LIGHT,
        name="hidden_grad",
    )(own, *gots, hidden, gain.reshape(1, -1), inv[:, None], inner[:, None])


def tok_sum(x):
    a = lax.ppermute(x, "tok", TOK_X)
    b = lax.ppermute(x, "tok", TOK_Y)
    c = lax.ppermute(x, "tok", TOK_D)
    return (x + a) + (b + c)


def small_box():
    return lax.axis_size("grp") == 2 and lax.axis_size("vocab") == 4


def along_z(x):
    return [x] + [lax.ppermute(x, "vocab", [(i, i ^ k) for i in range(4)]) for k in range(1, 4)]


def range_gather(x, ordered):
    if not small_box():
        return lax.all_gather(x, ("grp", "vocab"), axis=0)
    own = jnp.stack(along_z(x))
    sets = jnp.concatenate([own, lax.ppermute(own, "grp", SWAP)])
    if ordered:
        sets = sets[jnp.bitwise_xor(lax.axis_index(("grp", "vocab")), jnp.arange(8))]
    return sets


def on_device(
    teacher_hidden,
    student_hidden,
    teacher_gain,
    student_gain,
    teacher_head,
    student_head,
    target_ids,
):
    blocks = lax.axis_size("grp") * lax.axis_size("vocab")
    own_rows = teacher_hidden.shape[0]
    all_rows = blocks * own_rows
    part_rows = own_rows // 2
    vocab_local = teacher_head.shape[0]
    half = vocab_local // 2
    teacher_width = teacher_hidden.shape[1] * lax.axis_size("tok")
    student_width = student_hidden.shape[1] * lax.axis_size("tok")
    t = lax.axis_index("tok")
    t_arr = t.astype(jnp.int32).reshape(1)
    base = (lax.axis_index(("grp", "vocab")) * vocab_local).astype(jnp.int32).reshape(1)

    halves = [slice(0, part_rows), slice(part_rows, own_rows)]

    def gather_rows(x, after=None):
        if after is not None:
            x, _ = lax.optimization_barrier((x, after))
        return lax.all_gather(x, ("grp", "vocab"), axis=0, tiled=True)

    if small_box():
        near = along_z(student_hidden[halves[0]])
        sets = jnp.stack(near)
        sets = jnp.concatenate([sets, lax.ppermute(sets, "grp", SWAP)])
        place = jnp.bitwise_xor(lax.axis_index(("grp", "vocab")), jnp.arange(blocks))
        student_a = sets[place].reshape(blocks * part_rows, -1)
        first = near[1]
    else:
        student_a = gather_rows(student_hidden[halves[0]])
        first = student_a
    teacher_a = gather_rows(teacher_hidden[halves[0]], first)

    student_wide, teacher_wide, _ = lax.optimization_barrier(
        (student_hidden, teacher_hidden, first)
    )
    student_wide, teacher_wide = student_wide.astype(f32), teacher_wide.astype(f32)
    squares = jnp.stack(
        [jnp.sum(student_wide * student_wide, axis=1), jnp.sum(teacher_wide * teacher_wide, axis=1)]
    )
    squares = tok_sum(squares)
    widths = jnp.array([[student_width], [teacher_width]], f32)
    inverse = lax.rsqrt(squares / widths + epsilon)
    four = inverse.reshape(4, part_rows).T
    high = lax.reduce_precision(four, 8, 7)
    mid = lax.reduce_precision(four - high, 8, 7)
    pieces = jnp.concatenate([high, mid, four - high - mid], axis=1)
    pieces = jnp.pad(pieces, ((0, 0), (0, LANES - 12))).astype(jnp.bfloat16)
    student_b_own = jnp.concatenate([student_hidden[halves[1]], pieces], axis=1)
    targets = target_ids.reshape(blocks, own_rows)

    def mine(x):
        x = lax.dynamic_slice_in_dim(x, t * QUARTER, QUARTER)
        return jnp.concatenate([x, x]).reshape(1, LANES)

    def start(rows, gain, head, dep):
        keep_p, send_p, keep_q, send_q = partial_logits(t_arr, rows, gain, head, (0, 1), dep)
        gots = (lax.ppermute(send_p, "tok", TOK_X), lax.ppermute(send_q, "tok", TOK_Y))
        return gots, (keep_p, keep_q), keep_q

    def onward(gots, keeps, head, dep):
        next_p, own_p, next_q, own_q = relay(gots, keeps, logits_tile(head), dep)
        last_p = lax.ppermute(next_p, "tok", TOK_Y)
        last_q = lax.ppermute(next_q, "tok", TOK_X)
        return (own_p, own_q), (last_p, last_q), own_q

    def share(grad):
        gx = lax.ppermute(grad, "tok", TOK_X)
        gy = lax.ppermute(grad, "tok", TOK_Y)
        corner = (gx[:, :half], gy[:, half:])
        dp = lax.ppermute(corner[0], "tok", TOK_Y)
        dq = lax.ppermute(corner[1], "tok", TOK_X)
        return (grad, gx, gy, dp, dq), corner[0]

    row_targets = [mine(targets[:, rows].reshape(-1)) for rows in halves]

    student, teacher = (student_gain, student_head), (teacher_gain, teacher_head)
    gots_sa, keeps_sa, dep = start(student_a, *student, base)
    student_b = gather_rows(student_b_own, dep)
    gots_ta, keeps_ta, dep = start(teacher_a, *teacher, dep)
    own_sa, last_sa, dep = onward(gots_sa, keeps_sa, student_head, dep)
    teacher_b = gather_rows(teacher_hidden[halves[1]], dep)
    gots_sb, keeps_sb, dep = start(student_b, *student, dep)
    pieces = student_b[:, student_hidden.shape[1] :].astype(f32)
    pieces = (pieces[:, 0:4] + pieces[:, 4:8]) + pieces[:, 8:12]
    inv_s, inv_t = [mine(pieces[:, k]) for k in (0, 1)], [mine(pieces[:, k]) for k in (2, 3)]
    logits_sa, stats = finish(
        student_kernel, own_sa, last_sa, inv_s[0], (row_targets[0], base), dep
    )
    own_ta, last_ta, dep = onward(gots_ta, keeps_ta, teacher_head, stats)
    gots_tb, keeps_tb, dep = start(teacher_b, *teacher, dep)
    logits_ta, stats_a = finish(
        teacher_kernel, own_ta, last_ta, inv_t[0], (logits_sa, stats), dep
    )
    own_sb, last_sb, dep = onward(gots_sb, keeps_sb, student_head, stats_a)
    all_a = range_gather(stats_a, False)
    own_tb, last_tb, dep = onward(gots_tb, keeps_tb, teacher_head, dep)
    grad_a, loss_a = slope(base, logits_sa, logits_ta, all_a, row_targets[0], dep)
    grads_a, corner = share(grad_a)
    logits_sb, stats = finish(
        student_kernel, own_sb, last_sb, inv_s[1], (row_targets[1], base), grad_a
    )
    logits_tb, stats_b = finish(
        teacher_kernel, own_tb, last_tb, inv_t[1], (logits_sb, stats), stats
    )
    all_b = range_gather(stats_b, False)
    grad_b, loss_b = slope(base, logits_sb, logits_tb, all_b, row_targets[1], corner)
    grads_b, _ = share(grad_b)

    infos = range_gather(jnp.stack([loss_a, loss_b]), False)
    inner = tree_sum([infos[k, :, 1, :QUARTER] for k in range(blocks)])
    losses = loss_a[0, :QUARTER] + loss_b[0, :QUARTER]
    shared = jnp.concatenate([inner, losses[None]])
    sets = [shared] + [lax.ppermute(shared, "tok", way) for way in (TOK_X, TOK_Y, TOK_D)]
    loss = jnp.sum(((sets[0] + sets[1]) + (sets[2] + sets[3]))[2]) / all_rows
    me = lax.axis_index(("grp", "vocab"))
    holder = me * part_rows // QUARTER
    inner = lax.dynamic_index_in_dim(jnp.stack(sets), jnp.bitwise_xor(t, holder), 0, False)
    inner = lax.dynamic_slice_in_dim(inner[:2], me * part_rows % QUARTER, part_rows, 1)
    own_inv = inverse[0]
    scale = [own_inv[rows] ** 2 * inner[n] / student_width for n, rows in enumerate(halves)]

    flip = lax.axis_index("grp").astype(jnp.int32).reshape(1) * int(small_box())

    def result(grads, part, dep):
        rows = halves[part]
        hidden, inv = student_hidden[rows], own_inv[rows]
        mine, other = norm_gradient(t_arr, flip, *grads, student_head, dep)
        if small_box():
            other = lax.ppermute(other, "grp", SWAP)
            z = lax.axis_index("vocab").astype(jnp.int32).reshape(1)
            own, *sends = fold(z, mine, other)
            gots = [
                lax.ppermute(x, "vocab", [(i, i ^ k) for i in range(4)])
                for k, x in enumerate(sends, 1)
            ]
            return last(own, gots, hidden, student_gain, inv, scale[part]), own
        norm = jnp.concatenate([mine, other])
        norm = lax.psum_scatter(norm, ("grp", "vocab"), scatter_dimension=0, tiled=True)
        out = inv[:, None] * student_gain * norm - hidden.astype(f32) * scale[part][:, None]
        return out.astype(jnp.bfloat16), mine

    out_a, dep = result(grads_a, 0, grad_b)
    out_b, _ = result(grads_b, 1, dep)
    return (loss, jnp.concatenate([out_a, out_b]))


def solution(mesh):
    in_specs = (
        P(("grp", "vocab"), "tok"),
        P(("grp", "vocab"), "tok"),
        P("tok"),
        P("tok"),
        P(("grp", "vocab"), "tok"),
        P(("grp", "vocab"), "tok"),
        P(),
    )
    out_specs = (P(), P(("grp", "vocab"), "tok"))
    return jax.shard_map(
        on_device, mesh=mesh, in_specs=in_specs, out_specs=out_specs, check_vma=False
    )
```

time: 681 us -> 396 us (0.58)
  waiting for transfers between devices: 476 us -> 85.7 us
  Pallas kernels: 0 us -> 192 us
  matrix products: 92.8 us -> 0 us
  blocking collectives: 67.5 us -> 0 us
  starting transfers between devices: 0.24 us -> 61.9 us
  local copies, waits for them, and re-layouts: 2.12 us -> 23.7 us
  other arithmetic: 25.3 us -> 10.2 us
    reduce_scatter x3 -> x0, waiting for transfers between devices: 337 us -> none  [the longest x1 137 us: on_device(): lax.psum_scatter(members[1], 'tok', scatter_dimension=0, tiled=True)]
    pallas_call x0 -> x20, Pallas kernels: none -> 192 us  [the longest x4 95.8 us: partial_logits(): pl.pallas_call(functools.partial(logits_kernel, parts, tiles, tile), grid...]
    all_gather x3, waiting for transfers between devices: 138 us -> 0.01 us  [gather_rows(): return lax.all_gather(x, ('grp', 'vocab'), axis=0, tiled=True)]
    dot_general x3 -> x0, matrix products: 92.8 us -> none  [the longest x1 42.2 us: on_device(): lax.dot_general(teacher_weighted, teacher_head, contract, preferred_eleme...]
    ppermute x0 -> x54, waiting for transfers between devices: none -> 85.6 us  [the longest x2 37 us: share(): dq = lax.ppermute(corner[1], 'tok', TOK_X)]
    ppermute x0 -> x54, starting transfers between devices: none -> 61.6 us  [the longest x12 19.2 us: along_z(): lax.ppermute(x, 'vocab', [(i, i ^ k) for i in range(4)])]
    psum x3 -> x0, blocking collectives: 34.4 us -> none  [the longest x1 13.7 us: on_device(): lax.psum((jnp.sum(mentor_power, axis=1), jnp.sum(mentor_power * score_gap...]
    pmax x2 -> x0, blocking collectives: 33.1 us -> none  [on_device(): lax.pmax((jnp.max(mentor_warmed_scores, axis=1), jnp.max(learner_score_ta...]
  transfers between devices with their start and end apart: 6 -> 57, of which waited for: 5 -> 18; matrix products, arithmetic and copies ran while one was open for 11% -> 5% of each run, Pallas kernels for 0% -> 49%
where the time goes in v2:
time: 396 us; the launch traced here: 389 us
  Pallas kernels  192 us (48%)
  waiting for transfers between devices  85.7 us (22%)
  starting transfers between devices  61.9 us (16%)
  local copies, waits for them, and re-layouts  23.7 us (6%)
  between operations  16.3 us (4%)
  other arithmetic  10.2 us (3%)
    pallas_call x4, Pallas kernels, partial_logits(): pl.pallas_call(functools.partial(logits_kernel, parts, tiles, tile), grid...  95.8 us
    ppermute x2, waiting for transfers between devices, share(): dq = lax.ppermute(corner[1], 'tok', TOK_X)  37 us
    pallas_call x2, Pallas kernels, norm_gradient(): pl.pallas_call(norm_grad_kernel, grid=(width // tile,), in_specs=[SMEM, S...  33.8 us
    pallas_call x4, Pallas kernels, relay(): pl.pallas_call(functools.partial(relay_kernel, step, tile), grid=(steps,)...  24.9 us
    ppermute x12, starting transfers between devices, along_z(): lax.ppermute(x, 'vocab', [(i, i ^ k) for i in range(4)])  19.2 us
    pallas_call x4, Pallas kernels, finish(): pl.pallas_call(body, in_specs=[VMEM] * 6 + [last_spec, ANY], out_specs=[V...  17.9 us
    ppermute x12, waiting for transfers between devices, along_z(): lax.ppermute(x, 'vocab', [(i, i ^ k) for i in range(4)])  12.8 us
    unnamed x98, local copies, waits for them, and re-layouts  12.5 us
  transfers between devices with their start and end apart: 57, of which 18 were waited for; matrix products, arithmetic and copies ran while one was open for 5% of the time, Pallas kernels for 49%

profile of v2, /device:TPU:0, one launch (start us, length us, event | category | flops | bytes accessed | tf_op | source)
XLA Modules:
  0.0 389.4 jit_solution(609319612311382057)
XLA Ops:
  8.3 5.1 %collective-permute-start.2 = (bf16[32,2048]{1,0:T(8,128)(2,1)S(1)}, bf16[32,2048]{1,0:T(8,128)(2,1)S(1)}, u32[]{:S(2)}, u32[]{:S(2)}) collective-permute-start(bf16[32,2048]{1,0:T(8,128)(2,1)S(1)} %get-tuple-element.127.hidden_ref), channel_id=1, source_target_pairs={{0,12},{4,8},{8,4},{12,0},{1,13},{5,9},{9,5},{13,1},{2,14},{6,10},... | collective-permute-start | bytes 393224 | tf_op jit(solution)/shard_map/ppermute | solution.py:479
  14.1 1.9 fusion.18
  15.9 5.9 %collective-permute-done = bf16[32,2048]{1,0:T(8,128)(2,1)S(1)} collective-permute-done((bf16[32,2048]{1,0:T(8,128)(2,1)S(1)}, bf16[32,2048]{1,0:T(8,128)(2,1)S(1)}, u32[]{:S(2)}, u32[]{:S(2)}) %collective-permute-start) | collective-permute-done | bytes 131104 | tf_op jit(solution)/shard_map/ppermute | solution.py:479
  22.4 1.6 collective-permute-start.9
  24.0 1.4 collective-permute-start.10
  26.2 2.3 collective-permute-done.10
  30.0 1.6 gather_fusion
  31.6 17.7 %logits.4 = (f32[4096,128]{1,0:T(8,128)}, s16[4112,128]{1,0:T(8,128)(2,1)}, f32[4096,128]{1,0:T(8,128)}, s16[4112,128]{1,0:T(8,128)(2,1)}) custom-call(s32[1]{0:T(128)} %bitcast.t_ref, bf16[256,2048]{1,0:T(8,128)(2,1)} %bitcast.80, f32[1,2048]{1,0:T(1,128)} %bitcast.84, bf16[8192,2048]{1,0:T(8,128)(2,1)} %h_ref.11, s32[1]{0:T(128)} %bitcast.8.dep_ref.base_ref), custom_call_target="tpu_custom_call" | custom-call | flops 1024 | bytes 1024 | tf_op jit(solution)/shard_map/logits/pallas_call | solution.py:129
  51.7 30.2 %logits.5 = (f32[4096,128]{1,0:T(8,128)}, s16[4112,128]{1,0:T(8,128)(2,1)}, f32[4096,128]{1,0:T(8,128)}, s16[4112,128]{1,0:T(8,128)(2,1)}) custom-call(s32[1]{0:T(128)} %bitcast.t_ref, bf16[256,4096]{1,0:T(8,128)(2,1)} %all-gather.4.cloned.1.call-done.rows_ref, f32[1,4096]{1,0:T(1,128)} %bitcast.88, bf16[8192,4096]{1,0:T(8,128)(2,1)} %h_ref.9, ...), custom_call_target="tpu_custom_call" | custom-call | flops 1024 | bytes 1024 | tf_op jit(solution)/shard_map/logits/pallas_call | solution.py:129
  83.3 6.1 %relay.4 = (s16[2064,128]{1,0:T(8,128)(2,1)}, f32[2048,128]{1,0:T(8,128)}, s16[2064,128]{1,0:T(8,128)(2,1)}, f32[2048,128]{1,0:T(8,128)}) custom-call(s16[4112,128]{1,0:T(8,128)(2,1)} %copy-done.4, s16[4112,128]{1,0:T(8,128)(2,1)} %copy-done.4, s16[4112,128]{1,0:T(8,128)(2,1)} %copy-done.4, f32[4096,128]{1,0:T(8,128)} %get-tuple-element.64.refs_3_.refs_4_, ...), custom_call_target="tpu_custom_call" | custom-call | flops 1024 | bytes 1024 | tf_op jit(solution)/shard_map/relay/pallas_call | solution.py:191
  89.5 1.5 collective-permute-start.11
  96.3 18.0 %logits.6 = (f32[4096,128]{1,0:T(8,128)}, s16[4112,128]{1,0:T(8,128)(2,1)}, f32[4096,128]{1,0:T(8,128)}, s16[4112,128]{1,0:T(8,128)(2,1)}) custom-call(s32[1]{0:T(128)} %bitcast.t_ref, bf16[256,2176]{1,0:T(8,128)(2,1)} %all-gather.6.cloned.1.call-done.rows_ref, f32[1,2048]{1,0:T(1,128)} %bitcast.85, bf16[8192,2048]{1,0:T(8,128)(2,1)} %h_ref.11, ...), custom_call_target="tpu_custom_call" | custom-call | flops 1024 | bytes 1024 | tf_op jit(solution)/shard_map/logits/pallas_call | solution.py:129
  114.3 1.7 collective-permute-start.21
  116.0 11.2 %collective-permute-done.6.lp = s16[2064,128]{1,0:T(8,128)(2,1)S(1)} collective-permute-done((s16[2064,128]{1,0:T(8,128)(2,1)}, s16[2064,128]{1,0:T(8,128)(2,1)S(1)}, u32[]{:S(2)}, u32[]{:S(2)}) %collective-permute-start.6) | collective-permute-done | bytes 528416 | tf_op jit(solution)/shard_map/ppermute | solution.py:561
  128.1 1.5 collective-permute-start.22
  130.9 4.4 %finish.4 = (f32[4096,128]{1,0:T(8,128)}, f32[8,128]{1,0:T(8,128)}) custom-call(f32[2048,128]{1,0:T(8,128)} %get-tuple-element.69.op, f32[2048,128]{1,0:T(8,128)} %get-tuple-element.70.dep_ref.oq, s16[2064,128]{1,0:T(8,128)(2,1)} %copy-done.20, s16[2064,128]{1,0:T(8,128)(2,1)} %copy-done.21, f32[1,128]{1,0:T(1,128)} %maximum_bitcast_fusion.inv_ref, ...), custom_call_target="tpu_custom_call" | custom-call | flops 1024 | bytes 1024 | tf_op jit(solution)/shard_map/finish/pallas_call | solution.py:276
  136.3 6.1 %relay.5 = (s16[2064,128]{1,0:T(8,128)(2,1)}, f32[2048,128]{1,0:T(8,128)}, s16[2064,128]{1,0:T(8,128)(2,1)}, f32[2048,128]{1,0:T(8,128)}) custom-call(s16[4112,128]{1,0:T(8,128)(2,1)} %copy-done.2, s16[4112,128]{1,0:T(8,128)(2,1)} %copy-done.2, s16[4112,128]{1,0:T(8,128)(2,1)} %copy-done.2, f32[4096,128]{1,0:T(8,128)} %get-tuple-element.79.refs_3_.refs_4_, ...), custom_call_target="tpu_custom_call" | custom-call | flops 1024 | bytes 1024 | tf_op jit(solution)/shard_map/relay/pallas_call | solution.py:191
  143.6 29.9 %logits.7 = (f32[4096,128]{1,0:T(8,128)}, s16[4112,128]{1,0:T(8,128)(2,1)}, f32[4096,128]{1,0:T(8,128)}, s16[4112,128]{1,0:T(8,128)(2,1)}) custom-call(s32[1]{0:T(128)} %bitcast.t_ref, bf16[256,4096]{1,0:T(8,128)(2,1)} %all-gather.8.cloned.1.call-done.rows_ref, f32[1,4096]{1,0:T(1,128)} %bitcast.89, bf16[8192,4096]{1,0:T(8,128)(2,1)} %h_ref.9, ...), custom_call_target="tpu_custom_call" | custom-call | flops 1024 | bytes 1024 | tf_op jit(solution)/shard_map/logits/pallas_call | solution.py:129
  173.4 1.6 collective-permute-start.19
  175.0 1.5 collective-permute-start.20
  176.5 1.3 reshape.155
  181.3 4.6 %finish.5 = (f32[4096,128]{1,0:T(8,128)}, f32[8,128]{1,0:T(8,128)}) custom-call(f32[2048,128]{1,0:T(8,128)} %get-tuple-element.82.op, f32[2048,128]{1,0:T(8,128)} %get-tuple-element.83.dep_ref.oq, s16[2064,128]{1,0:T(8,128)(2,1)} %collective-permute-done.13.lp, s16[2064,128]{1,0:T(8,128)(2,1)} %collective-permute-done.14.lq, ...), custom_call_target="tpu_custom_call" | custom-call | flops 1024 | bytes 1024 | tf_op jit(solution)/shard_map/finish/pallas_call | solution.py:276
  185.9 1.9 collective-permute-start.17
  187.8 1.1 collective-permute-start.16
  188.9 1.4 collective-permute-start.15
  191.0 6.1 %relay.6 = (s16[2064,128]{1,0:T(8,128)(2,1)}, f32[2048,128]{1,0:T(8,128)}, s16[2064,128]{1,0:T(8,128)(2,1)}, f32[2048,128]{1,0:T(8,128)}) custom-call(s16[4112,128]{1,0:T(8,128)(2,1)} %copy-done, s16[4112,128]{1,0:T(8,128)(2,1)} %copy-done, s16[4112,128]{1,0:T(8,128)(2,1)} %copy-done, f32[4096,128]{1,0:T(8,128)} %get-tuple-element.94.refs_3_.refs_4_, ...), custom_call_target="tpu_custom_call" | custom-call | flops 1024 | bytes 1024 | tf_op jit(solution)/shard_map/relay/pallas_call | solution.py:191
  198.4 1.5 collective-permute-done.20.refs_5_.refs_6_.refs_7_
  199.9 6.5 %relay.7 = (s16[2064,128]{1,0:T(8,128)(2,1)}, f32[2048,128]{1,0:T(8,128)}, s16[2064,128]{1,0:T(8,128)(2,1)}, f32[2048,128]{1,0:T(8,128)}) custom-call(s16[4112,128]{1,0:T(8,128)(2,1)} %copy-done.3, s16[4112,128]{1,0:T(8,128)(2,1)} %copy-done.3, s16[4112,128]{1,0:T(8,128)(2,1)} %copy-done.3, f32[4096,128]{1,0:T(8,128)} %get-tuple-element.91.refs_3_.refs_4_, ...), custom_call_target="tpu_custom_call" | custom-call | flops 1024 | bytes 1024 | tf_op jit(solution)/shard_map/relay/pallas_call | solution.py:191
  206.4 2.5 collective-permute-start.25
  210.2 5.1 %slope.2 = (bf16[64,8192]{1,0:T(8,128)(2,1)}, f32[8,128]{1,0:T(8,128)}) custom-call(f32[4096,128]{1,0:T(8,128)} %get-tuple-element.77.student_ref, f32[4096,128]{1,0:T(8,128)} %get-tuple-element.88.teacher_ref, f32[8,8,128]{2,1,0:T(8,128)} %copy-done.33, s32[1,128]{1,0:T(1,128)} %add_bitcast_fusion.target_ref, s32[1]{0:T(128)} %bitcast.8.dep_ref.base_ref, ...), custom_call_target="tpu_custom_call" | custom-call | flops 1024 | bytes 1024 | tf_op jit(solution)/shard_map/slope/pallas_call | solution.py:347
  215.4 1.4 collective-permute-start.31
  217.6 4.4 %finish.6 = (f32[4096,128]{1,0:T(8,128)}, f32[8,128]{1,0:T(8,128)}) custom-call(f32[2048,128]{1,0:T(8,128)} %get-tuple-element.99.op, f32[2048,128]{1,0:T(8,128)} %get-tuple-element.96.refs_10_.oq, s16[2064,128]{1,0:T(8,128)(2,1)} %copy-done.16, s16[2064,128]{1,0:T(8,128)(2,1)} %copy-done.17, f32[1,128]{1,0:T(1,128)} %maximum_bitcast_fusion.2.inv_ref, ...), custom_call_target="tpu_custom_call" | custom-call | flops 1024 | bytes 1024 | tf_op jit(solution)/shard_map/finish/pallas_call | solution.py:276
  222.1 2.0 collective-permute-done.26.lq
  224.9 4.6 %finish.7 = (f32[4096,128]{1,0:T(8,128)}, f32[8,128]{1,0:T(8,128)}) custom-call(f32[2048,128]{1,0:T(8,128)} %get-tuple-element.104.op, f32[2048,128]{1,0:T(8,128)} %get-tuple-element.97.dep.oq, s16[2064,128]{1,0:T(8,128)(2,1)} %copy-done.18, s16[2064,128]{1,0:T(8,128)(2,1)} %copy-done.19, f32[1,128]{1,0:T(1,128)} %maximum_bitcast_fusion.3.inv_ref, ...), custom_call_target="tpu_custom_call" | custom-call | flops 1024 | bytes 1024 | tf_op jit(solution)/shard_map/finish/pallas_call | solution.py:276
  229.5 1.9 collective-permute-start.29
  232.2 1.7 collective-permute-start.27
  236.8 1.2 collective-permute-done.30
  238.0 6.3 %collective-permute-done.31.gx = bf16[64,8192]{1,0:T(8,128)(2,1)S(1)} collective-permute-done((bf16[64,8192]{1,0:T(8,128)(2,1)}, bf16[64,8192]{1,0:T(8,128)(2,1)S(1)}, u32[]{:S(2)}, u32[]{:S(2)}) %collective-permute-start.31) | collective-permute-done | bytes 1048608 | tf_op jit(solution)/shard_map/ppermute | solution.py:566
  245.2 5.1 %slope.3 = (bf16[64,8192]{1,0:T(8,128)(2,1)}, f32[8,128]{1,0:T(8,128)}) custom-call(f32[4096,128]{1,0:T(8,128)} %get-tuple-element.103.student_ref, f32[4096,128]{1,0:T(8,128)} %get-tuple-element.108.teacher_ref, f32[8,8,128]{2,1,0:T(8,128)} %copy-done.34, s32[1,128]{1,0:T(1,128)} %add_bitcast_fusion.1.target_ref, s32[1]{0:T(128)} %bitcast.8.dep_ref.base_ref, ...), custom_call_target="tpu_custom_call" | custom-call | flops 1024 | bytes 1024 | tf_op jit(solution)/shard_map/slope/pallas_call | solution.py:347
  250.8 1.5 collective-permute-start.46
  252.9 1.5 collective-permute-start.40
  254.4 31.6 %collective-permute-done.41.dq = bf16[64,4096]{1,0:T(8,128)(2,1)S(1)} collective-permute-done((bf16[64,4096]{1,0:T(8,128)(2,1)S(1)}, bf16[64,4096]{1,0:T(8,128)(2,1)S(1)}, u32[]{:S(2)}, u32[]{:S(2)}) %collective-permute-start.41) | collective-permute-done | bytes 524320 | tf_op jit(solution)/shard_map/ppermute | solution.py:570
  287.0 16.8 %norm_grad.2 = (f32[128,2048]{1,0:T(8,128)}, f32[128,2048]{1,0:T(8,128)}) custom-call(s32[1]{0:T(128)} %bitcast.t_ref, s32[1]{0:T(128)} %bitcast.35.flip_ref, bf16[64,8192]{1,0:T(8,128)(2,1)} %get-tuple-element.102.dep.own, bf16[64,8192]{1,0:T(8,128)(2,1)} %copy-done.9, bf16[64,8192]{1,0:T(8,128)(2,1)} %copy-done.8, bf16[64,4096]{1,0:T(8,128)(2,1)} %copy-done.25, ...), custom_call_target="tpu_custom_call" | custom-call | flops 1024 | bytes 1024 | tf_op jit(solution)/shard_map/norm_grad/pallas_call | solution.py:391
  304.0 2.5 collective-permute-start.32
  306.5 2.0 collective-permute-done.33
  308.5 2.0 collective-permute-start.34
  310.6 3.4 collective-permute-done.34
  314.0 1.8 collective-permute-start.49
  315.8 1.1 collective-permute-start.48
  316.9 1.1 collective-permute-start.37
  318.8 1.7 collective-permute-start.36
  320.5 2.6 fold.2
  323.1 5.4 %collective-permute-done.49.dq = bf16[64,4096]{1,0:T(8,128)(2,1)S(1)} collective-permute-done((bf16[64,4096]{1,0:T(8,128)(2,1)S(1)}, bf16[64,4096]{1,0:T(8,128)(2,1)S(1)}, u32[]{:S(2)}, u32[]{:S(2)}) %collective-permute-start.49) | collective-permute-done | bytes 524320 | tf_op jit(solution)/shard_map/ppermute | solution.py:570
  328.4 1.6 collective-permute-done.48.dp
  330.8 17.0 %norm_grad.3 = (f32[128,2048]{1,0:T(8,128)}, f32[128,2048]{1,0:T(8,128)}) custom-call(s32[1]{0:T(128)} %bitcast.t_ref, s32[1]{0:T(128)} %bitcast.35.flip_ref, bf16[64,8192]{1,0:T(8,128)(2,1)} %get-tuple-element.111.dep.own, bf16[64,8192]{1,0:T(8,128)(2,1)} %copy-done.7, bf16[64,8192]{1,0:T(8,128)(2,1)} %copy-done.6, bf16[64,4096]{1,0:T(8,128)(2,1)} %copy-done.23, ...), custom_call_target="tpu_custom_call" | custom-call | flops 1024 | bytes 1024 | tf_op jit(solution)/shard_map/norm_grad/pallas_call | solution.py:391
  351.8 2.6 collective-permute-start.44
  354.3 1.8 collective-permute-start.45
  357.1 2.6 fold.3
  359.7 2.6 collective-permute-start.52
  362.3 1.8 collective-permute-start.53
  366.5 2.0 hidden_grad.2
  368.6 8.6 %collective-permute-done.52.p2 = s16[32,2176]{1,0:T(8,128)(2,1)S(1)} collective-permute-done((s16[32,2176]{1,0:T(8,128)(2,1)}, s16[32,2176]{1,0:T(8,128)(2,1)S(1)}, u32[]{:S(2)}, u32[]{:S(2)}) %collective-permute-start.52) | collective-permute-done | bytes 139296 | tf_op jit(solution)/shard_map/ppermute | solution.py:632
  377.8 2.0 hidden_grad.3
  379.9 1.7 pad_maximum_fusion.1
  (236 shorter events, 42.4 us)
Async XLA Ops:
  7.2 44.5 %all-gather.4.cloned.1.call-start = ((), (), s32[]{:S(2)}) async-start(), calls=%async_computation | async-start | bytes 2359296 | tf_op jit(solution)/shard_map/all_gather | solution.py:518
  8.3 21.0 %copy-start.13 = (bf16[32,2048]{1,0:T(8,128)(2,1)}, bf16[32,2048]{1,0:T(8,128)(2,1)S(1)}, u32[]{:S(2)}) copy-start(bf16[32,2048]{1,0:T(8,128)(2,1)S(1)} %get-tuple-element.128.hidden_ref) | copy-start | bytes 393220
  8.3 17.6 %collective-permute-start.2 = (bf16[32,2048]{1,0:T(8,128)(2,1)S(1)}, bf16[32,2048]{1,0:T(8,128)(2,1)S(1)}, u32[]{:S(2)}, u32[]{:S(2)}) collective-permute-start(bf16[32,2048]{1,0:T(8,128)(2,1)S(1)} %get-tuple-element.127.hidden_ref), channel_id=1, source_target_pairs={{0,12},{4,8},{8,4},{12,0},{1,13},{5,9},{9,5},{13,1},{2,14},{6,10},... | collective-permute-start | bytes 393224 | tf_op jit(solution)/shard_map/ppermute | solution.py:479
  13.4 12.5 %collective-permute-start.1 = (bf16[32,2048]{1,0:T(8,128)(2,1)S(1)}, bf16[32,2048]{1,0:T(8,128)(2,1)S(1)}, u32[]{:S(2)}, u32[]{:S(2)}) collective-permute-start(bf16[32,2048]{1,0:T(8,128)(2,1)S(1)} %get-tuple-element.127.hidden_ref), channel_id=1, source_target_pairs={{0,8},{4,12},{8,0},{12,4},{1,9},{5,13},{9,1},{13,5},{2,10},{6,14},... | collective-permute-start | bytes 393224 | tf_op jit(solution)/shard_map/ppermute | solution.py:479
  13.4 8.4 %collective-permute-start = (bf16[32,2048]{1,0:T(8,128)(2,1)S(1)}, bf16[32,2048]{1,0:T(8,128)(2,1)S(1)}, u32[]{:S(2)}, u32[]{:S(2)}) collective-permute-start(bf16[32,2048]{1,0:T(8,128)(2,1)S(1)} %get-tuple-element.127.hidden_ref), channel_id=1, source_target_pairs={{0,4},{4,0},{8,12},{12,8},{1,5},{5,1},{9,13},{13,9},{2,6},{6,2},{1... | collective-permute-start | bytes 393224 | tf_op jit(solution)/shard_map/ppermute | solution.py:479
  21.9 72.6 %all-gather.6.cloned.1.call-start = ((), (), s32[]{:S(2)}) async-start(), calls=%async_computation.1 | async-start | bytes 1253376 | tf_op jit(solution)/shard_map/all_gather | solution.py:518
  22.4 3.8 collective-permute-start.9
  24.0 4.5 %collective-permute-start.10 = (f32[2,64]{1,0:T(2,128)S(1)}, f32[2,64]{1,0:T(2,128)S(1)}, u32[]{:S(2)}, u32[]{:S(2)}) collective-permute-start(f32[2,64]{1,0:T(2,128)S(1)} %pad_maximum_fusion.8), channel_id=1, source_target_pairs={{0,3},{1,2},{2,1},{3,0},{4,7},{5,6},{6,5},{7,4},{8,11},{9,10},{10,... | collective-permute-start | bytes 1544 | tf_op jit(solution)/shard_map/ppermute | solution.py:470
  25.4 3.6 collective-permute-start.8
  26.0 4.0 %collective-permute-start.3 = (bf16[4,32,2048]{2,1,0:T(8,128)(2,1)S(1)}, bf16[4,32,2048]{2,1,0:T(8,128)(2,1)S(1)}, u32[]{:S(2)}, u32[]{:S(2)}) collective-permute-start(bf16[4,32,2048]{2,1,0:T(8,128)(2,1)S(1)} %pad_maximum_fusion), channel_id=1, source_target_pairs={{0,16},{16,0},{1,17},{17,1},{2,18},{18,2},{3,19},{19,3},{4,20},{20... | collective-permute-start | bytes 1572872 | tf_op jit(solution)/shard_map/ppermute | solution.py:523
  49.4 94.2 %all-gather.8.cloned.1.call-start = ((), (), s32[]{:S(2)}) async-start(), calls=%async_computation.2 | async-start | bytes 2359296 | tf_op jit(solution)/shard_map/all_gather | solution.py:518
  49.6 32.3 %collective-permute-start.4 = (s16[4112,128]{1,0:T(8,128)(2,1)}, s16[4112,128]{1,0:T(8,128)(2,1)S(1)}, u32[]{:S(2)}, u32[]{:S(2)}) collective-permute-start(s16[4112,128]{1,0:T(8,128)(2,1)} %get-tuple-element.63), channel_id=1, source_target_pairs={{0,1},{1,0},{2,3},{3,2},{4,5},{5,4},{6,7},{7,6},{8,9},{9,8},{10,11... | collective-permute-start | bytes 3158024 | tf_op jit(solution)/shard_map/ppermute | solution.py:556
  50.7 31.3 %collective-permute-start.5 = (s16[4112,128]{1,0:T(8,128)(2,1)}, s16[4112,128]{1,0:T(8,128)(2,1)S(1)}, u32[]{:S(2)}, u32[]{:S(2)}) collective-permute-start(s16[4112,128]{1,0:T(8,128)(2,1)} %get-tuple-element.65), channel_id=1, source_target_pairs={{0,2},{1,3},{2,0},{3,1},{4,6},{5,7},{6,4},{7,5},{8,10},{9,11},{10,... | collective-permute-start | bytes 3158024 | tf_op jit(solution)/shard_map/ppermute | solution.py:556
  89.5 45.8 %collective-permute-start.11 = (s16[4112,128]{1,0:T(8,128)(2,1)}, s16[4112,128]{1,0:T(8,128)(2,1)S(1)}, u32[]{:S(2)}, u32[]{:S(2)}) collective-permute-start(s16[4112,128]{1,0:T(8,128)(2,1)} %get-tuple-element.78), channel_id=1, source_target_pairs={{0,1},{1,0},{2,3},{3,2},{4,5},{5,4},{6,7},{7,6},{8,9},{9,8},{10,11... | collective-permute-start | bytes 3158024 | tf_op jit(solution)/shard_map/ppermute | solution.py:556
  91.0 44.3 %collective-permute-start.12 = (s16[4112,128]{1,0:T(8,128)(2,1)}, s16[4112,128]{1,0:T(8,128)(2,1)}, u32[]{:S(2)}, u32[]{:S(2)}) collective-permute-start(s16[4112,128]{1,0:T(8,128)(2,1)} %get-tuple-element.80), channel_id=1, source_target_pairs={{0,2},{1,3},{2,0},{3,1},{4,6},{5,7},{6,4},{7,5},{8,10},{9,11},{10,... | collective-permute-start | bytes 3158024 | tf_op jit(solution)/shard_map/ppermute | solution.py:556
  93.5 33.8 %collective-permute-start.6 = (s16[2064,128]{1,0:T(8,128)(2,1)}, s16[2064,128]{1,0:T(8,128)(2,1)S(1)}, u32[]{:S(2)}, u32[]{:S(2)}) collective-permute-start(s16[2064,128]{1,0:T(8,128)(2,1)} %get-tuple-element.71), channel_id=1, source_target_pairs={{0,2},{1,3},{2,0},{3,1},{4,6},{5,7},{6,4},{7,5},{8,10},{9,11},{10,... | collective-permute-start | bytes 1585160 | tf_op jit(solution)/shard_map/ppermute | solution.py:561
  95.3 34.8 %collective-permute-start.7 = (s16[2064,128]{1,0:T(8,128)(2,1)}, s16[2064,128]{1,0:T(8,128)(2,1)S(1)}, u32[]{:S(2)}, u32[]{:S(2)}) collective-permute-start(s16[2064,128]{1,0:T(8,128)(2,1)} %get-tuple-element.72), channel_id=1, source_target_pairs={{0,1},{1,0},{2,3},{3,2},{4,5},{5,4},{6,7},{7,6},{8,9},{9,8},{10,11... | collective-permute-start | bytes 1585160 | tf_op jit(solution)/shard_map/ppermute | solution.py:562
  114.3 73.5 %collective-permute-start.21 = (s16[4112,128]{1,0:T(8,128)(2,1)}, s16[4112,128]{1,0:T(8,128)(2,1)S(1)}, u32[]{:S(2)}, u32[]{:S(2)}) collective-permute-start(s16[4112,128]{1,0:T(8,128)(2,1)} %get-tuple-element.93), channel_id=1, source_target_pairs={{0,1},{1,0},{2,3},{3,2},{4,5},{5,4},{6,7},{7,6},{8,9},{9,8},{10,11... | collective-permute-start | bytes 3158024 | tf_op jit(solution)/shard_map/ppermute | solution.py:556
  128.1 60.8 %collective-permute-start.22 = (s16[4112,128]{1,0:T(8,128)(2,1)}, s16[4112,128]{1,0:T(8,128)(2,1)S(1)}, u32[]{:S(2)}, u32[]{:S(2)}) collective-permute-start(s16[4112,128]{1,0:T(8,128)(2,1)} %get-tuple-element.95), channel_id=1, source_target_pairs={{0,2},{1,3},{2,0},{3,1},{4,6},{5,7},{6,4},{7,5},{8,10},{9,11},{10,... | collective-permute-start | bytes 3158024 | tf_op jit(solution)/shard_map/ppermute | solution.py:556
  142.4 32.6 %collective-permute-start.13 = (s16[2064,128]{1,0:T(8,128)(2,1)}, s16[2064,128]{1,0:T(8,128)(2,1)}, u32[]{:S(2)}, u32[]{:S(2)}) collective-permute-start(s16[2064,128]{1,0:T(8,128)(2,1)} %get-tuple-element.84), channel_id=1, source_target_pairs={{0,2},{1,3},{2,0},{3,1},{4,6},{5,7},{6,4},{7,5},{8,10},{9,11},{10,... | collective-permute-start | bytes 1585160 | tf_op jit(solution)/shard_map/ppermute | solution.py:561
  143.0 38.3 %collective-permute-start.14 = (s16[2064,128]{1,0:T(8,128)(2,1)}, s16[2064,128]{1,0:T(8,128)(2,1)}, u32[]{:S(2)}, u32[]{:S(2)}) collective-permute-start(s16[2064,128]{1,0:T(8,128)(2,1)} %get-tuple-element.85), channel_id=1, source_target_pairs={{0,1},{1,0},{2,3},{3,2},{4,5},{5,4},{6,7},{7,6},{8,9},{9,8},{10,11... | collective-permute-start | bytes 1585160 | tf_op jit(solution)/shard_map/ppermute | solution.py:562
  173.4 25.0 %collective-permute-start.19 = (s16[4112,128]{1,0:T(8,128)(2,1)}, s16[4112,128]{1,0:T(8,128)(2,1)S(1)}, u32[]{:S(2)}, u32[]{:S(2)}) collective-permute-start(s16[4112,128]{1,0:T(8,128)(2,1)} %get-tuple-element.90), channel_id=1, source_target_pairs={{0,1},{1,0},{2,3},{3,2},{4,5},{5,4},{6,7},{7,6},{8,9},{9,8},{10,11... | collective-permute-start | bytes 3158024 | tf_op jit(solution)/shard_map/ppermute | solution.py:556
  175.0 24.9 %collective-permute-start.20 = (s16[4112,128]{1,0:T(8,128)(2,1)}, s16[4112,128]{1,0:T(8,128)(2,1)}, u32[]{:S(2)}, u32[]{:S(2)}) collective-permute-start(s16[4112,128]{1,0:T(8,128)(2,1)} %get-tuple-element.92), channel_id=1, source_target_pairs={{0,2},{1,3},{2,0},{3,1},{4,6},{5,7},{6,4},{7,5},{8,10},{9,11},{10,... | collective-permute-start | bytes 3158024 | tf_op jit(solution)/shard_map/ppermute | solution.py:556
  185.9 11.3 %collective-permute-start.17 = (f32[8,128]{1,0:T(8,128)}, f32[8,128]{1,0:T(8,128)S(1)}, u32[]{:S(2)}, u32[]{:S(2)}) collective-permute-start(f32[8,128]{1,0:T(8,128)} %get-tuple-element.89.refs_10_), channel_id=1, source_target_pairs={{0,12},{4,8},{8,4},{12,0},{1,13},{5,9},{9,5},{13,1},{2,14},{6,10},... | collective-permute-start | bytes 12296 | tf_op jit(solution)/shard_map/ppermute | solution.py:479
  187.8 10.0 %collective-permute-start.16 = (f32[8,128]{1,0:T(8,128)}, f32[8,128]{1,0:T(8,128)S(1)}, u32[]{:S(2)}, u32[]{:S(2)}) collective-permute-start(f32[8,128]{1,0:T(8,128)} %get-tuple-element.89.refs_10_), channel_id=1, source_target_pairs={{0,8},{4,12},{8,0},{12,4},{1,9},{5,13},{9,1},{13,5},{2,10},{6,14},... | collective-permute-start | bytes 12296 | tf_op jit(solution)/shard_map/ppermute | solution.py:479
  188.9 9.5 %collective-permute-start.15 = (f32[8,128]{1,0:T(8,128)}, f32[8,128]{1,0:T(8,128)S(1)}, u32[]{:S(2)}, u32[]{:S(2)}) collective-permute-start(f32[8,128]{1,0:T(8,128)} %get-tuple-element.89.refs_10_), channel_id=1, source_target_pairs={{0,4},{4,0},{8,12},{12,8},{1,5},{5,1},{9,13},{13,9},{2,6},{6,2},{1... | collective-permute-start | bytes 12296 | tf_op jit(solution)/shard_map/ppermute | solution.py:479
  197.2 18.2 %collective-permute-start.23 = (s16[2064,128]{1,0:T(8,128)(2,1)}, s16[2064,128]{1,0:T(8,128)(2,1)S(1)}, u32[]{:S(2)}, u32[]{:S(2)}) collective-permute-start(s16[2064,128]{1,0:T(8,128)(2,1)} %get-tuple-element.100), channel_id=1, source_target_pairs={{0,2},{1,3},{2,0},{3,1},{4,6},{5,7},{6,4},{7,5},{8,10},{9,11},{10,... | collective-permute-start | bytes 1585160 | tf_op jit(solution)/shard_map/ppermute | solution.py:561
  197.8 19.0 %collective-permute-start.24 = (s16[2064,128]{1,0:T(8,128)(2,1)}, s16[2064,128]{1,0:T(8,128)(2,1)S(1)}, u32[]{:S(2)}, u32[]{:S(2)}) collective-permute-start(s16[2064,128]{1,0:T(8,128)(2,1)} %get-tuple-element.101), channel_id=1, source_target_pairs={{0,1},{1,0},{2,3},{3,2},{4,5},{5,4},{6,7},{7,6},{8,9},{9,8},{10,11... | collective-permute-start | bytes 1585160 | tf_op jit(solution)/shard_map/ppermute | solution.py:562
  198.3 11.3 %collective-permute-start.18 = (f32[4,8,128]{2,1,0:T(8,128)S(1)}, f32[4,8,128]{2,1,0:T(8,128)S(1)}, u32[]{:S(2)}, u32[]{:S(2)}) collective-permute-start(f32[4,8,128]{2,1,0:T(8,128)S(1)} %pad_maximum_fusion.4), channel_id=1, source_target_pairs={{0,16},{16,0},{1,17},{17,1},{2,18},{18,2},{3,19},{19,3},{4,20},{20... | collective-permute-start | bytes 49160 | tf_op jit(solution)/shard_map/ppermute | solution.py:486
  206.4 15.7 %collective-permute-start.25 = (s16[2064,128]{1,0:T(8,128)(2,1)}, s16[2064,128]{1,0:T(8,128)(2,1)S(1)}, u32[]{:S(2)}, u32[]{:S(2)}) collective-permute-start(s16[2064,128]{1,0:T(8,128)(2,1)} %get-tuple-element.105), channel_id=1, source_target_pairs={{0,2},{1,3},{2,0},{3,1},{4,6},{5,7},{6,4},{7,5},{8,10},{9,11},{10,... | collective-permute-start | bytes 1585160 | tf_op jit(solution)/shard_map/ppermute | solution.py:561
  209.0 15.2 %collective-permute-start.26 = (s16[2064,128]{1,0:T(8,128)(2,1)}, s16[2064,128]{1,0:T(8,128)(2,1)S(1)}, u32[]{:S(2)}, u32[]{:S(2)}) collective-permute-start(s16[2064,128]{1,0:T(8,128)(2,1)} %get-tuple-element.106), channel_id=1, source_target_pairs={{0,1},{1,0},{2,3},{3,2},{4,5},{5,4},{6,7},{7,6},{8,9},{9,8},{10,11... | collective-permute-start | bytes 1585160 | tf_op jit(solution)/shard_map/ppermute | solution.py:562
  215.3 37.0 %collective-permute-start.39 = (bf16[64,8192]{1,0:T(8,128)(2,1)}, bf16[64,8192]{1,0:T(8,128)(2,1)S(1)}, u32[]{:S(2)}, u32[]{:S(2)}) collective-permute-start(bf16[64,8192]{1,0:T(8,128)(2,1)} %get-tuple-element.102.dep.own), channel_id=1, source_target_pairs={{0,2},{1,3},{2,0},{3,1},{4,6},{5,7},{6,4},{7,5},{8,10},{9,11},{10,... | collective-permute-start | bytes 3145736 | tf_op jit(solution)/shard_map/ppermute | solution.py:567
  215.4 29.0 %collective-permute-start.31 = (bf16[64,8192]{1,0:T(8,128)(2,1)}, bf16[64,8192]{1,0:T(8,128)(2,1)S(1)}, u32[]{:S(2)}, u32[]{:S(2)}) collective-permute-start(bf16[64,8192]{1,0:T(8,128)(2,1)} %get-tuple-element.102.dep.own), channel_id=1, source_target_pairs={{0,1},{1,0},{2,3},{3,2},{4,5},{5,4},{6,7},{7,6},{8,9},{9,8},{10,11... | collective-permute-start | bytes 3145736 | tf_op jit(solution)/shard_map/ppermute | solution.py:566
  229.5 5.6 %collective-permute-start.29 = (f32[8,128]{1,0:T(8,128)}, f32[8,128]{1,0:T(8,128)S(1)}, u32[]{:S(2)}, u32[]{:S(2)}) collective-permute-start(f32[8,128]{1,0:T(8,128)} %get-tuple-element.109), channel_id=1, source_target_pairs={{0,12},{4,8},{8,4},{12,0},{1,13},{5,9},{9,5},{13,1},{2,14},{6,10},... | collective-permute-start | bytes 12296 | tf_op jit(solution)/shard_map/ppermute | solution.py:479
  231.4 4.7 %collective-permute-start.28 = (f32[8,128]{1,0:T(8,128)}, f32[8,128]{1,0:T(8,128)S(1)}, u32[]{:S(2)}, u32[]{:S(2)}) collective-permute-start(f32[8,128]{1,0:T(8,128)} %get-tuple-element.109), channel_id=1, source_target_pairs={{0,8},{4,12},{8,0},{12,4},{1,9},{5,13},{9,1},{13,5},{2,10},{6,14},... | collective-permute-start | bytes 12296 | tf_op jit(solution)/shard_map/ppermute | solution.py:479
  232.2 3.9 %collective-permute-start.27 = (f32[8,128]{1,0:T(8,128)}, f32[8,128]{1,0:T(8,128)S(1)}, u32[]{:S(2)}, u32[]{:S(2)}) collective-permute-start(f32[8,128]{1,0:T(8,128)} %get-tuple-element.109), channel_id=1, source_target_pairs={{0,4},{4,0},{8,12},{12,8},{1,5},{5,1},{9,13},{13,9},{2,6},{6,2},{1... | collective-permute-start | bytes 12296 | tf_op jit(solution)/shard_map/ppermute | solution.py:479
  236.8 1.2 collective-permute-start.30
  250.3 63.7 %collective-permute-start.47 = (bf16[64,8192]{1,0:T(8,128)(2,1)}, bf16[64,8192]{1,0:T(8,128)(2,1)S(1)}, u32[]{:S(2)}, u32[]{:S(2)}) collective-permute-start(bf16[64,8192]{1,0:T(8,128)(2,1)} %get-tuple-element.111.dep.own), channel_id=1, source_target_pairs={{0,2},{1,3},{2,0},{3,1},{4,6},{5,7},{6,4},{7,5},{8,10},{9,11},{10,... | collective-permute-start | bytes 3145736 | tf_op jit(solution)/shard_map/ppermute | solution.py:567
  250.8 65.0 %collective-permute-start.46 = (bf16[64,8192]{1,0:T(8,128)(2,1)}, bf16[64,8192]{1,0:T(8,128)(2,1)S(1)}, u32[]{:S(2)}, u32[]{:S(2)}) collective-permute-start(bf16[64,8192]{1,0:T(8,128)(2,1)} %get-tuple-element.111.dep.own), channel_id=1, source_target_pairs={{0,1},{1,0},{2,3},{3,2},{4,5},{5,4},{6,7},{7,6},{8,9},{9,8},{10,11... | collective-permute-start | bytes 3145736 | tf_op jit(solution)/shard_map/ppermute | solution.py:566
  252.3 33.7 %copy-start.8 = (bf16[64,8192]{1,0:T(8,128)(2,1)}, bf16[64,8192]{1,0:T(8,128)(2,1)S(1)}, u32[]{:S(2)}) copy-start(bf16[64,8192]{1,0:T(8,128)(2,1)S(1)} %collective-permute-done.39.gy) | copy-start | bytes 3145732
  252.3 33.7 %collective-permute-start.41 = (bf16[64,4096]{1,0:T(8,128)(2,1)S(1)}, bf16[64,4096]{1,0:T(8,128)(2,1)S(1)}, u32[]{:S(2)}, u32[]{:S(2)}) collective-permute-start(bf16[64,4096]{1,0:T(8,128)(2,1)S(1)} %slice.167), channel_id=1, source_target_pairs={{0,1},{1,0},{2,3},{3,2},{4,5},{5,4},{6,7},{7,6},{8,9},{9,8},{10,11... | collective-permute-start | bytes 1572872 | tf_op jit(solution)/shard_map/ppermute | solution.py:570
  252.9 33.1 %collective-permute-start.40 = (bf16[64,4096]{1,0:T(8,128)(2,1)S(1)}, bf16[64,4096]{1,0:T(8,128)(2,1)S(1)}, u32[]{:S(2)}, u32[]{:S(2)}) collective-permute-start(bf16[64,4096]{1,0:T(8,128)(2,1)S(1)} %copy-done.11), channel_id=1, source_target_pairs={{0,2},{1,3},{2,0},{3,1},{4,6},{5,7},{6,4},{7,5},{8,10},{9,11},{10,... | collective-permute-start | bytes 1572872 | tf_op jit(solution)/shard_map/ppermute | solution.py:569
  287.0 16.8 %copy-start.36 = (f32[8,128]{1,0:T(8,128)S(1)}, f32[8,128]{1,0:T(8,128)}, u32[]{:S(2)}) copy-start(f32[8,128]{1,0:T(8,128)} %get-tuple-element.98) | copy-start | bytes 12292
  287.0 16.8 %copy-start.37 = (f32[8,128]{1,0:T(8,128)S(1)}, f32[8,128]{1,0:T(8,128)}, u32[]{:S(2)}) copy-start(f32[8,128]{1,0:T(8,128)} %get-tuple-element.110) | copy-start | bytes 12292
  303.9 14.9 %collective-permute-start.42 = (f32[128,2048]{1,0:T(8,128)}, f32[128,2048]{1,0:T(8,128)S(1)}, u32[]{:S(2)}, u32[]{:S(2)}) collective-permute-start(f32[128,2048]{1,0:T(8,128)} %get-tuple-element.113), channel_id=1, source_target_pairs={{0,16},{16,0},{1,17},{17,1},{2,18},{18,2},{3,19},{19,3},{4,20},{20... | collective-permute-start | bytes 3145736 | tf_op jit(solution)/shard_map/ppermute | solution.py:628
  303.9 4.6 %collective-permute-start.33 = (f32[2,8,128]{2,1,0:T(8,128)S(1)}, f32[2,8,128]{2,1,0:T(8,128)S(1)}, u32[]{:S(2)}, u32[]{:S(2)}) collective-permute-start(f32[2,8,128]{2,1,0:T(8,128)S(1)} %get-tuple-element.137), channel_id=1, source_target_pairs={{0,8},{4,12},{8,0},{12,4},{1,9},{5,13},{9,1},{13,5},{2,10},{6,14},... | collective-permute-start | bytes 24584 | tf_op jit(solution)/shard_map/ppermute | solution.py:479
  304.0 6.6 %collective-permute-start.32 = (f32[2,8,128]{2,1,0:T(8,128)S(1)}, f32[2,8,128]{2,1,0:T(8,128)S(1)}, u32[]{:S(2)}, u32[]{:S(2)}) collective-permute-start(f32[2,8,128]{2,1,0:T(8,128)S(1)} %get-tuple-element.137), channel_id=1, source_target_pairs={{0,4},{4,0},{8,12},{12,8},{1,5},{5,1},{9,13},{13,9},{2,6},{6,2},{1... | collective-permute-start | bytes 24584 | tf_op jit(solution)/shard_map/ppermute | solution.py:479
  308.5 5.4 %collective-permute-start.34 = (f32[2,8,128]{2,1,0:T(8,128)S(1)}, f32[2,8,128]{2,1,0:T(8,128)S(1)}, u32[]{:S(2)}, u32[]{:S(2)}) collective-permute-start(f32[2,8,128]{2,1,0:T(8,128)S(1)} %get-tuple-element.137), channel_id=1, source_target_pairs={{0,12},{4,8},{8,4},{12,0},{1,13},{5,9},{9,5},{13,1},{2,14},{6,10},... | collective-permute-start | bytes 24584 | tf_op jit(solution)/shard_map/ppermute | solution.py:479
  314.0 2.9 collective-permute-start.35
  314.0 14.4 %collective-permute-start.49 = (bf16[64,4096]{1,0:T(8,128)(2,1)S(1)}, bf16[64,4096]{1,0:T(8,128)(2,1)S(1)}, u32[]{:S(2)}, u32[]{:S(2)}) collective-permute-start(bf16[64,4096]{1,0:T(8,128)(2,1)S(1)} %slice.169), channel_id=1, source_target_pairs={{0,1},{1,0},{2,3},{3,2},{4,5},{5,4},{6,7},{7,6},{8,9},{9,8},{10,11... | collective-permute-start | bytes 1572872 | tf_op jit(solution)/shard_map/ppermute | solution.py:570
  315.8 14.2 %collective-permute-start.48 = (bf16[64,4096]{1,0:T(8,128)(2,1)S(1)}, bf16[64,4096]{1,0:T(8,128)(2,1)S(1)}, u32[]{:S(2)}, u32[]{:S(2)}) collective-permute-start(bf16[64,4096]{1,0:T(8,128)(2,1)S(1)} %slice.168), channel_id=1, source_target_pairs={{0,2},{1,3},{2,0},{3,1},{4,6},{5,7},{6,4},{7,5},{8,10},{9,11},{10,... | collective-permute-start | bytes 1572872 | tf_op jit(solution)/shard_map/ppermute | solution.py:569
  316.9 32.5 %collective-permute-start.37 = (f32[3,64]{1,0:T(4,128)S(1)}, f32[3,64]{1,0:T(4,128)S(1)}, u32[]{:S(2)}, u32[]{:S(2)}) collective-permute-start(f32[3,64]{1,0:T(4,128)S(1)} %pad_maximum_fusion.7), channel_id=1, source_target_pairs={{0,2},{1,3},{2,0},{3,1},{4,6},{5,7},{6,4},{7,5},{8,10},{9,11},{10,... | collective-permute-start | bytes 2312 | tf_op jit(solution)/shard_map/ppermute | solution.py:612
  318.0 31.5 %collective-permute-start.38 = (f32[3,64]{1,0:T(4,128)S(1)}, f32[3,64]{1,0:T(4,128)S(1)}, u32[]{:S(2)}, u32[]{:S(2)}) collective-permute-start(f32[3,64]{1,0:T(4,128)S(1)} %pad_maximum_fusion.7), channel_id=1, source_target_pairs={{0,3},{1,2},{2,1},{3,0},{4,7},{5,6},{6,5},{7,4},{8,11},{9,10},{10,... | collective-permute-start | bytes 2312 | tf_op jit(solution)/shard_map/ppermute | solution.py:612
  318.8 30.7 %collective-permute-start.36 = (f32[3,64]{1,0:T(4,128)S(1)}, f32[3,64]{1,0:T(4,128)S(1)}, u32[]{:S(2)}, u32[]{:S(2)}) collective-permute-start(f32[3,64]{1,0:T(4,128)S(1)} %pad_maximum_fusion.7), channel_id=1, source_target_pairs={{0,1},{1,0},{2,3},{3,2},{4,5},{5,4},{6,7},{7,6},{8,9},{9,8},{10,11... | collective-permute-start | bytes 2312 | tf_op jit(solution)/shard_map/ppermute | solution.py:612
  330.8 20.2 %copy-start.42 = (s16[32,2176]{1,0:T(8,128)(2,1)S(1)}, s16[32,2176]{1,0:T(8,128)(2,1)}, u32[]{:S(2)}) copy-start(s16[32,2176]{1,0:T(8,128)(2,1)} %get-tuple-element.115) | copy-start | bytes 417796
  330.8 20.9 %copy-start.41 = (s16[32,2176]{1,0:T(8,128)(2,1)S(1)}, s16[32,2176]{1,0:T(8,128)(2,1)}, u32[]{:S(2)}) copy-start(s16[32,2176]{1,0:T(8,128)(2,1)} %get-tuple-element.116) | copy-start | bytes 417796
  330.8 23.5 %copy-start.40 = (s16[32,2176]{1,0:T(8,128)(2,1)S(1)}, s16[32,2176]{1,0:T(8,128)(2,1)}, u32[]{:S(2)}) copy-start(s16[32,2176]{1,0:T(8,128)(2,1)} %get-tuple-element.117) | copy-start | bytes 417796
  347.8 8.3 %collective-permute-start.50 = (f32[128,2048]{1,0:T(8,128)}, f32[128,2048]{1,0:T(8,128)S(1)}, u32[]{:S(2)}, u32[]{:S(2)}) collective-permute-start(f32[128,2048]{1,0:T(8,128)} %get-tuple-element.119), channel_id=1, source_target_pairs={{0,16},{16,0},{1,17},{17,1},{2,18},{18,2},{3,19},{19,3},{4,20},{20... | collective-permute-start | bytes 3145736 | tf_op jit(solution)/shard_map/ppermute | solution.py:628
  351.1 11.2 %collective-permute-start.43 = (s16[32,2176]{1,0:T(8,128)(2,1)S(1)}, s16[32,2176]{1,0:T(8,128)(2,1)S(1)}, u32[]{:S(2)}, u32[]{:S(2)}) collective-permute-start(s16[32,2176]{1,0:T(8,128)(2,1)S(1)} %copy-done.42), channel_id=1, source_target_pairs={{0,4},{4,0},{8,12},{12,8},{1,5},{5,1},{9,13},{13,9},{2,6},{6,2},{1... | collective-permute-start | bytes 417800 | tf_op jit(solution)/shard_map/ppermute | solution.py:632
  351.8 13.4 %collective-permute-start.44 = (s16[32,2176]{1,0:T(8,128)(2,1)S(1)}, s16[32,2176]{1,0:T(8,128)(2,1)S(1)}, u32[]{:S(2)}, u32[]{:S(2)}) collective-permute-start(s16[32,2176]{1,0:T(8,128)(2,1)S(1)} %copy-done.41), channel_id=1, source_target_pairs={{0,8},{4,12},{8,0},{12,4},{1,9},{5,13},{9,1},{13,5},{2,10},{6,14},... | collective-permute-start | bytes 417800 | tf_op jit(solution)/shard_map/ppermute | solution.py:632
  354.3 10.9 %collective-permute-start.45 = (s16[32,2176]{1,0:T(8,128)(2,1)S(1)}, s16[32,2176]{1,0:T(8,128)(2,1)S(1)}, u32[]{:S(2)}, u32[]{:S(2)}) collective-permute-start(s16[32,2176]{1,0:T(8,128)(2,1)S(1)} %copy-done.40), channel_id=1, source_target_pairs={{0,12},{4,8},{8,4},{12,0},{1,13},{5,9},{9,5},{13,1},{2,14},{6,10},... | collective-permute-start | bytes 417800 | tf_op jit(solution)/shard_map/ppermute | solution.py:632
  359.7 8.9 %collective-permute-start.51 = (s16[32,2176]{1,0:T(8,128)(2,1)}, s16[32,2176]{1,0:T(8,128)(2,1)S(1)}, u32[]{:S(2)}, u32[]{:S(2)}) collective-permute-start(s16[32,2176]{1,0:T(8,128)(2,1)} %get-tuple-element.121), channel_id=1, source_target_pairs={{0,4},{4,0},{8,12},{12,8},{1,5},{5,1},{9,13},{13,9},{2,6},{6,2},{1... | collective-permute-start | bytes 417800 | tf_op jit(solution)/shard_map/ppermute | solution.py:632
  359.7 17.4 %collective-permute-start.52 = (s16[32,2176]{1,0:T(8,128)(2,1)}, s16[32,2176]{1,0:T(8,128)(2,1)S(1)}, u32[]{:S(2)}, u32[]{:S(2)}) collective-permute-start(s16[32,2176]{1,0:T(8,128)(2,1)} %get-tuple-element.122), channel_id=1, source_target_pairs={{0,8},{4,12},{8,0},{12,4},{1,9},{5,13},{9,1},{13,5},{2,10},{6,14},... | collective-permute-start | bytes 417800 | tf_op jit(solution)/shard_map/ppermute | solution.py:632
  362.3 14.9 %collective-permute-start.53 = (s16[32,2176]{1,0:T(8,128)(2,1)}, s16[32,2176]{1,0:T(8,128)(2,1)S(1)}, u32[]{:S(2)}, u32[]{:S(2)}) collective-permute-start(s16[32,2176]{1,0:T(8,128)(2,1)} %get-tuple-element.123), channel_id=1, source_target_pairs={{0,12},{4,8},{8,4},{12,0},{1,13},{5,9},{9,5},{13,1},{2,14},{6,10},... | collective-permute-start | bytes 417800 | tf_op jit(solution)/shard_map/ppermute | solution.py:632
  (36 other events, 139.8 us)
Sparse Core Ops, SparseCore 0:
  22.0 29.2 all-gather.3
  52.9 21.8 all-gather.5
  89.5 28.2 all-gather.7

commit v3 on v2

--- a/solution.py
+++ b/solution.py
@@ -201,6 +201,12 @@
     )(*operands, dep)
 
 
+def inverse_norms(pieces_ref, k):
+    x = pieces_ref[...].astype(f32)
+    x = jnp.transpose(jnp.concatenate([x, x], axis=0))
+    return (x[k : k + 1] + x[k + 4 : k + 5]) + x[k + 8 : k + 9]
+
+
 def merged(op, x):
     return op(x, swap_lanes(x))
 
@@ -227,10 +233,10 @@
     return jnp.where(low_lanes(shape), row, row + packed)
 
 
-def student_kernel(op, oq, lp, lq, inv_ref, target_ref, base_ref, dep, out_ref, stats_ref):
+def student_kernel(k, op, oq, lp, lq, inv_ref, target_ref, base_ref, dep, out_ref, stats_ref):
     packed = op.shape[0]
     step = min(512, packed)
-    top = summed((op, oq), (lp, lq), inv_ref[...], out_ref)
+    top = summed((op, oq), (lp, lq), inverse_norms(inv_ref, k), out_ref)
     soft = jnp.zeros((1, LANES), f32)
     plain = jnp.zeros((1, LANES), f32)
     hit = jnp.zeros((1, LANES), f32)
@@ -249,10 +255,10 @@
     stats_ref[...] = stats
 
 
-def teacher_kernel(op, oq, lp, lq, inv_ref, student_ref, before_ref, dep, out_ref, stats_ref):
+def teacher_kernel(k, op, oq, lp, lq, inv_ref, student_ref, before_ref, dep, out_ref, stats_ref):
     packed = op.shape[0]
     step = min(512, packed)
-    top = summed((op, oq), (lp, lq), inv_ref[...], out_ref)
+    top = summed((op, oq), (lp, lq), inverse_norms(inv_ref, k), out_ref)
     top = top * (1.0 / heat)
     total = jnp.zeros((1, LANES), f32)
     cross = jnp.zeros((1, LANES), f32)
@@ -270,11 +276,11 @@
     stats_ref[...] = stats
 
 
-def finish(body, owns, lasts, inv, extra, dep):
+def finish(body, k, owns, lasts, inv, extra, dep):
     packed = owns[0].shape[0]
     last_spec = SMEM if body is student_kernel else VMEM
     return pl.pallas_call(
-        body,
+        functools.partial(body, k),
         in_specs=[VMEM] * 6 + [last_spec, ANY],
         out_specs=[VMEM] * 2,
         out_shape=[
@@ -293,8 +299,14 @@
     return parts[0]
 
 
+def thirds(x):
+    high = x.astype(jnp.bfloat16).astype(f32)
+    mid = (x - high).astype(jnp.bfloat16).astype(f32)
+    return [high, mid, x - high - mid]
+
+
 def slope_kernel(
-    student_ref, teacher_ref, stats_ref, target_ref, base_ref, dep, grad_ref, loss_ref
+    student_ref, teacher_ref, stats_ref, target_ref, base_ref, dep, grad_ref
 ):
     packed = student_ref.shape[0] // 2
     step = min(512, packed)
@@ -339,129 +351,162 @@
         at = 2 * (n * step // packed) * packed + (n * step) % packed
         grad_ref[:, at : at + step] = g[:QUARTER]
         grad_ref[:, at + packed : at + packed + step] = g[QUARTER:]
-    rows_out = jnp.where(row_is((8, LANES), 0), row_loss, 0.0)
-    loss_ref[...] = jnp.where(row_is((8, LANES), 1), merged(jnp.add, inner), rows_out)
+    extra = jnp.zeros((LANES, LANES), f32)
+    for n, value in enumerate(thirds(merged(jnp.add, inner)) + thirds(row_loss)):
+        extra = jnp.where(row_is(extra.shape, n), value, extra)
+    extra = jnp.transpose(extra).astype(jnp.bfloat16)
+    grad_ref[:, 2 * 2 * packed :] = extra[:QUARTER]
 
 
 def slope(base, student, teacher, stats, targets, dep):
     return pl.pallas_call(
         slope_kernel,
         in_specs=[VMEM] * 4 + [SMEM, ANY],
-        out_specs=[VMEM] * 2,
-        out_shape=[
-            jax.ShapeDtypeStruct((QUARTER, 2 * student.shape[0]), jnp.bfloat16),
-            jax.ShapeDtypeStruct((8, LANES), f32),
-        ],
+        out_specs=VMEM,
+        out_shape=jax.ShapeDtypeStruct((QUARTER, 2 * student.shape[0] + LANES), jnp.bfloat16),
         compiler_params=PARAMS,
         cost_estimate=LIGHT,
         name="slope",
     )(student, teacher, stats, targets, base, dep)
 
 
-def norm_grad_kernel(t_ref, flip_ref, own, gx, gy, dp, dq, h_ref, dep, keep_ref, send_ref, lhs):
+def norm_grad_kernel(t_ref, flip_ref, own, gx, gy, dp, dq, h_ref, dep, keep, send, loss, lhs):
+    vocab, tile = h_ref.shape
     half = dp.shape[1]
-
-    @pl.when(pl.program_id(0) == 0)
+    j = pl.program_id(0)
+    t = jnp.bitwise_xor(t_ref[0], 2 * flip_ref[0])
+
+    def place(n, columns, value):
+        quarter = jnp.bitwise_xor(t, n)
+        at = pl.ds(pl.multiple_of(lax.rem(quarter, 2) * QUARTER, QUARTER), QUARTER)
+
+        @pl.when(quarter < 2)
+        def _():
+            keep[at, columns] = value
+
+        @pl.when(quarter >= 2)
+        def _():
+            send[at, columns] = value
+
+    @pl.when(j == 0)
     def _():
         for n, ref in enumerate((own, gx, gy)):
-            lhs[n * QUARTER : (n + 1) * QUARTER, :] = ref[...]
+            lhs[n * QUARTER : (n + 1) * QUARTER, :] = ref[:, :vocab]
         lhs[3 * QUARTER :, :half] = dp[...]
-        lhs[3 * QUARTER :, half:] = dq[...]
+        lhs[3 * QUARTER :, half:] = dq[:, : vocab - half]
+        losses = []
+        for n, ref in enumerate((own, gx, gy, dq)):
+            x = ref[:, ref.shape[1] - LANES :].astype(f32)
+            lane = lax.broadcasted_iota(jnp.int32, x.shape, 1)
+            inner = jnp.sum(jnp.where(lane < 3, x, 0.0), axis=1, keepdims=True)
+            place(n, slice(keep.shape[1] - LANES, keep.shape[1]), jnp.broadcast_to(inner, x.shape))
+            x = jnp.where((lane >= 3) & (lane < 6), x, 0.0)
+            losses.append(jnp.sum(jnp.sum(x, axis=1, keepdims=True), axis=0, keepdims=True))
+        loss[...] = jnp.broadcast_to(tree_sum(losses), loss.shape)
 
     r = jnp.dot(lhs[...], h_ref[...], preferred_element_type=f32)
-    t = jnp.bitwise_xor(t_ref[0], 2 * flip_ref[0])
+    columns = pl.ds(pl.multiple_of(j * tile, tile), tile)
     for n in range(4):
-        quarter = jnp.bitwise_xor(t, n)
-        at = pl.ds(pl.multiple_of(lax.rem(quarter, 2) * QUARTER, QUARTER), QUARTER)
-
-        @pl.when(quarter < 2)
-        def _():
-            keep_ref[at, :] = r[n * QUARTER : (n + 1) * QUARTER]
-
-        @pl.when(quarter >= 2)
-        def _():
-            send_ref[at, :] = r[n * QUARTER : (n + 1) * QUARTER]
+        place(n, columns, r[n * QUARTER : (n + 1) * QUARTER])
 
 
 def norm_gradient(t, flip, own, gx, gy, dp, dq, head, dep):
     vocab, width = head.shape
     tile = min(512, width)
-    full = pl.BlockSpec((QUARTER, vocab), lambda j: (0, 0))
-    part = pl.BlockSpec((QUARTER, vocab // 2), lambda j: (0, 0))
+    parts = (own, gx, gy, dp, dq)
+    rows = jax.ShapeDtypeStruct((2 * QUARTER, width + LANES), f32)
     return pl.pallas_call(
         norm_grad_kernel,
         grid=(width // tile,),
-        in_specs=[SMEM, SMEM, full, full, full, part, part]
+        in_specs=[SMEM, SMEM]
+        + [pl.BlockSpec(x.shape, lambda j: (0, 0)) for x in parts]
         + [pl.BlockSpec((vocab, tile), lambda j: (0, j)), ANY],
-        out_specs=[pl.BlockSpec((2 * QUARTER, tile), lambda j: (0, j))] * 2,
-        out_shape=[jax.ShapeDtypeStruct((2 * QUARTER, width), f32)] * 2,
+        out_specs=[pl.BlockSpec(rows.shape, lambda j: (0, 0))] * 2
+        + [pl.BlockSpec((8, LANES), lambda j: (0, 0))],
+        out_shape=[rows, rows, jax.ShapeDtypeStruct((8, LANES), f32)],
         scratch_shapes=[pltpu.VMEM((4 * QUARTER, vocab), jnp.bfloat16)],
         compiler_params=PARAMS,
         cost_estimate=LIGHT,
         name="norm_grad",
-    )(t, flip, own, gx, gy, dp, dq, head, dep)
-
-
-def row_encode(x):
-    top = jnp.max(jnp.abs(x), axis=1, keepdims=True)
+    )(t, flip, *parts, head, dep)
+
+
+def exponent(top):
     e = jnp.ceil(jnp.log2(jnp.maximum(top, 2.0**-44))).astype(jnp.int32)
-    e = jnp.clip(e, -44, 44)
-    q = jnp.clip(jnp.round(x * pow2(15 - e)), -32767.0, 32767.0)
-    return q.astype(jnp.int32).astype(jnp.int16), e
-
-
-def fold_kernel(z_ref, mine_ref, other_ref, own_ref, *sends):
-    rows, width = own_ref.shape
+    return jnp.clip(e, -44, 44)
+
+
+def fold_kernel(z_ref, mine_ref, other_ref, dep_p, dep_q, own_ref, *sends):
+    rows, width = own_ref.shape[0], own_ref.shape[1] - LANES
     for k in range(4):
         at = pl.ds(pl.multiple_of(jnp.bitwise_xor(z_ref[0], k) * rows, rows), rows)
         x = mine_ref[at, :] + other_ref[at, :]
         if k == 0:
             own_ref[...] = x
-        else:
-            q, e = row_encode(x)
-            sends[k - 1][:, :width] = q
-            sends[k - 1][:, width:] = jnp.broadcast_to(e, (rows, LANES)).astype(jnp.int16)
-
-
-def fold(z, mine, other):
+            continue
+        norm, inner = x[:, :width], x[:, width:]
+        e = exponent(jnp.max(jnp.abs(norm), axis=1, keepdims=True))
+        q = jnp.clip(jnp.round(norm * pow2(15 - e)), -32767.0, 32767.0)
+        sends[k - 1][:, :width] = q.astype(jnp.int32).astype(jnp.int16)
+        e_inner = exponent(jnp.abs(inner))
+        inner = jnp.clip(inner * pow2(15 - e_inner), -32767.0, 32767.0)
+        high = jnp.round(inner)
+        low = jnp.round((inner - high) * 32768.0)
+        lane = lax.broadcasted_iota(jnp.int32, inner.shape, 1)
+        tail = jnp.where(lane == 0, jnp.broadcast_to(e, inner.shape), e_inner)
+        tail = jnp.where(lane == 2, high.astype(jnp.int32), tail)
+        tail = jnp.where(lane == 3, low.astype(jnp.int32), tail)
+        sends[k - 1][:, width:] = tail.astype(jnp.int16)
+
+
+def fold(z, mine, other, deps):
     rows, width = other.shape
     return pl.pallas_call(
         fold_kernel,
-        grid=(1,),
-        in_specs=[
-            SMEM,
-            pl.BlockSpec((rows, width), lambda j: (0, 0)),
-            pl.BlockSpec((rows, width), lambda j: (0, 0)),
-        ],
+        in_specs=[SMEM, VMEM, VMEM, ANY, ANY],
         out_specs=[VMEM] * 4,
         out_shape=[jax.ShapeDtypeStruct((rows // 4, width), f32)]
-        + [jax.ShapeDtypeStruct((rows // 4, width + LANES), jnp.int16)] * 3,
+        + [jax.ShapeDtypeStruct((rows // 4, width), jnp.int16)] * 3,
         compiler_params=PARAMS,
         cost_estimate=LIGHT,
         name="fold",
-    )(z, mine, other)
-
-
-def last_kernel(own_ref, p1, p2, p3, hidden_ref, gain_ref, inv_ref, inner_ref, out_ref):
-    width = own_ref.shape[1]
-    norm = own_ref[...]
+    )(z, mine, other, *deps)
+
+
+def last_kernel(features, own_ref, p1, p2, p3, hidden_ref, gain_ref, inv_ref, before, out_ref):
+    width = hidden_ref.shape[1]
+    norm, inner = own_ref[:, :width], own_ref[:, width : width + 1]
     for p in (p1, p2, p3):
-        e = p[:, width:].astype(jnp.int32)[:, :1]
-        norm = norm + p[:, :width].astype(jnp.int32).astype(f32) * pow2(e - 15)
-    out = inv_ref[...] * gain_ref[...] * norm - hidden_ref[...].astype(f32) * inner_ref[...]
+        tail = p[:, width:].astype(jnp.int32)
+        norm = norm + p[:, :width].astype(jnp.int32).astype(f32) * pow2(tail[:, 0:1] - 15)
+        value = tail[:, 2:3].astype(f32) + tail[:, 3:4].astype(f32) * (1.0 / 32768.0)
+        inner = inner + value * pow2(tail[:, 1:2] - 15)
+    inv = inv_ref[:, :1]
+    scale = inv * inv * inner * (1.0 / features)
+    out = inv * gain_ref[...] * norm - hidden_ref[...].astype(f32) * scale
     out_ref[...] = out.astype(jnp.bfloat16)
 
 
-def last(own, gots, hidden, gain, inv, inner):
+def last(features, own, gots, hidden, gain, inv, part, before):
+    count, width = own.shape[0], hidden.shape[1]
+    block = pl.BlockSpec((count, width), lambda j: (part, 0))
+    given = before is not None
     return pl.pallas_call(
-        last_kernel,
-        in_specs=[VMEM] * 8,
-        out_specs=VMEM,
-        out_shape=jax.ShapeDtypeStruct(own.shape, jnp.bfloat16),
+        functools.partial(last_kernel, features),
+        grid=(1,),
+        in_specs=[VMEM] * 4
+        + [block, VMEM, pl.BlockSpec((count, LANES), lambda j: (part, 0)), ANY],
+        out_specs=block,
+        out_shape=jax.ShapeDtypeStruct(hidden.shape, jnp.bfloat16),
+        input_output_aliases={7: 0} if given else {},
         compiler_params=PARAMS,
         cost_estimate=LIGHT,
         name="hidden_grad",
-    )(own, *gots, hidden, gain.reshape(1, -1), inv[:, None], inner[:, None])
+    )(own, *gots, hidden, gain.reshape(1, -1), inv, before if given else inv)
+
+
+def tie(x, *others):
+    return lax.optimization_barrier((x, *others))[0]
 
 
 def tok_sum(x):
@@ -568,79 +613,73 @@
         corner = (gx[:, :half], gy[:, half:])
         dp = lax.ppermute(corner[0], "tok", TOK_Y)
         dq = lax.ppermute(corner[1], "tok", TOK_X)
-        return (grad, gx, gy, dp, dq), corner[0]
+        return (grad, gx, gy, dp, dq), corner
 
     row_targets = [mine(targets[:, rows].reshape(-1)) for rows in halves]
 
     student, teacher = (student_gain, student_head), (teacher_gain, teacher_head)
-    gots_sa, keeps_sa, dep = start(student_a, *student, base)
+    gots_sa, keeps_sa, dep = start(student_a, *student, tie(base, *row_targets))
     student_b = gather_rows(student_b_own, dep)
     gots_ta, keeps_ta, dep = start(teacher_a, *teacher, dep)
     own_sa, last_sa, dep = onward(gots_sa, keeps_sa, student_head, dep)
     teacher_b = gather_rows(teacher_hidden[halves[1]], dep)
     gots_sb, keeps_sb, dep = start(student_b, *student, dep)
-    pieces = student_b[:, student_hidden.shape[1] :].astype(f32)
-    pieces = (pieces[:, 0:4] + pieces[:, 4:8]) + pieces[:, 8:12]
-    inv_s, inv_t = [mine(pieces[:, k]) for k in (0, 1)], [mine(pieces[:, k]) for k in (2, 3)]
+    pieces = student_b[:, student_hidden.shape[1] :]
+    pieces = lax.dynamic_slice_in_dim(pieces, t * QUARTER, QUARTER)
+    own_ta, last_ta, dep = onward(gots_ta, keeps_ta, teacher_head, tie(dep, pieces))
+    gots_tb, keeps_tb, dep = start(teacher_b, *teacher, dep)
     logits_sa, stats = finish(
-        student_kernel, own_sa, last_sa, inv_s[0], (row_targets[0], base), dep
-    )
-    own_ta, last_ta, dep = onward(gots_ta, keeps_ta, teacher_head, stats)
-    gots_tb, keeps_tb, dep = start(teacher_b, *teacher, dep)
+        student_kernel, 0, own_sa, last_sa, pieces, (row_targets[0], base), dep
+    )
+    own_sb, last_sb, dep = onward(gots_sb, keeps_sb, student_head, stats)
     logits_ta, stats_a = finish(
-        teacher_kernel, own_ta, last_ta, inv_t[0], (logits_sa, stats), dep
-    )
-    own_sb, last_sb, dep = onward(gots_sb, keeps_sb, student_head, stats_a)
+        teacher_kernel, 2, own_ta, last_ta, pieces, (logits_sa, stats), dep
+    )
     all_a = range_gather(stats_a, False)
-    own_tb, last_tb, dep = onward(gots_tb, keeps_tb, teacher_head, dep)
-    grad_a, loss_a = slope(base, logits_sa, logits_ta, all_a, row_targets[0], dep)
+    own_tb, last_tb, dep = onward(gots_tb, keeps_tb, teacher_head, stats_a)
+    grad_a = slope(base, logits_sa, logits_ta, all_a, row_targets[0], dep)
     grads_a, corner = share(grad_a)
     logits_sb, stats = finish(
-        student_kernel, own_sb, last_sb, inv_s[1], (row_targets[1], base), grad_a
+        student_kernel, 1, own_sb, last_sb, pieces, (row_targets[1], base), grad_a
     )
     logits_tb, stats_b = finish(
-        teacher_kernel, own_tb, last_tb, inv_t[1], (logits_sb, stats), stats
+        teacher_kernel, 3, own_tb, last_tb, pieces, (logits_sb, stats), stats
     )
     all_b = range_gather(stats_b, False)
-    grad_b, loss_b = slope(base, logits_sb, logits_tb, all_b, row_targets[1], corner)
-    grads_b, _ = share(grad_b)
-
-    infos = range_gather(jnp.stack([loss_a, loss_b]), False)
-    inner = tree_sum([infos[k, :, 1, :QUARTER] for k in range(blocks)])
-    losses = loss_a[0, :QUARTER] + loss_b[0, :QUARTER]
-    shared = jnp.concatenate([inner, losses[None]])
-    sets = [shared] + [lax.ppermute(shared, "tok", way) for way in (TOK_X, TOK_Y, TOK_D)]
-    loss = jnp.sum(((sets[0] + sets[1]) + (sets[2] + sets[3]))[2]) / all_rows
-    me = lax.axis_index(("grp", "vocab"))
-    holder = me * part_rows // QUARTER
-    inner = lax.dynamic_index_in_dim(jnp.stack(sets), jnp.bitwise_xor(t, holder), 0, False)
-    inner = lax.dynamic_slice_in_dim(inner[:2], me * part_rows % QUARTER, part_rows, 1)
-    own_inv = inverse[0]
-    scale = [own_inv[rows] ** 2 * inner[n] / student_width for n, rows in enumerate(halves)]
-
+    dep = tie(stats_b, *corner)
+    grad_b = slope(base, logits_sb, logits_tb, all_b, row_targets[1], dep)
+    grads_b, corner = share(grad_b)
+
+    own_inv = jnp.broadcast_to(inverse[0][:, None], (own_rows, LANES))
     flip = lax.axis_index("grp").astype(jnp.int32).reshape(1) * int(small_box())
 
-    def result(grads, part, dep):
-        rows = halves[part]
-        hidden, inv = student_hidden[rows], own_inv[rows]
-        mine, other = norm_gradient(t_arr, flip, *grads, student_head, dep)
+    def result(grads, part, dep, fold_deps, before):
+        mine, other, loss = norm_gradient(t_arr, flip, *grads, student_head, dep)
         if small_box():
             other = lax.ppermute(other, "grp", SWAP)
             z = lax.axis_index("vocab").astype(jnp.int32).reshape(1)
-            own, *sends = fold(z, mine, other)
+            own, *sends = fold(z, mine, other, fold_deps)
             gots = [
                 lax.ppermute(x, "vocab", [(i, i ^ k) for i in range(4)])
                 for k, x in enumerate(sends, 1)
             ]
-            return last(own, gots, hidden, student_gain, inv, scale[part]), own
+            out = last(
+                student_width, own, gots, student_hidden, student_gain, own_inv, part, before
+            )
+            return out, loss, out
         norm = jnp.concatenate([mine, other])
         norm = lax.psum_scatter(norm, ("grp", "vocab"), scatter_dimension=0, tiled=True)
-        out = inv[:, None] * student_gain * norm - hidden.astype(f32) * scale[part][:, None]
-        return out.astype(jnp.bfloat16), mine
-
-    out_a, dep = result(grads_a, 0, grad_b)
-    out_b, _ = result(grads_b, 1, dep)
-    return (loss, jnp.concatenate([out_a, out_b]))
+        at, width = halves[part], student_hidden.shape[1]
+        inv, inner = own_inv[at, :1], norm[:, width : width + 1]
+        out = inv * student_gain * norm[:, :width]
+        out = out - student_hidden[at].astype(f32) * (inv * inv * inner / student_width)
+        return out.astype(jnp.bfloat16), loss, mine
+
+    dep = tie(grad_b, own_inv)
+    out, loss_a, dep = result(grads_a, 0, dep, corner, None)
+    second, loss_b, _ = result(grads_b, 1, dep, (t_arr, t_arr), out)
+    loss = (loss_a[0, 0] + loss_b[0, 0]) / all_rows
+    return (loss, second if small_box() else jnp.concatenate([out, second]))
 
 
 def solution(mesh):

time: 396 us -> 349 us (0.88)
  waiting for transfers between devices: 85.7 us -> 49.9 us
  starting transfers between devices: 61.9 us -> 53.4 us
  other arithmetic: 10.2 us -> 3.94 us
    ppermute x2, waiting for transfers between devices: 37 us -> 0.01 us  [share(): dq = lax.ppermute(corner[1], 'tok', TOK_X)]
    ppermute x2, waiting for transfers between devices: 0.01 us -> 10.2 us  [share(): gy = lax.ppermute(grad, 'tok', TOK_Y)]
    ppermute x4, waiting for transfers between devices: 11.4 us -> 3.22 us  [onward(): last_p = lax.ppermute(next_p, 'tok', TOK_Y)]
    ppermute x6, waiting for transfers between devices: 9.1 us -> 15.9 us  [result(): lax.ppermute(x, 'vocab', [(i, i ^ k) for i in range(4)])]
    ppermute x2, waiting for transfers between devices: 6.32 us -> 0.01 us  [share(): gx = lax.ppermute(grad, 'tok', TOK_X)]
    ppermute x12 -> x9, waiting for transfers between devices: 12.8 us -> 6.9 us  [along_z(): lax.ppermute(x, 'vocab', [(i, i ^ k) for i in range(4)])]
    ppermute x12 -> x9, starting transfers between devices: 19.2 us -> 14.5 us  [along_z(): lax.ppermute(x, 'vocab', [(i, i ^ k) for i in range(4)])]
    ppermute x2, waiting for transfers between devices: 1.56 us -> 5.83 us  [share(): dp = lax.ppermute(corner[0], 'tok', TOK_Y)]
  transfers between devices with their start and end apart: 57 -> 50, of which waited for: 18 -> 16; matrix products, arithmetic and copies ran while one was open for 5% -> 4% of each run, Pallas kernels for 49% -> 50%
where the time goes in v3:
time: 349 us; the launch traced here: 342 us
  Pallas kernels  194 us (56%)
  starting transfers between devices  53.4 us (15%)
  waiting for transfers between devices  49.9 us (14%)
  local copies, waits for them, and re-layouts  24.7 us (7%)
  between operations  16.8 us (5%)
  other arithmetic  3.94 us (1%)
    pallas_call x4, Pallas kernels, partial_logits(): pl.pallas_call(functools.partial(logits_kernel, parts, tiles, tile), grid...  95.7 us
    pallas_call x2, Pallas kernels, norm_gradient(): pl.pallas_call(norm_grad_kernel, grid=(width // tile,), in_specs=[SMEM, S...  34.9 us
    pallas_call x4, Pallas kernels, relay(): pl.pallas_call(functools.partial(relay_kernel, step, tile), grid=(steps,)...  24.8 us
    pallas_call x4, Pallas kernels, finish(): pl.pallas_call(functools.partial(body, k), in_specs=[VMEM] * 6 + [last_sp...  18 us
    ppermute x6, waiting for transfers between devices, result(): lax.ppermute(x, 'vocab', [(i, i ^ k) for i in range(4)])  15.9 us
    unnamed x88, local copies, waits for them, and re-layouts  15 us
    ppermute x9, starting transfers between devices, along_z(): lax.ppermute(x, 'vocab', [(i, i ^ k) for i in range(4)])  14.5 us
    pallas_call x2, Pallas kernels, slope(): pl.pallas_call(slope_kernel, in_specs=[VMEM] * 4 + [SMEM, ANY], out_specs...  10.5 us
  transfers between devices with their start and end apart: 50, of which 16 were waited for; matrix products, arithmetic and copies ran while one was open for 4% of the time, Pallas kernels for 50%

profile of v3, /device:TPU:0, one launch (start us, length us, event | category | flops | bytes accessed | tf_op | source)
XLA Modules:
  0.0 342.3 jit_solution(9643947464641733819)
XLA Ops:
  7.2 1.1 fusion.9
  8.3 3.1 collective-permute-start
  11.4 2.6 collective-permute-start.1
  15.8 1.9 fusion.8
  18.8 2.7 collective-permute-start.10
  22.4 2.0 collective-permute-done.1
  26.7 1.6 gather_fusion
  28.3 17.7 %logits.4 = (f32[4096,128]{1,0:T(8,128)}, s16[4112,128]{1,0:T(8,128)(2,1)}, f32[4096,128]{1,0:T(8,128)}, s16[4112,128]{1,0:T(8,128)(2,1)}) custom-call(s32[1]{0:T(128)} %bitcast.t_ref.dep_p.dep_q, bf16[256,2048]{1,0:T(8,128)(2,1)} %bitcast.50, f32[1,2048]{1,0:T(1,128)} %bitcast.54, bf16[8192,2048]{1,0:T(8,128)(2,1)} %h_ref.11, s32[1]{0:T(128)} %bitcast.9.dep_ref.base_ref), custom_call_target="tpu_custom_call" | custom-call | flops 1024 | bytes 1024 | tf_op jit(solution)/shard_map/logits/pallas_call | solution.py:129
  46.3 1.6 collective-permute-start.4
  47.8 1.2 collective-permute-start.5
  49.0 30.2 %logits.5 = (f32[4096,128]{1,0:T(8,128)}, s16[4112,128]{1,0:T(8,128)(2,1)}, f32[4096,128]{1,0:T(8,128)}, s16[4112,128]{1,0:T(8,128)(2,1)}) custom-call(s32[1]{0:T(128)} %bitcast.t_ref.dep_p.dep_q, bf16[256,4096]{1,0:T(8,128)(2,1)} %all-gather.4.cloned.1.call-done.rows_ref, f32[1,4096]{1,0:T(1,128)} %bitcast.58, bf16[8192,4096]{1,0:T(8,128)(2,1)} %h_ref.9, ...), custom_call_target="tpu_custom_call" | custom-call | flops 1024 | bytes 1024 | tf_op jit(solution)/shard_map/logits/pallas_call | solution.py:129
  80.5 6.1 %relay.4 = (s16[2064,128]{1,0:T(8,128)(2,1)}, f32[2048,128]{1,0:T(8,128)}, s16[2064,128]{1,0:T(8,128)(2,1)}, f32[2048,128]{1,0:T(8,128)}) custom-call(s16[4112,128]{1,0:T(8,128)(2,1)} %copy-done.5, s16[4112,128]{1,0:T(8,128)(2,1)} %copy-done.5, s16[4112,128]{1,0:T(8,128)(2,1)} %copy-done.5, f32[4096,128]{1,0:T(8,128)} %get-tuple-element.67.refs_3_.refs_4_, ...), custom_call_target="tpu_custom_call" | custom-call | flops 1024 | bytes 1024 | tf_op jit(solution)/shard_map/relay/pallas_call | solution.py:191
  86.7 1.5 collective-permute-start.11
  88.2 1.5 collective-permute-start.12
  89.7 17.7 %logits.6 = (f32[4096,128]{1,0:T(8,128)}, s16[4112,128]{1,0:T(8,128)(2,1)}, f32[4096,128]{1,0:T(8,128)}, s16[4112,128]{1,0:T(8,128)(2,1)}) custom-call(s32[1]{0:T(128)} %bitcast.t_ref.dep_p.dep_q, bf16[256,2176]{1,0:T(8,128)(2,1)} %all-gather.6.cloned.1.call-done.rows_ref, f32[1,2048]{1,0:T(1,128)} %bitcast.55, bf16[8192,2048]{1,0:T(8,128)(2,1)} %h_ref.11, ...), custom_call_target="tpu_custom_call" | custom-call | flops 1024 | bytes 1024 | tf_op jit(solution)/shard_map/logits/pallas_call | solution.py:129
  108.5 1.5 collective-permute-start.16
  110.0 3.1 collective-permute-done.11.refs_0_.refs_1_.refs_2_
  113.1 1.5 collective-permute-start.7
  115.1 6.1 %relay.5 = (s16[2064,128]{1,0:T(8,128)(2,1)}, f32[2048,128]{1,0:T(8,128)}, s16[2064,128]{1,0:T(8,128)(2,1)}, f32[2048,128]{1,0:T(8,128)}) custom-call(s16[4112,128]{1,0:T(8,128)(2,1)} %copy-done.4, s16[4112,128]{1,0:T(8,128)(2,1)} %copy-done.4, s16[4112,128]{1,0:T(8,128)(2,1)} %copy-done.4, f32[4096,128]{1,0:T(8,128)} %get-tuple-element.81.refs_3_.refs_4_, ...), custom_call_target="tpu_custom_call" | custom-call | flops 1024 | bytes 1024 | tf_op jit(solution)/shard_map/relay/pallas_call | solution.py:191
  121.2 1.5 collective-permute-start.13
  122.8 3.2 collective-permute-done.6.lp
  126.5 30.1 %logits.7 = (f32[4096,128]{1,0:T(8,128)}, s16[4112,128]{1,0:T(8,128)(2,1)}, f32[4096,128]{1,0:T(8,128)}, s16[4112,128]{1,0:T(8,128)(2,1)}) custom-call(s32[1]{0:T(128)} %bitcast.t_ref.dep_p.dep_q, bf16[256,4096]{1,0:T(8,128)(2,1)} %all-gather.8.cloned.1.call-done.rows_ref, f32[1,4096]{1,0:T(1,128)} %bitcast.59, bf16[8192,4096]{1,0:T(8,128)(2,1)} %h_ref.9, ...), custom_call_target="tpu_custom_call" | custom-call | flops 1024 | bytes 1024 | tf_op jit(solution)/shard_map/logits/pallas_call | solution.py:129
  156.7 1.5 collective-permute-start.21
  158.2 1.5 collective-permute-start.22
  159.7 4.4 %finish.4 = (f32[4096,128]{1,0:T(8,128)}, f32[8,128]{1,0:T(8,128)}) custom-call(f32[2048,128]{1,0:T(8,128)} %get-tuple-element.72.op, f32[2048,128]{1,0:T(8,128)} %get-tuple-element.73.dep_ref.oq, s16[2064,128]{1,0:T(8,128)(2,1)} %collective-permute-done.6.lp, s16[2064,128]{1,0:T(8,128)(2,1)} %collective-permute-done.7.lq, ...), custom_call_target="tpu_custom_call" | custom-call | flops 1024 | bytes 1024 | tf_op jit(solution)/shard_map/finish/pallas_call | solution.py:282
  165.1 6.1 %relay.6 = (s16[2064,128]{1,0:T(8,128)(2,1)}, f32[2048,128]{1,0:T(8,128)}, s16[2064,128]{1,0:T(8,128)(2,1)}, f32[2048,128]{1,0:T(8,128)}) custom-call(s16[4112,128]{1,0:T(8,128)(2,1)} %copy-done.2, s16[4112,128]{1,0:T(8,128)(2,1)} %copy-done.2, s16[4112,128]{1,0:T(8,128)(2,1)} %copy-done.2, f32[4096,128]{1,0:T(8,128)} %get-tuple-element.93.refs_3_.refs_4_, ...), custom_call_target="tpu_custom_call" | custom-call | flops 1024 | bytes 1024 | tf_op jit(solution)/shard_map/relay/pallas_call | solution.py:191
  172.2 4.7 %finish.5 = (f32[4096,128]{1,0:T(8,128)}, f32[8,128]{1,0:T(8,128)}) custom-call(f32[2048,128]{1,0:T(8,128)} %get-tuple-element.88.op, f32[2048,128]{1,0:T(8,128)} %get-tuple-element.85.dep_ref.oq, s16[2064,128]{1,0:T(8,128)(2,1)} %copy-done.23, s16[2064,128]{1,0:T(8,128)(2,1)} %copy-done.24, bf16[64,128]{1,0:T(8,128)(2,1)} %constant_dynamic-slice_fusion.inv_ref, ...), custom_call_target="tpu_custom_call" | custom-call | flops 1024 | bytes 1024 | tf_op jit(solution)/shard_map/finish/pallas_call | solution.py:282
  176.9 1.5 collective-permute-start.17
  178.4 1.0 collective-permute-start.18
  179.4 1.8 collective-permute-start.19
  183.7 1.4 collective-permute-done.19
  187.1 6.5 %relay.7 = (s16[2064,128]{1,0:T(8,128)(2,1)}, f32[2048,128]{1,0:T(8,128)}, s16[2064,128]{1,0:T(8,128)(2,1)}, f32[2048,128]{1,0:T(8,128)}) custom-call(s16[4112,128]{1,0:T(8,128)(2,1)} %copy-done, s16[4112,128]{1,0:T(8,128)(2,1)} %copy-done, s16[4112,128]{1,0:T(8,128)(2,1)} %copy-done, f32[4096,128]{1,0:T(8,128)} %get-tuple-element.99.refs_3_.refs_4_, ...), custom_call_target="tpu_custom_call" | custom-call | flops 1024 | bytes 1024 | tf_op jit(solution)/shard_map/relay/pallas_call | solution.py:191
  194.3 1.6 collective-permute-start.30
  196.5 5.3 %slope.2.dep.own = bf16[64,8320]{1,0:T(8,128)(2,1)} custom-call(f32[4096,128]{1,0:T(8,128)} %get-tuple-element.87.student_ref, f32[4096,128]{1,0:T(8,128)} %get-tuple-element.96.teacher_ref, f32[8,8,128]{2,1,0:T(8,128)} %copy-done.33, s32[1,128]{1,0:T(1,128)} %add_bitcast_fusion.target_ref, s32[1]{0:T(128)} %bitcast.9.dep_ref.base_ref, ...), custom_call_target="tpu_custom_call" | custom-call | flops 1024 | bytes 1024 | tf_op jit(solution)/shard_map/slope/pallas_call | solution.py:362
  201.8 1.4 collective-permute-start.24
  204.4 4.4 %finish.6 = (f32[4096,128]{1,0:T(8,128)}, f32[8,128]{1,0:T(8,128)}) custom-call(f32[2048,128]{1,0:T(8,128)} %get-tuple-element.102.op, f32[2048,128]{1,0:T(8,128)} %get-tuple-element.95.dep.oq, s16[2064,128]{1,0:T(8,128)(2,1)} %copy-done.21, s16[2064,128]{1,0:T(8,128)(2,1)} %copy-done.22, bf16[64,128]{1,0:T(8,128)(2,1)} %constant_dynamic-slice_fusion.inv_ref, ...), custom_call_target="tpu_custom_call" | custom-call | flops 1024 | bytes 1024 | tf_op jit(solution)/shard_map/finish/pallas_call | solution.py:282
  210.2 4.6 %finish.7 = (f32[4096,128]{1,0:T(8,128)}, f32[8,128]{1,0:T(8,128)}) custom-call(f32[2048,128]{1,0:T(8,128)} %get-tuple-element.106.op, f32[2048,128]{1,0:T(8,128)} %get-tuple-element.101.dep.oq, s16[2064,128]{1,0:T(8,128)(2,1)} %copy-done.19, s16[2064,128]{1,0:T(8,128)(2,1)} %copy-done.20, bf16[64,128]{1,0:T(8,128)(2,1)} %constant_dynamic-slice_fusion.inv_ref, ...), custom_call_target="tpu_custom_call" | custom-call | flops 1024 | bytes 1024 | tf_op jit(solution)/shard_map/finish/pallas_call | solution.py:282
  214.8 2.4 collective-permute-start.32
  217.2 1.9 collective-permute-start.33
  219.9 3.0 collective-permute-done.33
  223.5 7.6 %collective-permute-done.24.gy = bf16[64,8320]{1,0:T(8,128)(2,1)S(1)} collective-permute-done((bf16[64,8320]{1,0:T(8,128)(2,1)}, bf16[64,8320]{1,0:T(8,128)(2,1)S(1)}, u32[]{:S(2)}, u32[]{:S(2)}) %collective-permute-start.24) | collective-permute-done | bytes 1064992 | tf_op jit(solution)/shard_map/ppermute | solution.py:612
  231.1 1.7 collective-permute-start.26
  234.2 5.3 %slope.3.dep.own = bf16[64,8320]{1,0:T(8,128)(2,1)} custom-call(f32[4096,128]{1,0:T(8,128)} %get-tuple-element.105.student_ref, f32[4096,128]{1,0:T(8,128)} %get-tuple-element.110.teacher_ref, f32[8,8,128]{2,1,0:T(8,128)} %copy-done.34, s32[1,128]{1,0:T(1,128)} %add_bitcast_fusion.1.target_ref, s32[1]{0:T(128)} %bitcast.9.dep_ref.base_ref, ...), custom_call_target="tpu_custom_call" | custom-call | flops 1024 | bytes 1024 | tf_op jit(solution)/shard_map/slope/pallas_call | solution.py:362
  239.5 1.4 collective-permute-start.36
  241.9 5.8 %collective-permute-done.25.dp = bf16[64,4096]{1,0:T(8,128)(2,1)S(1)} collective-permute-done((bf16[64,4096]{1,0:T(8,128)(2,1)S(1)}, bf16[64,4096]{1,0:T(8,128)(2,1)S(1)}, u32[]{:S(2)}, u32[]{:S(2)}) %collective-permute-start.25) | collective-permute-done | bytes 524320 | tf_op jit(solution)/shard_map/ppermute | solution.py:614
  248.8 17.5 %norm_grad.2 = (f32[128,2176]{1,0:T(8,128)}, f32[128,2176]{1,0:T(8,128)}, f32[8,128]{1,0:T(8,128)}) custom-call(s32[1]{0:T(128)} %bitcast.t_ref.dep_p.dep_q, s32[1]{0:T(128)} %bitcast.1.flip_ref, bf16[64,8320]{1,0:T(8,128)(2,1)} %slope.2.dep.own, bf16[64,8320]{1,0:T(8,128)(2,1)} %copy-done.10, bf16[64,8320]{1,0:T(8,128)(2,1)} %copy-done.8, ...), custom_call_target="tpu_custom_call" | custom-call | flops 1024 | bytes 1024 | tf_op jit(solution)/shard_map/norm_grad/pallas_call | solution.py:418
  266.4 2.6 collective-permute-done.36.gy
  269.6 1.2 collective-permute-start.37
  270.8 1.1 copy-done.16
  271.9 2.7 fold.2
  274.7 1.9 collective-permute-start.41
  276.6 2.4 collective-permute-start.42
  279.1 1.9 collective-permute-done.40.p1
  280.9 6.7 %collective-permute-done.41.p2 = s16[32,2176]{1,0:T(8,128)(2,1)S(1)} collective-permute-done((s16[32,2176]{1,0:T(8,128)(2,1)}, s16[32,2176]{1,0:T(8,128)(2,1)S(1)}, u32[]{:S(2)}, u32[]{:S(2)}) %collective-permute-start.41) | collective-permute-done | bytes 139296 | tf_op jit(solution)/shard_map/ppermute | solution.py:663
  288.3 2.2 hidden_grad.2.dep.before
  292.1 17.4 %norm_grad.3 = (f32[128,2176]{1,0:T(8,128)}, f32[128,2176]{1,0:T(8,128)}, f32[8,128]{1,0:T(8,128)}) custom-call(s32[1]{0:T(128)} %bitcast.t_ref.dep_p.dep_q, s32[1]{0:T(128)} %bitcast.1.flip_ref, bf16[64,8320]{1,0:T(8,128)(2,1)} %slope.3.dep.own, bf16[64,8320]{1,0:T(8,128)(2,1)} %copy-done.11, bf16[64,8320]{1,0:T(8,128)(2,1)} %copy-done.9, ...), custom_call_target="tpu_custom_call" | custom-call | flops 1024 | bytes 1024 | tf_op jit(solution)/shard_map/norm_grad/pallas_call | solution.py:418
  309.4 3.0 collective-permute-done.43.other_ref
  313.4 2.7 fold.3
  316.1 2.0 collective-permute-start.44
  318.1 2.4 collective-permute-start.46
  320.5 1.2 slice.52
  321.7 1.2 slice.55
  324.2 7.4 %collective-permute-done.45.p2 = s16[32,2176]{1,0:T(8,128)(2,1)S(1)} collective-permute-done((s16[32,2176]{1,0:T(8,128)(2,1)}, s16[32,2176]{1,0:T(8,128)(2,1)S(1)}, u32[]{:S(2)}, u32[]{:S(2)}) %collective-permute-start.45) | collective-permute-done | bytes 139296 | tf_op jit(solution)/shard_map/ppermute | solution.py:663
  332.3 2.2 hidden_grad.3
  (186 shorter events, 29.9 us)
Async XLA Ops:
  7.2 11.2 %copy-start.7 = (bf16[64,2048]{1,0:T(8,128)(2,1)S(1)}, bf16[64,2048]{1,0:T(8,128)(2,1)}, u32[]{:S(2)}) copy-start(bf16[64,2048]{1,0:T(8,128)(2,1)} %hidden_ref.3) | copy-start | bytes 786436
  7.2 11.2 %copy-start.13 = (bf16[64,4096]{1,0:T(8,128)(2,1)S(1)}, bf16[64,4096]{1,0:T(8,128)(2,1)}, u32[]{:S(2)}) copy-start(bf16[64,4096]{1,0:T(8,128)(2,1)} %param.8) | copy-start | bytes 1572868
  7.2 41.9 %all-gather.4.cloned.1.call-start = ((), (), s32[]{:S(2)}) async-start(), calls=%async_computation | async-start | bytes 2359296 | tf_op jit(solution)/shard_map/all_gather | solution.py:563
  8.3 10.0 %collective-permute-start = (bf16[32,2048]{1,0:T(8,128)(2,1)S(1)}, bf16[32,2048]{1,0:T(8,128)(2,1)S(1)}, u32[]{:S(2)}, u32[]{:S(2)}) collective-permute-start(bf16[32,2048]{1,0:T(8,128)(2,1)S(1)} %get-tuple-element.132), channel_id=1, source_target_pairs={{0,4},{4,0},{8,12},{12,8},{1,5},{5,1},{9,13},{13,9},{2,6},{6,2},{1... | collective-permute-start | bytes 393224 | tf_op jit(solution)/shard_map/ppermute | solution.py:524
  11.4 12.9 %collective-permute-start.1 = (bf16[32,2048]{1,0:T(8,128)(2,1)S(1)}, bf16[32,2048]{1,0:T(8,128)(2,1)S(1)}, u32[]{:S(2)}, u32[]{:S(2)}) collective-permute-start(bf16[32,2048]{1,0:T(8,128)(2,1)S(1)} %get-tuple-element.132), channel_id=1, source_target_pairs={{0,8},{4,12},{8,0},{12,4},{1,9},{5,13},{9,1},{13,5},{2,10},{6,14},... | collective-permute-start | bytes 393224 | tf_op jit(solution)/shard_map/ppermute | solution.py:524
  14.0 10.3 %collective-permute-start.2 = (bf16[32,2048]{1,0:T(8,128)(2,1)S(1)}, bf16[32,2048]{1,0:T(8,128)(2,1)S(1)}, u32[]{:S(2)}, u32[]{:S(2)}) collective-permute-start(bf16[32,2048]{1,0:T(8,128)(2,1)S(1)} %get-tuple-element.132), channel_id=1, source_target_pairs={{0,12},{4,8},{8,4},{12,0},{1,13},{5,9},{9,5},{13,1},{2,14},{6,10},... | collective-permute-start | bytes 393224 | tf_op jit(solution)/shard_map/ppermute | solution.py:524
  18.3 71.4 %all-gather.6.cloned.1.call-start = ((), (), s32[]{:S(2)}) async-start(), calls=%async_computation.1 | async-start | bytes 1253376 | tf_op jit(solution)/shard_map/all_gather | solution.py:563
  18.6 7.0 %copy-start.35 = (f32[2]{0:T(128)S(1)}, f32[2]{0:T(128)}, u32[]{:S(2)}) copy-start(f32[2]{0:T(128)} %constant.43) | copy-start | bytes 28
  18.8 5.7 %collective-permute-start.10 = (f32[2,64]{1,0:T(2,128)S(1)}, f32[2,64]{1,0:T(2,128)S(1)}, u32[]{:S(2)}, u32[]{:S(2)}) collective-permute-start(f32[2,64]{1,0:T(2,128)S(1)} %pad_maximum_fusion.4), channel_id=1, source_target_pairs={{0,3},{1,2},{2,1},{3,0},{4,7},{5,6},{6,5},{7,4},{8,11},{9,10},{10,... | collective-permute-start | bytes 1544 | tf_op jit(solution)/shard_map/ppermute | solution.py:515
  21.5 3.6 %collective-permute-start.8 = (f32[2,64]{1,0:T(2,128)S(1)}, f32[2,64]{1,0:T(2,128)S(1)}, u32[]{:S(2)}, u32[]{:S(2)}) collective-permute-start(f32[2,64]{1,0:T(2,128)S(1)} %pad_maximum_fusion.4), channel_id=1, source_target_pairs={{0,1},{1,0},{2,3},{3,2},{4,5},{5,4},{6,7},{7,6},{8,9},{9,8},{10,11... | collective-permute-start | bytes 1544 | tf_op jit(solution)/shard_map/ppermute | solution.py:513
  22.1 3.6 %collective-permute-start.9 = (f32[2,64]{1,0:T(2,128)S(1)}, f32[2,64]{1,0:T(2,128)S(1)}, u32[]{:S(2)}, u32[]{:S(2)}) collective-permute-start(f32[2,64]{1,0:T(2,128)S(1)} %pad_maximum_fusion.4), channel_id=1, source_target_pairs={{0,2},{1,3},{2,0},{3,1},{4,6},{5,7},{6,4},{7,5},{8,10},{9,11},{10,... | collective-permute-start | bytes 1544 | tf_op jit(solution)/shard_map/ppermute | solution.py:514
  24.4 2.3 collective-permute-start.3
  46.0 80.5 %all-gather.8.cloned.1.call-start = ((), (), s32[]{:S(2)}) async-start(), calls=%async_computation.2 | async-start | bytes 2359296 | tf_op jit(solution)/shard_map/all_gather | solution.py:563
  46.3 33.0 %collective-permute-start.4 = (s16[4112,128]{1,0:T(8,128)(2,1)}, s16[4112,128]{1,0:T(8,128)(2,1)S(1)}, u32[]{:S(2)}, u32[]{:S(2)}) collective-permute-start(s16[4112,128]{1,0:T(8,128)(2,1)} %get-tuple-element.66), channel_id=1, source_target_pairs={{0,1},{1,0},{2,3},{3,2},{4,5},{5,4},{6,7},{7,6},{8,9},{9,8},{10,11... | collective-permute-start | bytes 3158024 | tf_op jit(solution)/shard_map/ppermute | solution.py:601
  47.8 31.4 %collective-permute-start.5 = (s16[4112,128]{1,0:T(8,128)(2,1)}, s16[4112,128]{1,0:T(8,128)(2,1)S(1)}, u32[]{:S(2)}, u32[]{:S(2)}) collective-permute-start(s16[4112,128]{1,0:T(8,128)(2,1)} %get-tuple-element.68), channel_id=1, source_target_pairs={{0,2},{1,3},{2,0},{3,1},{4,6},{5,7},{6,4},{7,5},{8,10},{9,11},{10,... | collective-permute-start | bytes 3158024 | tf_op jit(solution)/shard_map/ppermute | solution.py:601
  86.7 26.4 %collective-permute-start.11 = (s16[4112,128]{1,0:T(8,128)(2,1)}, s16[4112,128]{1,0:T(8,128)(2,1)S(1)}, u32[]{:S(2)}, u32[]{:S(2)}) collective-permute-start(s16[4112,128]{1,0:T(8,128)(2,1)} %get-tuple-element.80), channel_id=1, source_target_pairs={{0,1},{1,0},{2,3},{3,2},{4,5},{5,4},{6,7},{7,6},{8,9},{9,8},{10,11... | collective-permute-start | bytes 3158024 | tf_op jit(solution)/shard_map/ppermute | solution.py:601
  88.2 26.9 %collective-permute-start.12 = (s16[4112,128]{1,0:T(8,128)(2,1)}, s16[4112,128]{1,0:T(8,128)(2,1)}, u32[]{:S(2)}, u32[]{:S(2)}) collective-permute-start(s16[4112,128]{1,0:T(8,128)(2,1)} %get-tuple-element.82), channel_id=1, source_target_pairs={{0,2},{1,3},{2,0},{3,1},{4,6},{5,7},{6,4},{7,5},{8,10},{9,11},{10,... | collective-permute-start | bytes 3158024 | tf_op jit(solution)/shard_map/ppermute | solution.py:601
  89.7 24.8 %slice-start = ((bf16[256,2176]{1,0:T(8,128)(2,1)}), bf16[256,128]{1,0:T(8,128)(2,1)S(1)}, s32[]{:S(2)}) async-start(bf16[256,2176]{1,0:T(8,128)(2,1)} %all-gather.6.cloned.1.call-done.rows_ref), calls=%async_computation.3 | async-start | bytes 131072 | tf_op jit(solution)/shard_map/slice | solution.py:627
  107.4 50.8 %collective-permute-start.15 = (s16[4112,128]{1,0:T(8,128)(2,1)}, s16[4112,128]{1,0:T(8,128)(2,1)S(1)}, u32[]{:S(2)}, u32[]{:S(2)}) collective-permute-start(s16[4112,128]{1,0:T(8,128)(2,1)} %get-tuple-element.92), channel_id=1, source_target_pairs={{0,1},{1,0},{2,3},{3,2},{4,5},{5,4},{6,7},{7,6},{8,9},{9,8},{10,11... | collective-permute-start | bytes 3158024 | tf_op jit(solution)/shard_map/ppermute | solution.py:601
  108.0 18.0 %collective-permute-start.6 = (s16[2064,128]{1,0:T(8,128)(2,1)}, s16[2064,128]{1,0:T(8,128)(2,1)}, u32[]{:S(2)}, u32[]{:S(2)}) collective-permute-start(s16[2064,128]{1,0:T(8,128)(2,1)} %get-tuple-element.74), channel_id=1, source_target_pairs={{0,2},{1,3},{2,0},{3,1},{4,6},{5,7},{6,4},{7,5},{8,10},{9,11},{10,... | collective-permute-start | bytes 1585160 | tf_op jit(solution)/shard_map/ppermute | solution.py:606
  108.5 55.5 %collective-permute-start.16 = (s16[4112,128]{1,0:T(8,128)(2,1)}, s16[4112,128]{1,0:T(8,128)(2,1)S(1)}, u32[]{:S(2)}, u32[]{:S(2)}) collective-permute-start(s16[4112,128]{1,0:T(8,128)(2,1)} %get-tuple-element.94), channel_id=1, source_target_pairs={{0,2},{1,3},{2,0},{3,1},{4,6},{5,7},{6,4},{7,5},{8,10},{9,11},{10,... | collective-permute-start | bytes 3158024 | tf_op jit(solution)/shard_map/ppermute | solution.py:601
  113.1 2.1 copy-start.4
  113.1 43.6 %collective-permute-start.7 = (s16[2064,128]{1,0:T(8,128)(2,1)}, s16[2064,128]{1,0:T(8,128)(2,1)}, u32[]{:S(2)}, u32[]{:S(2)}) collective-permute-start(s16[2064,128]{1,0:T(8,128)(2,1)} %get-tuple-element.75), channel_id=1, source_target_pairs={{0,1},{1,0},{2,3},{3,2},{4,5},{5,4},{6,7},{7,6},{8,9},{9,8},{10,11... | collective-permute-start | bytes 1585160 | tf_op jit(solution)/shard_map/ppermute | solution.py:607
  121.2 50.0 %collective-permute-start.13 = (s16[2064,128]{1,0:T(8,128)(2,1)}, s16[2064,128]{1,0:T(8,128)(2,1)S(1)}, u32[]{:S(2)}, u32[]{:S(2)}) collective-permute-start(s16[2064,128]{1,0:T(8,128)(2,1)} %get-tuple-element.89), channel_id=1, source_target_pairs={{0,2},{1,3},{2,0},{3,1},{4,6},{5,7},{6,4},{7,5},{8,10},{9,11},{10,... | collective-permute-start | bytes 1585160 | tf_op jit(solution)/shard_map/ppermute | solution.py:606
  126.0 45.2 %collective-permute-start.14 = (s16[2064,128]{1,0:T(8,128)(2,1)}, s16[2064,128]{1,0:T(8,128)(2,1)S(1)}, u32[]{:S(2)}, u32[]{:S(2)}) collective-permute-start(s16[2064,128]{1,0:T(8,128)(2,1)} %get-tuple-element.90), channel_id=1, source_target_pairs={{0,1},{1,0},{2,3},{3,2},{4,5},{5,4},{6,7},{7,6},{8,9},{9,8},{10,11... | collective-permute-start | bytes 1585160 | tf_op jit(solution)/shard_map/ppermute | solution.py:607
  156.7 29.1 %collective-permute-start.21 = (s16[4112,128]{1,0:T(8,128)(2,1)}, s16[4112,128]{1,0:T(8,128)(2,1)S(1)}, u32[]{:S(2)}, u32[]{:S(2)}) collective-permute-start(s16[4112,128]{1,0:T(8,128)(2,1)} %get-tuple-element.98), channel_id=1, source_target_pairs={{0,1},{1,0},{2,3},{3,2},{4,5},{5,4},{6,7},{7,6},{8,9},{9,8},{10,11... | collective-permute-start | bytes 3158024 | tf_op jit(solution)/shard_map/ppermute | solution.py:601
  158.2 5.8 %copy-start.2 = (s16[4112,128]{1,0:T(8,128)(2,1)}, s16[4112,128]{1,0:T(8,128)(2,1)S(1)}, u32[]{:S(2)}) copy-start(s16[4112,128]{1,0:T(8,128)(2,1)S(1)} %collective-permute-done.15.refs_0_.refs_1_.refs_2_) | copy-start | bytes 3158020
  158.2 27.6 %collective-permute-start.22 = (s16[4112,128]{1,0:T(8,128)(2,1)}, s16[4112,128]{1,0:T(8,128)(2,1)S(1)}, u32[]{:S(2)}, u32[]{:S(2)}) collective-permute-start(s16[4112,128]{1,0:T(8,128)(2,1)} %get-tuple-element.100), channel_id=1, source_target_pairs={{0,2},{1,3},{2,0},{3,1},{4,6},{5,7},{6,4},{7,5},{8,10},{9,11},{10,... | collective-permute-start | bytes 3158024 | tf_op jit(solution)/shard_map/ppermute | solution.py:601
  172.2 9.8 %copy-start.37 = (s16[2064,128]{1,0:T(8,128)(2,1)S(1)}, s16[2064,128]{1,0:T(8,128)(2,1)}, u32[]{:S(2)}) copy-start(s16[2064,128]{1,0:T(8,128)(2,1)} %get-tuple-element.103) | copy-start | bytes 1585156
  172.2 10.9 %copy-start.36 = (s16[2064,128]{1,0:T(8,128)(2,1)S(1)}, s16[2064,128]{1,0:T(8,128)(2,1)}, u32[]{:S(2)}) copy-start(s16[2064,128]{1,0:T(8,128)(2,1)} %get-tuple-element.104) | copy-start | bytes 1585156
  176.9 5.1 %collective-permute-start.17 = (f32[8,128]{1,0:T(8,128)}, f32[8,128]{1,0:T(8,128)S(1)}, u32[]{:S(2)}, u32[]{:S(2)}) collective-permute-start(f32[8,128]{1,0:T(8,128)} %get-tuple-element.97.refs_10_), channel_id=1, source_target_pairs={{0,4},{4,0},{8,12},{12,8},{1,5},{5,1},{9,13},{13,9},{2,6},{6,2},{1... | collective-permute-start | bytes 12296 | tf_op jit(solution)/shard_map/ppermute | solution.py:524
  178.4 4.7 %collective-permute-start.18 = (f32[8,128]{1,0:T(8,128)}, f32[8,128]{1,0:T(8,128)S(1)}, u32[]{:S(2)}, u32[]{:S(2)}) collective-permute-start(f32[8,128]{1,0:T(8,128)} %get-tuple-element.97.refs_10_), channel_id=1, source_target_pairs={{0,8},{4,12},{8,0},{12,4},{1,9},{5,13},{9,1},{13,5},{2,10},{6,14},... | collective-permute-start | bytes 12296 | tf_op jit(solution)/shard_map/ppermute | solution.py:524
  179.4 5.6 %collective-permute-start.19 = (f32[8,128]{1,0:T(8,128)}, f32[8,128]{1,0:T(8,128)S(1)}, u32[]{:S(2)}, u32[]{:S(2)}) collective-permute-start(f32[8,128]{1,0:T(8,128)} %get-tuple-element.97.refs_10_), channel_id=1, source_target_pairs={{0,12},{4,8},{8,4},{12,0},{1,13},{5,9},{9,5},{13,1},{2,14},{6,10},... | collective-permute-start | bytes 12296 | tf_op jit(solution)/shard_map/ppermute | solution.py:524
  182.0 21.2 %collective-permute-start.27 = (s16[2064,128]{1,0:T(8,128)(2,1)S(1)}, s16[2064,128]{1,0:T(8,128)(2,1)S(1)}, u32[]{:S(2)}, u32[]{:S(2)}) collective-permute-start(s16[2064,128]{1,0:T(8,128)(2,1)S(1)} %copy-done.37), channel_id=1, source_target_pairs={{0,2},{1,3},{2,0},{3,1},{4,6},{5,7},{6,4},{7,5},{8,10},{9,11},{10,... | collective-permute-start | bytes 1585160 | tf_op jit(solution)/shard_map/ppermute | solution.py:606
  183.1 20.5 %collective-permute-start.28 = (s16[2064,128]{1,0:T(8,128)(2,1)S(1)}, s16[2064,128]{1,0:T(8,128)(2,1)S(1)}, u32[]{:S(2)}, u32[]{:S(2)}) collective-permute-start(s16[2064,128]{1,0:T(8,128)(2,1)S(1)} %copy-done.36), channel_id=1, source_target_pairs={{0,1},{1,0},{2,3},{3,2},{4,5},{5,4},{6,7},{7,6},{8,9},{9,8},{10,11... | collective-permute-start | bytes 1585160 | tf_op jit(solution)/shard_map/ppermute | solution.py:607
  185.7 10.2 %collective-permute-start.20 = (f32[4,8,128]{2,1,0:T(8,128)S(1)}, f32[4,8,128]{2,1,0:T(8,128)S(1)}, u32[]{:S(2)}, u32[]{:S(2)}) collective-permute-start(f32[4,8,128]{2,1,0:T(8,128)S(1)} %pad_maximum_fusion.2), channel_id=1, source_target_pairs={{0,16},{16,0},{1,17},{17,1},{2,18},{18,2},{3,19},{19,3},{4,20},{20... | collective-permute-start | bytes 49160 | tf_op jit(solution)/shard_map/ppermute | solution.py:531
  193.6 15.3 %collective-permute-start.29 = (s16[2064,128]{1,0:T(8,128)(2,1)}, s16[2064,128]{1,0:T(8,128)(2,1)S(1)}, u32[]{:S(2)}, u32[]{:S(2)}) collective-permute-start(s16[2064,128]{1,0:T(8,128)(2,1)} %get-tuple-element.107), channel_id=1, source_target_pairs={{0,2},{1,3},{2,0},{3,1},{4,6},{5,7},{6,4},{7,5},{8,10},{9,11},{10,... | collective-permute-start | bytes 1585160 | tf_op jit(solution)/shard_map/ppermute | solution.py:606
  194.3 15.1 %collective-permute-start.30 = (s16[2064,128]{1,0:T(8,128)(2,1)}, s16[2064,128]{1,0:T(8,128)(2,1)S(1)}, u32[]{:S(2)}, u32[]{:S(2)}) collective-permute-start(s16[2064,128]{1,0:T(8,128)(2,1)} %get-tuple-element.108), channel_id=1, source_target_pairs={{0,1},{1,0},{2,3},{3,2},{4,5},{5,4},{6,7},{7,6},{8,9},{9,8},{10,11... | collective-permute-start | bytes 1585160 | tf_op jit(solution)/shard_map/ppermute | solution.py:607
  201.8 29.3 %collective-permute-start.24 = (bf16[64,8320]{1,0:T(8,128)(2,1)}, bf16[64,8320]{1,0:T(8,128)(2,1)S(1)}, u32[]{:S(2)}, u32[]{:S(2)}) collective-permute-start(bf16[64,8320]{1,0:T(8,128)(2,1)} %slope.2.dep.own), channel_id=1, source_target_pairs={{0,2},{1,3},{2,0},{3,1},{4,6},{5,7},{6,4},{7,5},{8,10},{9,11},{10,... | collective-permute-start | bytes 3194888 | tf_op jit(solution)/shard_map/ppermute | solution.py:612
  203.2 29.6 %collective-permute-start.23 = (bf16[64,8320]{1,0:T(8,128)(2,1)}, bf16[64,8320]{1,0:T(8,128)(2,1)S(1)}, u32[]{:S(2)}, u32[]{:S(2)}) collective-permute-start(bf16[64,8320]{1,0:T(8,128)(2,1)} %slope.2.dep.own), channel_id=1, source_target_pairs={{0,1},{1,0},{2,3},{3,2},{4,5},{5,4},{6,7},{7,6},{8,9},{9,8},{10,11... | collective-permute-start | bytes 3194888 | tf_op jit(solution)/shard_map/ppermute | solution.py:611
  214.8 5.1 %collective-permute-start.31 = (f32[8,128]{1,0:T(8,128)}, f32[8,128]{1,0:T(8,128)S(1)}, u32[]{:S(2)}, u32[]{:S(2)}) collective-permute-start(f32[8,128]{1,0:T(8,128)} %get-tuple-element.112.dep), channel_id=1, source_target_pairs={{0,4},{4,0},{8,12},{12,8},{1,5},{5,1},{9,13},{13,9},{2,6},{6,2},{1... | collective-permute-start | bytes 12296 | tf_op jit(solution)/shard_map/ppermute | solution.py:524
  214.8 5.1 %collective-permute-start.32 = (f32[8,128]{1,0:T(8,128)}, f32[8,128]{1,0:T(8,128)S(1)}, u32[]{:S(2)}, u32[]{:S(2)}) collective-permute-start(f32[8,128]{1,0:T(8,128)} %get-tuple-element.112.dep), channel_id=1, source_target_pairs={{0,8},{4,12},{8,0},{12,4},{1,9},{5,13},{9,1},{13,5},{2,10},{6,14},... | collective-permute-start | bytes 12296 | tf_op jit(solution)/shard_map/ppermute | solution.py:524
  217.2 5.6 %collective-permute-start.33 = (f32[8,128]{1,0:T(8,128)}, f32[8,128]{1,0:T(8,128)S(1)}, u32[]{:S(2)}, u32[]{:S(2)}) collective-permute-start(f32[8,128]{1,0:T(8,128)} %get-tuple-element.112.dep), channel_id=1, source_target_pairs={{0,12},{4,8},{8,4},{12,0},{1,13},{5,9},{9,5},{13,1},{2,14},{6,10},... | collective-permute-start | bytes 12296 | tf_op jit(solution)/shard_map/ppermute | solution.py:524
  223.5 10.1 %collective-permute-start.34 = (f32[4,8,128]{2,1,0:T(8,128)S(1)}, f32[4,8,128]{2,1,0:T(8,128)S(1)}, u32[]{:S(2)}, u32[]{:S(2)}) collective-permute-start(f32[4,8,128]{2,1,0:T(8,128)S(1)} %pad_maximum_fusion.3), channel_id=1, source_target_pairs={{0,16},{16,0},{1,17},{17,1},{2,18},{18,2},{3,19},{19,3},{4,20},{20... | collective-permute-start | bytes 49160 | tf_op jit(solution)/shard_map/ppermute | solution.py:531
  231.1 8.4 %copy-start.8 = (bf16[64,8320]{1,0:T(8,128)(2,1)}, bf16[64,8320]{1,0:T(8,128)(2,1)S(1)}, u32[]{:S(2)}) copy-start(bf16[64,8320]{1,0:T(8,128)(2,1)S(1)} %collective-permute-done.24.gy) | copy-start | bytes 3194884
  231.1 16.7 %collective-permute-start.26 = (bf16[64,4224]{1,0:T(8,128)(2,1)S(1)}, bf16[64,4224]{1,0:T(8,128)(2,1)S(1)}, u32[]{:S(2)}, u32[]{:S(2)}) collective-permute-start(bf16[64,4224]{1,0:T(8,128)(2,1)S(1)} %slice.60), channel_id=1, source_target_pairs={{0,1},{1,0},{2,3},{3,2},{4,5},{5,4},{6,7},{7,6},{8,9},{9,8},{10,11... | collective-permute-start | bytes 1622024 | tf_op jit(solution)/shard_map/ppermute | solution.py:615
  232.8 6.7 %copy-start.10 = (bf16[64,8320]{1,0:T(8,128)(2,1)}, bf16[64,8320]{1,0:T(8,128)(2,1)S(1)}, u32[]{:S(2)}) copy-start(bf16[64,8320]{1,0:T(8,128)(2,1)S(1)} %collective-permute-done.23.gx) | copy-start | bytes 3194884
  232.8 14.9 %collective-permute-start.25 = (bf16[64,4096]{1,0:T(8,128)(2,1)S(1)}, bf16[64,4096]{1,0:T(8,128)(2,1)S(1)}, u32[]{:S(2)}, u32[]{:S(2)}) collective-permute-start(bf16[64,4096]{1,0:T(8,128)(2,1)S(1)} %slice.59), channel_id=1, source_target_pairs={{0,2},{1,3},{2,0},{3,1},{4,6},{5,7},{6,4},{7,5},{8,10},{9,11},{10,... | collective-permute-start | bytes 1572872 | tf_op jit(solution)/shard_map/ppermute | solution.py:614
  239.5 29.5 %collective-permute-start.36 = (bf16[64,8320]{1,0:T(8,128)(2,1)}, bf16[64,8320]{1,0:T(8,128)(2,1)S(1)}, u32[]{:S(2)}, u32[]{:S(2)}) collective-permute-start(bf16[64,8320]{1,0:T(8,128)(2,1)} %slope.3.dep.own), channel_id=1, source_target_pairs={{0,2},{1,3},{2,0},{3,1},{4,6},{5,7},{6,4},{7,5},{8,10},{9,11},{10,... | collective-permute-start | bytes 3194888 | tf_op jit(solution)/shard_map/ppermute | solution.py:612
  240.8 28.7 %collective-permute-start.35 = (bf16[64,8320]{1,0:T(8,128)(2,1)}, bf16[64,8320]{1,0:T(8,128)(2,1)S(1)}, u32[]{:S(2)}, u32[]{:S(2)}) collective-permute-start(bf16[64,8320]{1,0:T(8,128)(2,1)} %slope.3.dep.own), channel_id=1, source_target_pairs={{0,1},{1,0},{2,3},{3,2},{4,5},{5,4},{6,7},{7,6},{8,9},{9,8},{10,11... | collective-permute-start | bytes 3194888 | tf_op jit(solution)/shard_map/ppermute | solution.py:611
  266.3 4.5 %collective-permute-start.39 = (f32[128,2176]{1,0:T(8,128)}, f32[128,2176]{1,0:T(8,128)S(1)}, u32[]{:S(2)}, u32[]{:S(2)}) collective-permute-start(f32[128,2176]{1,0:T(8,128)} %get-tuple-element.116), channel_id=1, source_target_pairs={{0,16},{16,0},{1,17},{17,1},{2,18},{18,2},{3,19},{19,3},{4,20},{20... | collective-permute-start | bytes 3342344 | tf_op jit(solution)/shard_map/ppermute | solution.py:659
  269.0 5.6 %copy-start.9 = (bf16[64,8320]{1,0:T(8,128)(2,1)}, bf16[64,8320]{1,0:T(8,128)(2,1)S(1)}, u32[]{:S(2)}) copy-start(bf16[64,8320]{1,0:T(8,128)(2,1)S(1)} %collective-permute-done.36.gy) | copy-start | bytes 3194884
  269.0 21.4 %collective-permute-start.38 = (bf16[64,4224]{1,0:T(8,128)(2,1)S(1)}, bf16[64,4224]{1,0:T(8,128)(2,1)S(1)}, u32[]{:S(2)}, u32[]{:S(2)}) collective-permute-start(bf16[64,4224]{1,0:T(8,128)(2,1)S(1)} %slice.62.dep_q), channel_id=1, source_target_pairs={{0,1},{1,0},{2,3},{3,2},{4,5},{5,4},{6,7},{7,6},{8,9},{9,8},{10,11... | collective-permute-start | bytes 1622024 | tf_op jit(solution)/shard_map/ppermute | solution.py:615
  269.5 5.1 %copy-start.11 = (bf16[64,8320]{1,0:T(8,128)(2,1)}, bf16[64,8320]{1,0:T(8,128)(2,1)S(1)}, u32[]{:S(2)}) copy-start(bf16[64,8320]{1,0:T(8,128)(2,1)S(1)} %collective-permute-done.35.gx) | copy-start | bytes 3194884
  269.6 20.9 %collective-permute-start.37 = (bf16[64,4096]{1,0:T(8,128)(2,1)S(1)}, bf16[64,4096]{1,0:T(8,128)(2,1)S(1)}, u32[]{:S(2)}, u32[]{:S(2)}) collective-permute-start(bf16[64,4096]{1,0:T(8,128)(2,1)S(1)} %slice.61.dep_p), channel_id=1, source_target_pairs={{0,2},{1,3},{2,0},{3,1},{4,6},{5,7},{6,4},{7,5},{8,10},{9,11},{10,... | collective-permute-start | bytes 1572872 | tf_op jit(solution)/shard_map/ppermute | solution.py:614
  274.6 6.3 %collective-permute-start.40 = (s16[32,2176]{1,0:T(8,128)(2,1)}, s16[32,2176]{1,0:T(8,128)(2,1)S(1)}, u32[]{:S(2)}, u32[]{:S(2)}) collective-permute-start(s16[32,2176]{1,0:T(8,128)(2,1)} %get-tuple-element.118), channel_id=1, source_target_pairs={{0,4},{4,0},{8,12},{12,8},{1,5},{5,1},{9,13},{13,9},{2,6},{6,2},{1... | collective-permute-start | bytes 417800 | tf_op jit(solution)/shard_map/ppermute | solution.py:663
  274.7 12.9 %collective-permute-start.41 = (s16[32,2176]{1,0:T(8,128)(2,1)}, s16[32,2176]{1,0:T(8,128)(2,1)S(1)}, u32[]{:S(2)}, u32[]{:S(2)}) collective-permute-start(s16[32,2176]{1,0:T(8,128)(2,1)} %get-tuple-element.119), channel_id=1, source_target_pairs={{0,8},{4,12},{8,0},{12,4},{1,9},{5,13},{9,1},{13,5},{2,10},{6,14},... | collective-permute-start | bytes 417800 | tf_op jit(solution)/shard_map/ppermute | solution.py:663
  276.6 10.9 %collective-permute-start.42 = (s16[32,2176]{1,0:T(8,128)(2,1)}, s16[32,2176]{1,0:T(8,128)(2,1)S(1)}, u32[]{:S(2)}, u32[]{:S(2)}) collective-permute-start(s16[32,2176]{1,0:T(8,128)(2,1)} %get-tuple-element.120), channel_id=1, source_target_pairs={{0,12},{4,8},{8,4},{12,0},{1,13},{5,9},{9,5},{13,1},{2,14},{6,10},... | collective-permute-start | bytes 417800 | tf_op jit(solution)/shard_map/ppermute | solution.py:663
  280.9 6.7 %copy-start.30 = (s16[32,2176]{1,0:T(8,128)(2,1)}, s16[32,2176]{1,0:T(8,128)(2,1)S(1)}, u32[]{:S(2)}) copy-start(s16[32,2176]{1,0:T(8,128)(2,1)S(1)} %collective-permute-done.40.p1) | copy-start | bytes 417796
  309.4 3.0 collective-permute-start.43
  316.1 8.1 %collective-permute-start.44 = (s16[32,2176]{1,0:T(8,128)(2,1)}, s16[32,2176]{1,0:T(8,128)(2,1)S(1)}, u32[]{:S(2)}, u32[]{:S(2)}) collective-permute-start(s16[32,2176]{1,0:T(8,128)(2,1)} %get-tuple-element.125), channel_id=1, source_target_pairs={{0,4},{4,0},{8,12},{12,8},{1,5},{5,1},{9,13},{13,9},{2,6},{6,2},{1... | collective-permute-start | bytes 417800 | tf_op jit(solution)/shard_map/ppermute | solution.py:663
  318.1 13.5 %collective-permute-start.45 = (s16[32,2176]{1,0:T(8,128)(2,1)}, s16[32,2176]{1,0:T(8,128)(2,1)S(1)}, u32[]{:S(2)}, u32[]{:S(2)}) collective-permute-start(s16[32,2176]{1,0:T(8,128)(2,1)} %get-tuple-element.126), channel_id=1, source_target_pairs={{0,8},{4,12},{8,0},{12,4},{1,9},{5,13},{9,1},{13,5},{2,10},{6,14},... | collective-permute-start | bytes 417800 | tf_op jit(solution)/shard_map/ppermute | solution.py:663
  318.1 13.5 %collective-permute-start.46 = (s16[32,2176]{1,0:T(8,128)(2,1)}, s16[32,2176]{1,0:T(8,128)(2,1)S(1)}, u32[]{:S(2)}, u32[]{:S(2)}) collective-permute-start(s16[32,2176]{1,0:T(8,128)(2,1)} %get-tuple-element.127), channel_id=1, source_target_pairs={{0,12},{4,8},{8,4},{12,0},{1,13},{5,9},{9,5},{13,1},{2,14},{6,10},... | collective-permute-start | bytes 417800 | tf_op jit(solution)/shard_map/ppermute | solution.py:663
  324.2 7.4 %copy-start.27 = (s16[32,2176]{1,0:T(8,128)(2,1)}, s16[32,2176]{1,0:T(8,128)(2,1)S(1)}, u32[]{:S(2)}) copy-start(s16[32,2176]{1,0:T(8,128)(2,1)S(1)} %collective-permute-done.44.p1) | copy-start | bytes 417796
  (25 other events, 23.1 us)
Sparse Core Ops, SparseCore 0:
  18.4 30.5 all-gather.3
  50.6 21.9 all-gather.5
  86.8 28.7 all-gather.7
